TPU v7x, 32 devices: a whole 2x2x4 slice. The times are simulated.
32 devices in a mesh: rows: 16 (over z, y, x), grp: 2 (over core).
Axes of the slice: x: 2, y: 2, z: 4, core: 2. Of those that a mesh axis runs over, the one named last changes fastest.
Arguments:
- earlier: bfloat16 [131072, 1024], P(('rows', 'grp')), may hold values from -6 to 6
- snapshots: bfloat16 [131072, 512], P(('rows', 'grp')), may hold values from -8 to 8
- later: bfloat16 [131072, 512], P(('rows', 'grp')), may hold values from -8 to 8
Outputs:
- basis: bfloat16 [131072, 512], P(('rows', 'grp'))
- factors: float32 [2, 256, 256], replicated
- shift_block: float32 [512, 512], replicated
All inputs are finite; a program needn't handle non-finite values.
Results may differ from a plain program's by a relative error of at most 0.0045.
The roundings to bfloat16 on the way count: a program that leaves them out, or rounds other values in their place, can miss the bound.
Values sent between devices are 32-bit elements; how exact they have to be, the bound alone decides.
No kernel may reach another device: no remote copies, remote signals or barrier semaphores. Data moves between devices by JAX's collectives and lax.ppermute only.
A program may use at most 128 MiB of HBM per device.

v0:
```python
import jax
import jax.numpy as jnp
from jax import lax
from jax.sharding import PartitionSpec as P

PANEL = 256


def inner(left, right):
    return jnp.einsum("rk,rc->kc", left, right, preferred_element_type=jnp.float32)


def applied(space, coeffs):
    return jnp.dot(space, coeffs.astype(jnp.bfloat16), preferred_element_type=jnp.float32)


def factor(gram, second):
    lower = jnp.linalg.cholesky(gram)
    inverse = jax.scipy.linalg.solve_triangular(
        lower, jnp.eye(gram.shape[0], dtype=jnp.float32), lower=True
    )
    newcols = jnp.dot(second, inverse.T, precision=lax.Precision.HIGHEST).astype(jnp.bfloat16)
    return (newcols, lower.T, inverse)


def body(earlier, snapshots, later):
    total = earlier.shape[0] * lax.axis_size("rows") * lax.axis_size("grp")
    panel_one = snapshots[:, :PANEL]
    panel_two = snapshots[:, PANEL:]
    first = lax.psum(inner(earlier, panel_one), ("rows", "grp")) / total
    once = (panel_one.astype(jnp.float32) - applied(earlier, first)).astype(jnp.bfloat16)
    second = lax.psum(inner(earlier, once), ("rows", "grp")) / total
    twice = once.astype(jnp.float32) - applied(earlier, second)
    local_gram = jnp.dot(twice.T, twice, precision=lax.Precision.HIGHEST)
    gram = lax.psum(local_gram, ("rows", "grp")) / total
    q_first, r_first, unused_inverse = factor(gram, twice)
    early_shift = lax.psum(inner(q_first, later), ("rows", "grp")) / total
    space = jnp.concatenate([earlier, q_first], axis=1)
    first = lax.psum(inner(space, panel_two), ("rows", "grp")) / total
    once = (panel_two.astype(jnp.float32) - applied(space, first)).astype(jnp.bfloat16)
    second = lax.psum(inner(space, once), ("rows", "grp")) / total
    twice = once.astype(jnp.float32) - applied(space, second)
    local_gram = jnp.dot(twice.T, twice, precision=lax.Precision.HIGHEST)
    gram = lax.psum(local_gram, ("rows", "grp")) / total
    twice_local = jnp.dot(twice.T, later.astype(jnp.float32), precision=lax.Precision.HIGHEST)
    twice_shift = lax.psum(twice_local, ("rows", "grp")) / total
    q_second, r_second, inverse = factor(gram, twice)
    basis = jnp.concatenate([q_first, q_second], axis=1)
    late_shift = jnp.dot(inverse, twice_shift, precision=lax.Precision.HIGHEST)
    shift_block = jnp.concatenate([early_shift, late_shift], axis=0)
    return (basis, jnp.stack([r_first, r_second]), shift_block)


def solution(mesh):
    placed = (P(("rows", "grp"), None), P(("rows", "grp"), None), P(("rows", "grp"), None))
    return jax.shard_map(
        body,
        mesh=mesh,
        in_specs=placed,
        out_specs=(P(("rows", "grp"), None), P(), P()),
        check_vma=False,
    )
```

profile of v0, /device:TPU:0, one launch (start us, length us, event | category | flops | bytes accessed | tf_op | source)
XLA Modules:
  0.0 1045.1 jit_solution(14619916477018706275)
XLA Ops:
  7.2 7.3 fusion.46
  19.0 128.3 %all-reduce.9.cloned.1.call-done = f32[1024,256]{1,0:T(8,128)} async-done(((f32[1024,256]{1,0:T(8,128)}), f32[1024,256]{1,0:T(8,128)}) %all-reduce.9.cloned.1.call-update) | async-done | bytes 1048592 | tf_op jit(solution)/shard_map/psum | solution.py:30
  153.9 7.7 convolution_bitcast_fusion.2
  161.9 128.6 %all-reduce.11.cloned.1.call-done = f32[1024,256]{1,0:T(8,128)} async-done(((f32[1024,256]{1,0:T(8,128)}), f32[1024,256]{1,0:T(8,128)}) %all-reduce.11.cloned.1.call-update) | async-done | bytes 1048592 | tf_op jit(solution)/shard_map/psum | solution.py:32
  303.3 123.7 %all-reduce.13.cloned.1.call-done = f32[256,256]{0,1:T(8,128)} async-done(((f32[256,256]{0,1:T(8,128)}), f32[256,256]{0,1:T(8,128)}) %all-reduce.13.cloned.1.call-update) | async-done | bytes 262160 | tf_op jit(solution)/shard_map/psum | solution.py:35
  429.1 11.7 %cholesky.130 = f32[128,128]{1,0:T(8,128)S(1)} custom-call(f32[128,128]{1,0:T(8,128)S(1)} %cholesky.194), custom_call_target="Cholesky" | custom-call | tf_op jit(solution)/shard_map/jit(cholesky)/cholesky | solution.py:18
  440.9 9.8 custom-call.13
  451.2 11.7 %cholesky.147 = f32[128,128]{1,0:T(8,128)S(1)} custom-call(f32[128,128]{1,0:T(8,128)S(1)} %convolution_subtract_fusion.5), custom_call_target="Cholesky" | custom-call | tf_op jit(solution)/shard_map/jit(cholesky)/cholesky | solution.py:18
  465.0 15.1 %while.4 = (s32[]{:T(128)}, f32[256,256]{1,0:T(8,128)S(1)}, s32[2,2]{1,0:T(2,128)S(1)}, f32[2,128,128]{2,1,0:T(8,128)S(1)}, s32[]{:T(128)}) while((s32[]{:T(128)}, f32[256,256]{1,0:T(8,128)S(1)}, s32[2,2]{1,0:T(2,128)S(1)}, f32[2,128,128]{2,1,0:T(8,128)S(1)}, s32[]{:T(128)}) %tuple.50), condition=%wide.while_cond, body=%wide.while_body.sunk | while | flops 2 | bytes 131181 | solution.py:19
  480.2 19.7 %custom-call.14 = f32[2,128,128]{1,2,0:T(8,128)S(1)} custom-call(f32[2,128,128]{2,1,0:T(8,128)S(1)} %get-tuple-element.19), custom_call_target="InvertDiagBlocksLowerTriangular" | custom-call | tf_op jit(solution)/shard_map/jit(_solve_triangular)/triangular_solve | solution.py:19
  500.7 7.2 convolution_convert_fusion.1
  510.4 8.6 fusion.4
  519.0 130.5 %all-reduce.15.cloned.1.call-done = f32[1280,256]{1,0:T(8,128)} async-done(((f32[1280,256]{1,0:T(8,128)}), f32[1280,256]{1,0:T(8,128)}) %all-reduce.15.cloned.1.call-update) | async-done | bytes 1310736 | tf_op jit(solution)/shard_map/psum | solution.py:39
  649.6 6.8 fusion.3
  657.7 7.4 fusion.48
  669.5 126.3 %all-reduce.17.cloned.1.call-done = f32[1280,256]{1,0:T(8,128)} async-done(((f32[1280,256]{1,0:T(8,128)}), f32[1280,256]{1,0:T(8,128)}) %all-reduce.17.cloned.1.call-update) | async-done | bytes 1310736 | tf_op jit(solution)/shard_map/psum | solution.py:41
  795.8 7.1 convolution_subtract_fusion
  807.2 7.8 fusion.52
  815.0 131.5 %all-reduce.19.cloned.1.call-done = (f32[256,256]{0,1:T(8,128)}, f32[256,512]{1,0:T(8,128)}, f32[256,512]{1,0:T(8,128)}) async-done(((f32[256,256]{0,1:T(8,128)}, f32[256,512]{1,0:T(8,128)}, f32[256,512]{1,0:T(8,128)}), (f32[256,256]{0,1:T(8,128)}, f32[256,512]{1,0:T(8,128)}, f32[256,512]{1,0:T(8,128)})) %all-reduce.19.cloned.1.call-update) | async-done | bytes 1310736 | tf_op jit(solution)/shard_map/psum | solution.py:44
  948.6 11.8 %cholesky.164 = f32[128,128]{1,0:T(8,128)S(1)} custom-call(f32[128,128]{1,0:T(8,128)S(1)} %cholesky.197), custom_call_target="Cholesky" | custom-call | tf_op jit(solution)/shard_map/jit(cholesky)/cholesky | solution.py:18
  960.6 9.8 custom-call.15
  970.8 11.7 %cholesky.181 = f32[128,128]{1,0:T(8,128)S(1)} custom-call(f32[128,128]{1,0:T(8,128)S(1)} %convolution_subtract_fusion.4), custom_call_target="Cholesky" | custom-call | tf_op jit(solution)/shard_map/jit(cholesky)/cholesky | solution.py:18
  989.9 19.7 %custom-call.16 = f32[2,128,128]{1,2,0:T(8,128)S(1)} custom-call(f32[2,128,128]{2,1,0:T(8,128)S(1)} %get-tuple-element.20), custom_call_target="InvertDiagBlocksLowerTriangular" | custom-call | tf_op jit(solution)/shard_map/jit(_solve_triangular)/triangular_solve | solution.py:19
  1010.5 12.4 %convolution_convert_fusion = bf16[4096,256]{0,1:T(8,128)(2,1)} fusion(f32[4096,256]{1,0:T(8,128)} %copy-done, f32[128,256]{1,0:T(8,128)S(1)} %fusion.29, f32[128,256]{1,0:T(8,128)S(1)} %fusion.24), kind=kOutput, calls=%fused_computation.9 | convolution fusion | flops 3222339584 | bytes 6553600 | tf_op jit(solution)/shard_map/dot_general | solution.py:22
  (91 shorter events, 73.4 us)
Async XLA Ops:
  7.2 140.0 %all-reduce.9.cloned.1.call-start = ((), (), s32[]{:S(2)}) async-start(), calls=%async_computation | async-start | bytes 2097152 | tf_op jit(solution)/shard_map/psum | solution.py:30
  14.5 1.6 slice-start
  14.5 275.9 %all-reduce.11.cloned.1.call-start = ((), (), s32[]{:S(2)}) async-start(), calls=%async_computation.1 | async-start | bytes 2097152 | tf_op jit(solution)/shard_map/psum | solution.py:32
  161.6 265.4 %all-reduce.13.cloned.1.call-start = ((), (), s32[]{:S(2)}) async-start(), calls=%async_computation.2 | async-start | bytes 524288 | tf_op jit(solution)/shard_map/psum | solution.py:35
  296.6 2.0 copy-start.1
  302.9 346.7 %all-reduce.15.cloned.1.call-start = ((), (), s32[]{:S(2)}) async-start(), calls=%async_computation.3 | async-start | bytes 2621440 | tf_op jit(solution)/shard_map/psum | solution.py:39
  519.0 276.8 %all-reduce.17.cloned.1.call-start = ((), (), s32[]{:S(2)}) async-start(), calls=%async_computation.4 | async-start | bytes 2621440 | tf_op jit(solution)/shard_map/psum | solution.py:41
  649.6 8.1 copy-start.3
  656.4 1.3 copy-start.7
  665.2 281.3 %all-reduce.19.cloned.1.call-start = ((), (), s32[]{:S(2)}) async-start(), calls=%async_computation.5 | async-start | bytes 2621440 | tf_op jit(solution)/shard_map/psum | solution.py:44
  795.8 7.1 copy-start.2
  802.9 4.3 copy-start
  1010.2 14.4 %copy-start.6 = (f32[256,512]{1,0:T(8,128)S(1)}, f32[256,512]{1,0:T(8,128)}, u32[]{:S(2)}) copy-start(f32[256,512]{1,0:T(8,128)} %get-tuple-element.42) | copy-start | bytes 1572868
  1010.5 15.0 %copy-start.5 = (f32[1,256,256]{1,2,0:T(8,128)S(1)}, f32[1,256,256]{1,2,0:T(8,128)}, u32[]{:S(2)}) copy-start(f32[1,256,256]{1,2,0:T(8,128)} %get-tuple-element.49) | copy-start | bytes 786436
  1030.5 6.5 copy-start.4
Sparse Core Ops, SparseCore 0:
  14.7 132.5 all-reduce.8
  161.7 128.6 all-reduce.10
  303.0 123.9 all-reduce.12
  519.1 130.4 all-reduce.14
  665.3 130.3 all-reduce.16
  815.1 131.3 all-reduce.18
where the time goes:
time: 1050 us
  waiting for transfers between devices  769 us (73%)
  other arithmetic  119 us (11%)
  matrix products  102 us (10%)
  local copies, waits for them, and re-layouts  25.9 us (2%)
  between operations  17.2 us (2%)
  loops' own time  11.2 us (1%)
    psum x2, waiting for transfers between devices, body(): gram = lax.psum(local_gram, ('rows', 'grp')) / total  255 us
    psum x1, waiting for transfers between devices, body(): first = lax.psum(inner(space, panel_two), ('rows', 'grp')) / total  131 us
    psum x1, waiting for transfers between devices, body(): second = lax.psum(inner(earlier, once), ('rows', 'grp')) / total  129 us
    psum x1, waiting for transfers between devices, body(): first = lax.psum(inner(earlier, panel_one), ('rows', 'grp')) / total  128 us
    psum x1, waiting for transfers between devices, body(): second = lax.psum(inner(space, once), ('rows', 'grp')) / total  126 us
    another operation x13, other arithmetic, factor(): lower = jnp.linalg.cholesky(gram)  68.7 us
    another operation x3, other arithmetic, factor(): jax.scipy.linalg.solve_triangular(lower, jnp.eye(gram.shape[0], dtype=jnp...  39.4 us
    dot_general x5, matrix products, inner(): jnp.einsum('rk,rc->kc', left, right, preferred_element_type=jnp.float32)  35.3 us
  transfers between devices with their start and end apart: 6, of which 6 were waited for; matrix products, arithmetic and copies ran while one was open for 1% of the time, Pallas kernels for 0%

commit v1 on v0

v1 whole, which is shorter than its diff:
```python
import jax
import jax.numpy as jnp
from jax import lax
from jax.experimental import pallas as pl
from jax.experimental.pallas import tpu as pltpu
from jax.sharding import PartitionSpec as P

AXES = ("rows", "grp")
HIGHEST = lax.Precision.HIGHEST
BF16 = jnp.bfloat16
F32 = jnp.float32
VMEM_BYTES = 58 * 2**20


def dot(a, b):
    return jnp.dot(a, b, preferred_element_type=F32)


def full(a, b):
    return jnp.dot(a, b, precision=HIGHEST, preferred_element_type=F32)


def wide(x):
    return x.astype(F32)


def split(x):
    high = x.astype(BF16)
    return high, (x - wide(high)).astype(BF16)


def factor_tile(groups, emit):
    count = len(groups)
    lane = lax.broadcasted_iota(jnp.int32, (8, 128), 1)
    sub = lax.broadcasted_iota(jnp.int32, (8, 128), 0)
    rows = list(groups)
    for k in range(count):
        base = 8 * k
        strip = rows[k]
        inside = (lane >= base) & (lane < base + 8)
        eye = jnp.where(lane == base + sub, 1.0, 0.0).astype(F32)
        mixed = jnp.where(inside, eye, strip)
        cols = [jnp.broadcast_to(strip[:, base + j:base + j + 1], (8, 128)) for j in range(8)]
        entry = {}
        for j in range(8):
            for i in range(j, 8):
                entry[i, j] = jnp.broadcast_to(cols[j][i:i + 1, :], (8, 128))
        scale = []
        low = {}
        for j in range(8):
            r = lax.rsqrt(entry[j, j])
            scale.append(r)
            for i in range(j + 1, 8):
                low[i, j] = entry[i, j] * r
            for c in range(j + 1, 8):
                for i in range(c, 8):
                    entry[i, c] = entry[i, c] - low[i, j] * low[c, j]
        upper, both = [], []
        for j in range(8):
            u = jnp.broadcast_to(strip[j:j + 1, :], (8, 128))
            v = jnp.broadcast_to(mixed[j:j + 1, :], (8, 128))
            for i in range(j):
                u = u - low[j, i] * upper[i]
                v = v - low[j, i] * both[i]
            upper.append(u * scale[j])
            both.append(v * scale[j])
        out_r = upper[0]
        out_m = both[0]
        for j in range(1, 8):
            out_r = jnp.where(sub == j, upper[j], out_r)
            out_m = jnp.where(sub == j, both[j], out_m)
        emit(
            k,
            jnp.where(lane >= base + sub, out_r, 0.0),
            jnp.where(lane <= base + sub, out_m, 0.0),
        )
        for g in range(k + 1, count):
            w = rows[g]
            new = jnp.where(inside, 0.0, w)
            left = []
            for j in range(8):
                c = jnp.broadcast_to(w[:, base + j:base + j + 1], (8, 128))
                for i in range(j):
                    c = c - left[i] * low[j, i]
                c = c * scale[j]
                left.append(c)
                new = new - c * both[j]
            rows[g] = new


def factor(r_ref, m_ref):
    n = r_ref.shape[0]
    h = 128

    def step(t, carry):
        top = pl.multiple_of(t * h, h)
        groups = [r_ref[pl.ds(pl.multiple_of(top + 8 * g, 8), 8), pl.ds(top, h)] for g in range(h // 8)]

        def emit(k, r, m):
            at = pl.ds(pl.multiple_of(top + 8 * k, 8), 8)
            r_ref[at, pl.ds(top, h)] = r
            m_ref[at, pl.ds(top, h)] = m

        factor_tile(groups, emit)

        @pl.when(t == 0)
        def _():
            inv = m_ref[:h, :h]
            u = full(inv, r_ref[:h, h:])
            ut = u.T
            r_ref[:h, h:] = u
            r_ref[h:, h:] = r_ref[h:, h:] - full(ut, u)
            m_ref[h:, :h] = full(ut, inv)
            r_ref[h:, :h] = jnp.zeros((n - h, h), F32)
            m_ref[:h, h:] = jnp.zeros((h, n - h), F32)

        return carry

    lax.fori_loop(0, n // h, step, 0)
    m_ref[h:, :h] = -full(m_ref[h:, h:], m_ref[h:, :h])


def place(core_ref, sums, total_ref):
    mine = core_ref[0]
    at = 0
    for own, other in sums:
        h = own.shape[0]
        total_ref[pl.ds(pl.multiple_of(at + mine * h, 8), h)] = own[...]
        total_ref[pl.ds(pl.multiple_of(at + (1 - mine) * h, 8), h)] = other[...]
        at += 2 * h


def deal(core_ref, total_ref, sends, keeps):
    mine = core_ref[0]
    at = 0
    for send, keep in zip(sends, keeps):
        h = send.shape[0]
        keep[...] = total_ref[pl.ds(pl.multiple_of(at + mine * h, 8), h)]
        send[...] = total_ref[pl.ds(pl.multiple_of(at + (1 - mine) * h, 8), h)]
        at += 2 * h


def cross_kernel(parts, scale, core_ref, e_ref, x_ref, *refs):
    sends, keeps, acc = refs[:parts], refs[parts:2 * parts], refs[-1]
    k = e_ref.shape[1]
    p = x_ref.shape[1] // 2
    step = pl.program_id(0)

    @pl.when(step == 0)
    def _():
        acc[...] = jnp.zeros_like(acc)

    et = e_ref[...].T
    at = 0
    for c in range(2):
        acc[at:at + k] += dot(et, x_ref[:, c * p:(c + 1) * p])
        at += k
    for j in range(k // p):
        m = (j + 1) * p
        acc[at:at + m] += dot(et[:m], e_ref[:, j * p:(j + 1) * p])
        at += m

    @pl.when(step == pl.num_programs(0) - 1)
    def _():
        acc[...] = acc[...] * scale
        deal(core_ref, acc, sends, keeps)


def first_kernel(parts, scale, core_ref, *refs):
    own, other = refs[:parts], refs[parts:2 * parts]
    (e_ref, x_ref, u_ref, hi_ref, lo_ref, z_ref, h_ref, b2_ref, send, keep,
     total, b_ref, sb_ref, offh, offl, acc, hl) = refs[2 * parts:]
    k = e_ref.shape[1]
    p = x_ref.shape[1] // 2
    step = pl.program_id(0)

    @pl.when(step == 0)
    def _():
        place(core_ref, list(zip(own, other)), total)
        at = 2 * k
        for j in range(k // p):
            cols = slice(j * p, (j + 1) * p)
            for i in range(j + 1):
                block = total[at:at + p]
                at += p
                if i == j:
                    a = lax.broadcasted_iota(jnp.int32, (p, p), 0)
                    b = lax.broadcasted_iota(jnp.int32, (p, p), 1)
                    block = block - jnp.where(a == b, 1.0, 0.0)
                high, low = split(block)
                rows = slice(i * p, (i + 1) * p)
                offh[rows, cols] = high
                offl[rows, cols] = low
                if i < j:
                    offh[cols, rows] = high.T
                    offl[cols, rows] = low.T
        for c in range(2):
            cols = slice(c * p, (c + 1) * p)
            coef = total[c * k:(c + 1) * k]
            b = coef.astype(BF16)
            b_ref[:, cols] = b
            after = (coef - wide(b)) - dot(offh[...], b) - dot(offl[...], b)
            if c == 0:
                sb = after.astype(BF16)
                sb_ref[...] = sb
                h_ref[...] = (after - wide(sb)) - dot(offh[...], sb) - dot(offl[...], sb)
            else:
                z_ref[...] = after
                b2_ref[...] = b
        acc[...] = jnp.zeros_like(acc)
        hl[...] = jnp.zeros_like(hl)

    t = dot(e_ref[...], b_ref[...])
    once = wide((wide(x_ref[:, :p]) - t[:, :p]).astype(BF16))
    u_ref[...] = wide(x_ref[:, p:]) - t[:, p:]
    high, low = split(once - dot(e_ref[...], sb_ref[...]))
    hi_ref[...] = high
    lo_ref[...] = low
    ht, lt = high.T, low.T
    acc[:p] += dot(ht, high)
    hl[...] += dot(ht, low)
    acc[p:] += dot(ht, x_ref[:, p:]) + dot(lt, x_ref[:, p:])

    @pl.when(step == pl.num_programs(0) - 1)
    def _():
        acc[:p] = acc[:p] + hl[...] + hl[...].T
        acc[...] = acc[...] * scale
        deal(core_ref, acc, [send], [keep])


def second_kernel(parts, scale, core_ref, own, other, z_ref, h_ref, b2_ref, e_ref, u_ref, hi_ref, lo_ref, l_ref, *refs):
    q_ref, hi2_ref, lo2_ref, r_ref, x_ref = refs[:5]
    sends, keeps = refs[5:5 + parts], refs[5 + parts:5 + 2 * parts]
    total, m_ref, ih, il, db, ub, lb, acc, hl = refs[5 + 2 * parts:]
    p = r_ref.shape[0]
    step = pl.program_id(0)

    @pl.when(step == 0)
    def _():
        place(core_ref, [(own, other)], total)
        r_ref[...] = total[:p]
        factor(r_ref, m_ref)
        inv = m_ref[...]
        invt = inv.T
        high, low = split(invt)
        ih[...] = high
        il[...] = low
        d = full(inv, total[p:])
        d_b = wide(d.astype(BF16))
        db[...] = d.astype(BF16)
        against = h_ref[...]
        at = against.T
        upper = (z_ref[...] - full(against, full(invt, d_b))).astype(BF16)
        ub[...] = upper
        lower = (d - d_b) - full(inv, full(at, wide(b2_ref[...])))
        lower_b = lower.astype(BF16)
        lb[...] = lower_b
        x_ref[...] = (lower - wide(lower_b)) - full(inv, full(at, wide(upper)))
        acc[...] = jnp.zeros_like(acc)
        hl[...] = jnp.zeros_like(hl)

    high, low = hi_ref[...], lo_ref[...]
    q = (dot(high, ih[...]) + dot(high, il[...]) + dot(low, ih[...])).astype(BF16)
    q_ref[...] = q
    once = wide((u_ref[...] - dot(q, db[...])).astype(BF16))
    high, low = split(once - dot(e_ref[...], ub[...]) - dot(q, lb[...]))
    hi2_ref[...] = high
    lo2_ref[...] = low
    ht, lt, qt = high.T, low.T, q.T
    acc[:p] += dot(ht, high)
    hl[...] += dot(ht, low)
    acc[p:2 * p] += dot(qt, high) + dot(qt, low)
    for c in range(2):
        right = l_ref[:, c * p:(c + 1) * p]
        acc[(2 + c) * p:(3 + c) * p] += dot(ht, right) + dot(lt, right)
        acc[(4 + c) * p:(5 + c) * p] += dot(qt, right)

    @pl.when(step == pl.num_programs(0) - 1)
    def _():
        acc[:p] = acc[:p] + hl[...] + hl[...].T
        acc[...] = acc[...] * scale
        deal(core_ref, acc, sends, keeps)


def last_kernel(parts, core_ref, *refs):
    own, other = refs[:parts], refs[parts:2 * parts]
    x_ref, r1_ref, q_ref, hi_ref, lo_ref, basis, factors, shift, total, r_ref, m_ref, ih, il, back = refs[2 * parts:]
    p = r_ref.shape[0]

    @pl.when(pl.program_id(0) == 0)
    def _():
        place(core_ref, list(zip(own, other)), total)
        res = total[p:2 * p]
        off = res - x_ref[...]
        offt = off.T
        cut = full(offt, res)
        r_ref[...] = total[:p] - cut - cut.T + full(offt, off)
        factor(r_ref, m_ref)
        inv = m_ref[...]
        invt = inv.T
        high, low = split(invt)
        ih[...] = high
        il[...] = low
        back[...] = full(off, invt).astype(BF16)
        factors[0] = r1_ref[...]
        factors[1] = r_ref[...]
        for c in range(2):
            cols = slice(c * p, (c + 1) * p)
            early = total[(4 + c) * p:(5 + c) * p]
            shift[:p, cols] = early
            shift[p:, cols] = full(inv, total[(2 + c) * p:(3 + c) * p] - full(offt, early))

    high, low = hi_ref[...], lo_ref[...]
    q = dot(high, ih[...]) + dot(high, il[...]) + dot(low, ih[...]) - dot(q_ref[...], back[...])
    basis[:, :p] = q_ref[...]
    basis[:, p:] = q.astype(BF16)


def exchange(x, axis, bit):
    size = lax.axis_size(axis)
    return lax.ppermute(x, axis, [(i, i ^ (1 << bit)) for i in range(size)])


def summed(sends, keeps, tail):
    bits = list(range(lax.axis_size("rows").bit_length() - 1))
    turn, last = bits[:-1], bits[-1:]
    orders = [turn[n % len(turn):] + turn[:n % len(turn)] + last for n in range(len(sends))]
    me = lax.axis_index("rows")
    parts = [keep + exchange(send, "grp", 0) for send, keep in zip(sends, keeps)]
    halving = len(bits) - tail
    for step in range(halving):
        for n, order in enumerate(orders):
            x, bit = parts[n], order[step]
            half = x.shape[0] // 2
            mine = (me >> bit) & 1
            send = lax.dynamic_slice_in_dim(x, (1 - mine) * half, half, 0)
            keep = lax.dynamic_slice_in_dim(x, mine * half, half, 0)
            parts[n] = keep + exchange(send, "rows", bit)
    for step in range(halving, len(bits)):
        for n, order in enumerate(orders):
            parts[n] = parts[n] + exchange(parts[n], "rows", order[step])
    for step in reversed(range(halving)):
        for n, order in enumerate(orders):
            x, bit = parts[n], order[step]
            other = exchange(x, "rows", bit)
            mine = ((me >> bit) & 1) == 1
            parts[n] = jnp.concatenate([jnp.where(mine, other, x), jnp.where(mine, x, other)], axis=0)
    return parts, [exchange(x, "grp", 0) for x in parts]


def body(earlier, snapshots, later):
    n, k = earlier.shape
    p = snapshots.shape[1] // 2
    devices = lax.axis_size(AXES)
    scale = 1.0 / (n * devices)
    core = lax.axis_index("grp").astype(jnp.int32).reshape(1)
    blocks = k // p
    rows = (2 * blocks + blocks * (blocks + 1) // 2) * p
    unit = 2 * devices * 8
    parts = 3 if rows % (3 * unit) == 0 else 1
    tile = 512 if n % 512 == 0 else n
    tall = 1024 if n % 1024 == 0 else tile

    def smem():
        return pl.BlockSpec(memory_space=pltpu.SMEM)

    def whole(*shape):
        return pl.BlockSpec(shape, lambda i: (0,) * len(shape))

    def tiled(cols, height=tile):
        return pl.BlockSpec((height, cols), lambda i: (i, 0))

    def shape(*dims, dtype=F32):
        return jax.ShapeDtypeStruct(dims, dtype)

    def call(kernel, name, steps, ins, outs, scratch, flops, size, *args):
        return pl.pallas_call(
            kernel,
            grid=(steps,),
            in_specs=[s for s in ins],
            out_specs=[s for s, _ in outs],
            out_shape=[s for _, s in outs],
            scratch_shapes=scratch,
            name=name,
            cost_estimate=pl.CostEstimate(flops=flops, bytes_accessed=size, transcendentals=0),
            compiler_params=pltpu.CompilerParams(
                dimension_semantics=("arbitrary",), vmem_limit_bytes=VMEM_BYTES
            ),
        )(*args)

    half = rows // parts // 2
    halves = [(whole(half, p), shape(half, p))] * (2 * parts)
    got = call(
        lambda *r: cross_kernel(parts, scale, *r), "cross", n // tall,
        [smem(), tiled(k, tall), tiled(2 * p, tall)],
        halves,
        [pltpu.VMEM((rows, p), F32)],
        2 * n * rows * p, 2 * n * (k + 2 * p),
        core, earlier, snapshots,
    )
    own, other = summed(got[:parts], got[parts:], 1)

    u, hi, lo, z, h, b2, send, keep = call(
        lambda *r: first_kernel(parts, scale, *r), "first", n // tile,
        [smem()] + [whole(half, p)] * (2 * parts) + [tiled(k), tiled(2 * p)],
        [
            (tiled(p), shape(n, p)),
            (tiled(p), shape(n, p, dtype=BF16)),
            (tiled(p), shape(n, p, dtype=BF16)),
            (whole(k, p), shape(k, p)),
            (whole(k, p), shape(k, p)),
            (whole(k, p), shape(k, p, dtype=BF16)),
            (whole(p, p), shape(p, p)),
            (whole(p, p), shape(p, p)),
        ],
        [
            pltpu.VMEM((rows, p), F32),
            pltpu.VMEM((k, 2 * p), BF16),
            pltpu.VMEM((k, p), BF16),
            pltpu.VMEM((k, k), BF16),
            pltpu.VMEM((k, k), BF16),
            pltpu.VMEM((2 * p, p), F32),
            pltpu.VMEM((p, p), F32),
        ],
        2 * n * p * (3 * k + 4 * p) + 12 * k * k * p, n * (2 * k + 12 * p),
        core, *own, *other, earlier, snapshots,
    )
    (own,), (other,) = summed([send], [keep], 2)

    got = call(
        lambda *r: second_kernel(3, scale, *r), "second", n // tile,
        [smem(), whole(p, p), whole(p, p), whole(k, p), whole(k, p), whole(k, p),
         tiled(k), tiled(p), tiled(p), tiled(p), tiled(2 * p)],
        [
            (tiled(p), shape(n, p, dtype=BF16)),
            (tiled(p), shape(n, p, dtype=BF16)),
            (tiled(p), shape(n, p, dtype=BF16)),
            (whole(p, p), shape(p, p)),
            (whole(p, p), shape(p, p)),
        ] + [(whole(p, p), shape(p, p))] * 6,
        [
            pltpu.VMEM((2 * p, p), F32),
            pltpu.VMEM((p, p), F32),
            pltpu.VMEM((p, p), BF16),
            pltpu.VMEM((p, p), BF16),
            pltpu.VMEM((p, p), BF16),
            pltpu.VMEM((k, p), BF16),
            pltpu.VMEM((p, p), BF16),
            pltpu.VMEM((6 * p, p), F32),
            pltpu.VMEM((p, p), F32),
        ],
        2 * n * p * (k + 15 * p), n * (2 * k + 18 * p),
        core, own, other, z, h, b2, earlier, u, hi, lo, later,
    )
    q_one, hi2, lo2, r_one, expected = got[:5]
    own, other = summed(got[5:8], got[8:], 2)

    return tuple(call(
        lambda *r: last_kernel(3, *r), "last", n // tile,
        [smem()] + [whole(p, p)] * 8 + [tiled(p)] * 3,
        [
            (tiled(2 * p), shape(n, 2 * p, dtype=BF16)),
            (whole(2, p, p), shape(2, p, p)),
            (whole(2 * p, 2 * p), shape(2 * p, 2 * p)),
        ],
        [
            pltpu.VMEM((6 * p, p), F32),
            pltpu.VMEM((p, p), F32),
            pltpu.VMEM((p, p), F32),
            pltpu.VMEM((p, p), BF16),
            pltpu.VMEM((p, p), BF16),
            pltpu.VMEM((p, p), BF16),
        ],
        2 * n * p * 4 * p, n * 10 * p,
        core, *own, *other, expected, r_one, q_one, hi2, lo2,
    ))


def solution(mesh):
    spec = P(("rows", "grp"), None)
    return jax.shard_map(
        body,
        mesh=mesh,
        in_specs=(spec, spec, spec),
        out_specs=(spec, P(), P()),
        check_vma=False,
    )
```

time: 1050 us -> 243 us (0.23)
  waiting for transfers between devices: 769 us -> 78.1 us
  other arithmetic: 119 us -> 8.06 us
  matrix products: 102 us -> 0 us
  Pallas kernels: 0 us -> 96.1 us
  starting transfers between devices: 0.78 us -> 54.3 us
  local copies, waits for them, and re-layouts: 25.9 us -> 4.38 us
  between operations: 17.2 us -> 1.39 us
  loops' own time: 11.2 us -> 0 us
    psum x6 -> x0, waiting for transfers between devices: 769 us -> none  [the longest x2 255 us: body(): gram = lax.psum(local_gram, ('rows', 'grp')) / total]
    another operation x19 -> x0, other arithmetic: 109 us -> none  [the longest x13 68.7 us: factor(): lower = jnp.linalg.cholesky(gram)]
    dot_general x15 -> x0, matrix products: 99.5 us -> none  [the longest x5 35.3 us: inner(): jnp.einsum('rk,rc->kc', left, right, preferred_element_type=jnp.float32)]
    pallas_call x0 -> x4, Pallas kernels: none -> 96.1 us  [call(): pl.pallas_call(kernel, grid=(steps,), in_specs=[s for s in ins], out_spec...]
    ppermute x0 -> x59, waiting for transfers between devices: none -> 78.1 us  [exchange(): return lax.ppermute(x, axis, [(i, i ^ 1 << bit) for i in range(size)])]
    ppermute x0 -> x59, starting transfers between devices: none -> 54.3 us  [exchange(): return lax.ppermute(x, axis, [(i, i ^ 1 << bit) for i in range(size)])]
    unnamed x21 -> x32, local copies, waits for them, and re-layouts: 15.2 us -> 3.26 us
    another operation x2 -> x0, loops' own time: 11.2 us -> none  [factor(): jax.scipy.linalg.solve_triangular(lower, jnp.eye(gram.shape[0], dtype=jnp...]
  transfers between devices with their start and end apart: 6 -> 59, of which waited for: 6 -> 45; matrix products, arithmetic and copies ran while one was open for 1% -> 3% of each run, Pallas kernels for 0% -> 0%
where the time goes in v1:
time: 243 us; the launch traced here: 242 us
  Pallas kernels  96.1 us (40%)
  waiting for transfers between devices  78.1 us (32%)
  starting transfers between devices  54.3 us (22%)
  other arithmetic  8.06 us (3%)
  local copies, waits for them, and re-layouts  4.38 us (2%)
    pallas_call x4, Pallas kernels, call(): pl.pallas_call(kernel, grid=(steps,), in_specs=[s for s in ins], out_spec...  96.1 us
    ppermute x59, waiting for transfers between devices, exchange(): return lax.ppermute(x, axis, [(i, i ^ 1 << bit) for i in range(size)])  78.1 us
    ppermute x59, starting transfers between devices, exchange(): return lax.ppermute(x, axis, [(i, i ^ 1 << bit) for i in range(size)])  54.3 us
    add x7, other arithmetic, summed(): keep + exchange(send, 'grp', 0)  6.74 us
  transfers between devices with their start and end apart: 59, of which 45 were waited for; matrix products, arithmetic and copies ran while one was open for 3% of the time, Pallas kernels for 0%

profile of v1, /device:TPU:0, one launch (start us, length us, event | category | flops | bytes accessed | tf_op | source)
XLA Modules:
  0.0 242.4 jit_solution(14066286516602506007)
XLA Ops:
  0.6 15.8 %cross.1 = (f32[768,256]{1,0:T(8,128)}, f32[768,256]{1,0:T(8,128)}, f32[768,256]{1,0:T(8,128)}, f32[768,256]{1,0:T(8,128)}, f32[768,256]{1,0:T(8,128)}, /*index=5*/f32[768,256]{1,0:T(8,128)}) custom-call(s32[1]{0:T(128)} %bitcast.r_0_, bf16[4096,1024]{1,0:T(8,128)(2,1)} %r_6_.1, bf16[4096,512]{1,0:T(8,128)(2,1)} %r_8_.1), custom_call_target="tpu_custom_call" | custom-call | flops 9663676416 | bytes 12582912 | tf_op jit(solution)/shard_map/cross/pallas_call | solution.py:377
  22.2 2.9 %collective-permute-start.17 = (f32[384,256]{1,0:T(8,128)}, f32[384,256]{1,0:T(8,128)S(1)}, u32[]{:S(2)}, u32[]{:S(2)}) collective-permute-start(f32[384,256]{1,0:T(8,128)} %constant_dynamic-slice_fusion.10), channel_id=1, source_target_pairs={{0,8},{2,10},{4,12},{6,14},{8,0},{10,2},{12,4},{14,6},{16,24},{18,... | collective-permute-start | bytes 1179656 | tf_op jit(solution)/shard_map/ppermute | solution.py:321
  29.7 5.0 %collective-permute-done.17 = f32[384,256]{1,0:T(8,128)S(1)} collective-permute-done((f32[384,256]{1,0:T(8,128)}, f32[384,256]{1,0:T(8,128)S(1)}, u32[]{:S(2)}, u32[]{:S(2)}) %collective-permute-start.17) | collective-permute-done | bytes 393248 | tf_op jit(solution)/shard_map/ppermute | solution.py:321
  38.3 2.0 collective-permute-done.1
  40.4 2.6 %collective-permute-done.18 = f32[192,256]{1,0:T(8,128)S(1)} collective-permute-done((f32[192,256]{1,0:T(8,128)S(1)}, f32[192,256]{1,0:T(8,128)S(1)}, u32[]{:S(2)}, u32[]{:S(2)}) %collective-permute-start.18) | collective-permute-done | bytes 196640 | tf_op jit(solution)/shard_map/ppermute | solution.py:321
  45.3 1.9 collective-permute-done.2
  48.2 2.7 %collective-permute-start.20 = (f32[96,256]{1,0:T(8,128)S(1)}, f32[96,256]{1,0:T(8,128)S(1)}, u32[]{:S(2)}, u32[]{:S(2)}) collective-permute-start(f32[96,256]{1,0:T(8,128)S(1)} %dynamic-slice_add_fusion.10), channel_id=1, source_target_pairs={{0,16},{2,18},{4,20},{6,22},{8,24},{10,26},{12,28},{14,30},{16,0},... | collective-permute-start | bytes 294920 | tf_op jit(solution)/shard_map/ppermute | solution.py:321
  52.9 2.7 %collective-permute-start.4 = (f32[96,256]{1,0:T(8,128)S(1)}, f32[96,256]{1,0:T(8,128)S(1)}, u32[]{:S(2)}, u32[]{:S(2)}) collective-permute-start(f32[96,256]{1,0:T(8,128)S(1)} %dynamic-slice_add_fusion.12), channel_id=1, source_target_pairs={{0,16},{2,18},{4,20},{6,22},{8,24},{10,26},{12,28},{14,30},{16,0},... | collective-permute-start | bytes 294920 | tf_op jit(solution)/shard_map/ppermute | solution.py:321
  55.6 3.8 %collective-permute-done.20 = f32[96,256]{1,0:T(8,128)S(1)} collective-permute-done((f32[96,256]{1,0:T(8,128)S(1)}, f32[96,256]{1,0:T(8,128)S(1)}, u32[]{:S(2)}, u32[]{:S(2)}) %collective-permute-start.20) | collective-permute-done | bytes 98336 | tf_op jit(solution)/shard_map/ppermute | solution.py:321
  71.1 3.9 %collective-permute-done.14 = f32[192,256]{1,0:T(8,128)S(1)} collective-permute-done((f32[192,256]{1,0:T(8,128)S(1)}, f32[192,256]{1,0:T(8,128)S(1)}, u32[]{:S(2)}, u32[]{:S(2)}) %collective-permute-start.14) | collective-permute-done | bytes 196640 | tf_op jit(solution)/shard_map/ppermute | solution.py:321
  77.7 3.2 %collective-permute-done.23 = f32[384,256]{1,0:T(8,128)S(1)} collective-permute-done((f32[384,256]{1,0:T(8,128)S(1)}, f32[384,256]{1,0:T(8,128)S(1)}, u32[]{:S(2)}, u32[]{:S(2)}) %collective-permute-start.23) | collective-permute-done | bytes 393248 | tf_op jit(solution)/shard_map/ppermute | solution.py:321
  81.1 1.8 collective-permute-done.15
  88.0 24.2 %first.1 = (f32[4096,256]{1,0:T(8,128)}, bf16[4096,256]{1,0:T(8,128)(2,1)}, bf16[4096,256]{1,0:T(8,128)(2,1)}, f32[1024,256]{1,0:T(8,128)}, f32[1024,256]{1,0:T(...) custom-call(s32[1]{0:T(128)} %bitcast.r_0_, f32[768,256]{1,0:T(8,128)} %copy-done.5, ...), custom_call_target="tpu_custom_call" | custom-call | flops 11811160064 | bytes 20971520 | tf_op jit(solution)/shard_map/first/pallas_call | solution.py:377
  116.1 4.5 %collective-permute-done.28 = f32[128,256]{1,0:T(8,128)S(1)} collective-permute-done((f32[128,256]{1,0:T(8,128)S(1)}, f32[128,256]{1,0:T(8,128)S(1)}, u32[]{:S(2)}, u32[]{:S(2)}) %collective-permute-start.28) | collective-permute-done | bytes 131104 | tf_op jit(solution)/shard_map/ppermute | solution.py:321
  121.4 3.5 %collective-permute-done.29 = f32[64,256]{1,0:T(8,128)S(1)} collective-permute-done((f32[64,256]{1,0:T(8,128)S(1)}, f32[64,256]{1,0:T(8,128)S(1)}, u32[]{:S(2)}, u32[]{:S(2)}) %collective-permute-start.29) | collective-permute-done | bytes 65568 | tf_op jit(solution)/shard_map/ppermute | solution.py:321
  125.7 3.6 %collective-permute-done.30 = f32[64,256]{1,0:T(8,128)S(1)} collective-permute-done((f32[64,256]{1,0:T(8,128)S(1)}, f32[64,256]{1,0:T(8,128)S(1)}, u32[]{:S(2)}, u32[]{:S(2)}) %collective-permute-start.30) | collective-permute-done | bytes 65568 | tf_op jit(solution)/shard_map/ppermute | solution.py:321
  130.8 4.4 %collective-permute-done.31 = f32[64,256]{1,0:T(8,128)S(1)} collective-permute-done((f32[64,256]{1,0:T(8,128)S(1)}, f32[64,256]{1,0:T(8,128)S(1)}, u32[]{:S(2)}, u32[]{:S(2)}) %collective-permute-start.31) | collective-permute-done | bytes 65568 | tf_op jit(solution)/shard_map/ppermute | solution.py:321
  136.0 3.5 %collective-permute-done.32 = f32[64,256]{1,0:T(8,128)S(1)} collective-permute-done((f32[64,256]{1,0:T(8,128)S(1)}, f32[64,256]{1,0:T(8,128)S(1)}, u32[]{:S(2)}, u32[]{:S(2)}) %collective-permute-start.32) | collective-permute-done | bytes 65568 | tf_op jit(solution)/shard_map/ppermute | solution.py:321
  140.7 3.9 %collective-permute-done.33 = f32[128,256]{1,0:T(8,128)S(1)} collective-permute-done((f32[128,256]{1,0:T(8,128)S(1)}, f32[128,256]{1,0:T(8,128)S(1)}, u32[]{:S(2)}, u32[]{:S(2)}) %collective-permute-start.33) | collective-permute-done | bytes 131104 | tf_op jit(solution)/shard_map/ppermute | solution.py:321
  147.0 35.9 %second.1 = (bf16[4096,256]{1,0:T(8,128)(2,1)}, bf16[4096,256]{1,0:T(8,128)(2,1)}, bf16[4096,256]{1,0:T(8,128)(2,1)}, f32[256,256]{1,0:T(8,128)}, f32[256,256]{1...) custom-call(s32[1]{0:T(128)} %bitcast.r_0_, ...), custom_call_target="tpu_custom_call" | custom-call | flops 10200547328 | bytes 27262976 | tf_op jit(solution)/shard_map/second/pallas_call | solution.py:377
  198.9 1.9 collective-permute-start.38
  200.8 2.0 collective-permute-start.53
  204.1 2.4 %collective-permute-start.39 = (f32[64,256]{1,0:T(8,128)S(1)}, f32[64,256]{1,0:T(8,128)S(1)}, u32[]{:S(2)}, u32[]{:S(2)}) collective-permute-start(f32[64,256]{1,0:T(8,128)S(1)} %add.244), channel_id=1, source_target_pairs={{0,16},{2,18},{4,20},{6,22},{8,24},{10,26},{12,28},{14,30},{16,0},... | collective-permute-start | bytes 196616 | tf_op jit(solution)/shard_map/ppermute | solution.py:321
  222.1 20.3 %last.1 = (bf16[4096,512]{1,0:T(8,128)(2,1)}, f32[2,256,256]{2,1,0:T(8,128)}, f32[512,512]{1,0:T(8,128)}) custom-call(s32[1]{0:T(128)} %bitcast.r_0_, f32[256,256]{1,0:T(8,128)} %copy-done.2, f32[256,256]{1,0:T(8,128)} %copy-done.1, f32[256,256]{1,0:T(8,128)} %copy-done, f32[256,256]{1,0:T(8,128)} %copy-done.10, f32[256,256]{1,0:T(8,128)} %copy-done.9, ...), custom_call_target="tpu_custom_call" | custom-call | flops 2147483648 | bytes 10485760 | tf_op jit(solution)/shard_map/last/pallas_call | solution.py:377
  (216 shorter events, 82.6 us)
Async XLA Ops:
  16.9 8.2 %collective-permute-start.8 = (f32[768,256]{1,0:T(8,128)}, f32[768,256]{1,0:T(8,128)S(1)}, u32[]{:S(2)}, u32[]{:S(2)}) collective-permute-start(f32[768,256]{1,0:T(8,128)} %get-tuple-element.31), channel_id=1, source_target_pairs={{0,1},{1,0},{2,3},{3,2},{4,5},{5,4},{6,7},{7,6},{8,9},{9,8},{10,11... | collective-permute-start | bytes 2359304 | tf_op jit(solution)/shard_map/ppermute | solution.py:321
  17.0 11.0 %collective-permute-start = (f32[768,256]{1,0:T(8,128)}, f32[768,256]{1,0:T(8,128)S(1)}, u32[]{:S(2)}, u32[]{:S(2)}) collective-permute-start(f32[768,256]{1,0:T(8,128)} %get-tuple-element.29), channel_id=1, source_target_pairs={{0,1},{1,0},{2,3},{3,2},{4,5},{5,4},{6,7},{7,6},{8,9},{9,8},{10,11... | collective-permute-start | bytes 2359304 | tf_op jit(solution)/shard_map/ppermute | solution.py:321
  22.2 12.6 %collective-permute-start.17 = (f32[384,256]{1,0:T(8,128)}, f32[384,256]{1,0:T(8,128)S(1)}, u32[]{:S(2)}, u32[]{:S(2)}) collective-permute-start(f32[384,256]{1,0:T(8,128)} %constant_dynamic-slice_fusion.10), channel_id=1, source_target_pairs={{0,8},{2,10},{4,12},{6,14},{8,0},{10,2},{12,4},{14,6},{16,24},{18,... | collective-permute-start | bytes 1179656 | tf_op jit(solution)/shard_map/ppermute | solution.py:321
  26.4 10.9 %collective-permute-start.9 = (f32[384,256]{1,0:T(8,128)S(1)}, f32[384,256]{1,0:T(8,128)S(1)}, u32[]{:S(2)}, u32[]{:S(2)}) collective-permute-start(f32[384,256]{1,0:T(8,128)S(1)} %constant_dynamic-slice_fusion.13), channel_id=1, source_target_pairs={{0,4},{2,6},{4,0},{6,2},{8,12},{10,14},{12,8},{14,10},{16,20},{18,... | collective-permute-start | bytes 1179656 | tf_op jit(solution)/shard_map/ppermute | solution.py:321
  28.1 12.1 %collective-permute-start.1 = (f32[384,256]{1,0:T(8,128)S(1)}, f32[384,256]{1,0:T(8,128)S(1)}, u32[]{:S(2)}, u32[]{:S(2)}) collective-permute-start(f32[384,256]{1,0:T(8,128)S(1)} %constant_dynamic-slice_fusion.16), channel_id=1, source_target_pairs={{0,2},{2,0},{4,6},{6,4},{8,10},{10,8},{12,14},{14,12},{16,18},{18,... | collective-permute-start | bytes 1179656 | tf_op jit(solution)/shard_map/ppermute | solution.py:321
  34.8 8.2 %collective-permute-start.18 = (f32[192,256]{1,0:T(8,128)S(1)}, f32[192,256]{1,0:T(8,128)S(1)}, u32[]{:S(2)}, u32[]{:S(2)}) collective-permute-start(f32[192,256]{1,0:T(8,128)S(1)} %constant_dynamic-slice_fusion.9), channel_id=1, source_target_pairs={{0,2},{2,0},{4,6},{6,4},{8,10},{10,8},{12,14},{14,12},{16,18},{18,... | collective-permute-start | bytes 589832 | tf_op jit(solution)/shard_map/ppermute | solution.py:321
  37.4 6.2 %collective-permute-start.10 = (f32[192,256]{1,0:T(8,128)S(1)}, f32[192,256]{1,0:T(8,128)S(1)}, u32[]{:S(2)}, u32[]{:S(2)}) collective-permute-start(f32[192,256]{1,0:T(8,128)S(1)} %constant_dynamic-slice_fusion.12), channel_id=1, source_target_pairs={{0,8},{2,10},{4,12},{6,14},{8,0},{10,2},{12,4},{14,6},{16,24},{18,... | collective-permute-start | bytes 589832 | tf_op jit(solution)/shard_map/ppermute | solution.py:321
  40.3 6.8 %collective-permute-start.2 = (f32[192,256]{1,0:T(8,128)S(1)}, f32[192,256]{1,0:T(8,128)S(1)}, u32[]{:S(2)}, u32[]{:S(2)}) collective-permute-start(f32[192,256]{1,0:T(8,128)S(1)} %constant_dynamic-slice_fusion.15), channel_id=1, source_target_pairs={{0,4},{2,6},{4,0},{6,2},{8,12},{10,14},{12,8},{14,10},{16,20},{18,... | collective-permute-start | bytes 589832 | tf_op jit(solution)/shard_map/ppermute | solution.py:321
  43.7 7.2 %collective-permute-start.11 = (f32[96,256]{1,0:T(8,128)S(1)}, f32[96,256]{1,0:T(8,128)S(1)}, u32[]{:S(2)}, u32[]{:S(2)}) collective-permute-start(f32[96,256]{1,0:T(8,128)S(1)} %constant_dynamic-slice_fusion.11), channel_id=1, source_target_pairs={{0,2},{2,0},{4,6},{6,4},{8,10},{10,8},{12,14},{14,12},{16,18},{18,... | collective-permute-start | bytes 294920 | tf_op jit(solution)/shard_map/ppermute | solution.py:321
  48.2 11.2 %collective-permute-start.20 = (f32[96,256]{1,0:T(8,128)S(1)}, f32[96,256]{1,0:T(8,128)S(1)}, u32[]{:S(2)}, u32[]{:S(2)}) collective-permute-start(f32[96,256]{1,0:T(8,128)S(1)} %dynamic-slice_add_fusion.10), channel_id=1, source_target_pairs={{0,16},{2,18},{4,20},{6,22},{8,24},{10,26},{12,28},{14,30},{16,0},... | collective-permute-start | bytes 294920 | tf_op jit(solution)/shard_map/ppermute | solution.py:321
  50.9 10.6 %collective-permute-start.12 = (f32[96,256]{1,0:T(8,128)S(1)}, f32[96,256]{1,0:T(8,128)S(1)}, u32[]{:S(2)}, u32[]{:S(2)}) collective-permute-start(f32[96,256]{1,0:T(8,128)S(1)} %dynamic-slice_add_fusion.11), channel_id=1, source_target_pairs={{0,16},{2,18},{4,20},{6,22},{8,24},{10,26},{12,28},{14,30},{16,0},... | collective-permute-start | bytes 294920 | tf_op jit(solution)/shard_map/ppermute | solution.py:321
  52.9 10.2 %collective-permute-start.4 = (f32[96,256]{1,0:T(8,128)S(1)}, f32[96,256]{1,0:T(8,128)S(1)}, u32[]{:S(2)}, u32[]{:S(2)}) collective-permute-start(f32[96,256]{1,0:T(8,128)S(1)} %dynamic-slice_add_fusion.12), channel_id=1, source_target_pairs={{0,16},{2,18},{4,20},{6,22},{8,24},{10,26},{12,28},{14,30},{16,0},... | collective-permute-start | bytes 294920 | tf_op jit(solution)/shard_map/ppermute | solution.py:321
  64.1 5.7 %collective-permute-start.22 = (f32[192,256]{1,0:T(8,128)S(1)}, f32[192,256]{1,0:T(8,128)S(1)}, u32[]{:S(2)}, u32[]{:S(2)}) collective-permute-start(f32[192,256]{1,0:T(8,128)S(1)} %pad_maximum_fusion.12), channel_id=1, source_target_pairs={{0,2},{2,0},{4,6},{6,4},{8,10},{10,8},{12,14},{14,12},{16,18},{18,... | collective-permute-start | bytes 589832 | tf_op jit(solution)/shard_map/ppermute | solution.py:321
  67.2 7.8 %collective-permute-start.14 = (f32[192,256]{1,0:T(8,128)S(1)}, f32[192,256]{1,0:T(8,128)S(1)}, u32[]{:S(2)}, u32[]{:S(2)}) collective-permute-start(f32[192,256]{1,0:T(8,128)S(1)} %pad_maximum_fusion.11), channel_id=1, source_target_pairs={{0,8},{2,10},{4,12},{6,14},{8,0},{10,2},{12,4},{14,6},{16,24},{18,... | collective-permute-start | bytes 589832 | tf_op jit(solution)/shard_map/ppermute | solution.py:321
  68.8 7.8 %collective-permute-start.6 = (f32[192,256]{1,0:T(8,128)S(1)}, f32[192,256]{1,0:T(8,128)S(1)}, u32[]{:S(2)}, u32[]{:S(2)}) collective-permute-start(f32[192,256]{1,0:T(8,128)S(1)} %pad_maximum_fusion.10), channel_id=1, source_target_pairs={{0,4},{2,6},{4,0},{6,2},{8,12},{10,14},{12,8},{14,10},{16,20},{18,... | collective-permute-start | bytes 589832 | tf_op jit(solution)/shard_map/ppermute | solution.py:321
  69.9 11.0 %collective-permute-start.23 = (f32[384,256]{1,0:T(8,128)S(1)}, f32[384,256]{1,0:T(8,128)S(1)}, u32[]{:S(2)}, u32[]{:S(2)}) collective-permute-start(f32[384,256]{1,0:T(8,128)S(1)} %pad_maximum_fusion.5), channel_id=1, source_target_pairs={{0,8},{2,10},{4,12},{6,14},{8,0},{10,2},{12,4},{14,6},{16,24},{18,... | collective-permute-start | bytes 1179656 | tf_op jit(solution)/shard_map/ppermute | solution.py:321
  75.1 7.8 %collective-permute-start.15 = (f32[384,256]{1,0:T(8,128)S(1)}, f32[384,256]{1,0:T(8,128)S(1)}, u32[]{:S(2)}, u32[]{:S(2)}) collective-permute-start(f32[384,256]{1,0:T(8,128)S(1)} %pad_maximum_fusion.4), channel_id=1, source_target_pairs={{0,4},{2,6},{4,0},{6,2},{8,12},{10,14},{12,8},{14,10},{16,20},{18,... | collective-permute-start | bytes 1179656 | tf_op jit(solution)/shard_map/ppermute | solution.py:321
  76.6 7.8 %collective-permute-start.7 = (f32[384,256]{1,0:T(8,128)S(1)}, f32[384,256]{1,0:T(8,128)S(1)}, u32[]{:S(2)}, u32[]{:S(2)}) collective-permute-start(f32[384,256]{1,0:T(8,128)S(1)} %pad_maximum_fusion.3), channel_id=1, source_target_pairs={{0,2},{2,0},{4,6},{6,4},{8,10},{10,8},{12,14},{14,12},{16,18},{18,... | collective-permute-start | bytes 1179656 | tf_op jit(solution)/shard_map/ppermute | solution.py:321
  129.3 5.9 %collective-permute-start.31 = (f32[64,256]{1,0:T(8,128)S(1)}, f32[64,256]{1,0:T(8,128)S(1)}, u32[]{:S(2)}, u32[]{:S(2)}) collective-permute-start(f32[64,256]{1,0:T(8,128)S(1)} %add.239), channel_id=1, source_target_pairs={{0,16},{2,18},{4,20},{6,22},{8,24},{10,26},{12,28},{14,30},{16,0},... | collective-permute-start | bytes 196616 | tf_op jit(solution)/shard_map/ppermute | solution.py:321
  188.6 5.9 %collective-permute-start.36 = (f32[128,256]{1,0:T(8,128)S(1)}, f32[128,256]{1,0:T(8,128)S(1)}, u32[]{:S(2)}, u32[]{:S(2)}) collective-permute-start(f32[128,256]{1,0:T(8,128)S(1)} %constant_dynamic-slice_fusion.5), channel_id=1, source_target_pairs={{0,2},{2,0},{4,6},{6,4},{8,10},{10,8},{12,14},{14,12},{16,18},{18,... | collective-permute-start | bytes 393224 | tf_op jit(solution)/shard_map/ppermute | solution.py:321
  196.8 6.0 %collective-permute-start.45 = (f32[64,256]{1,0:T(8,128)S(1)}, f32[64,256]{1,0:T(8,128)S(1)}, u32[]{:S(2)}, u32[]{:S(2)}) collective-permute-start(f32[64,256]{1,0:T(8,128)S(1)} %dynamic-slice_add_fusion.14), channel_id=1, source_target_pairs={{0,2},{2,0},{4,6},{6,4},{8,10},{10,8},{12,14},{14,12},{16,18},{18,... | collective-permute-start | bytes 196616 | tf_op jit(solution)/shard_map/ppermute | solution.py:321
  200.8 6.4 %collective-permute-start.53 = (f32[64,256]{1,0:T(8,128)S(1)}, f32[64,256]{1,0:T(8,128)S(1)}, u32[]{:S(2)}, u32[]{:S(2)}) collective-permute-start(f32[64,256]{1,0:T(8,128)S(1)} %add.262), channel_id=1, source_target_pairs={{0,16},{2,18},{4,20},{6,22},{8,24},{10,26},{12,28},{14,30},{16,0},... | collective-permute-start | bytes 196616 | tf_op jit(solution)/shard_map/ppermute | solution.py:321
  202.8 6.0 %collective-permute-start.46 = (f32[64,256]{1,0:T(8,128)S(1)}, f32[64,256]{1,0:T(8,128)S(1)}, u32[]{:S(2)}, u32[]{:S(2)}) collective-permute-start(f32[64,256]{1,0:T(8,128)S(1)} %add.253), channel_id=1, source_target_pairs={{0,16},{2,18},{4,20},{6,22},{8,24},{10,26},{12,28},{14,30},{16,0},... | collective-permute-start | bytes 196616 | tf_op jit(solution)/shard_map/ppermute | solution.py:321
  204.1 6.2 %collective-permute-start.39 = (f32[64,256]{1,0:T(8,128)S(1)}, f32[64,256]{1,0:T(8,128)S(1)}, u32[]{:S(2)}, u32[]{:S(2)}) collective-permute-start(f32[64,256]{1,0:T(8,128)S(1)} %add.244), channel_id=1, source_target_pairs={{0,16},{2,18},{4,20},{6,22},{8,24},{10,26},{12,28},{14,30},{16,0},... | collective-permute-start | bytes 196616 | tf_op jit(solution)/shard_map/ppermute | solution.py:321
  (51 other events, 187.2 us)

commit v2 on v1

--- a/solution.py
+++ b/solution.py
@@ -9,7 +9,7 @@
 HIGHEST = lax.Precision.HIGHEST
 BF16 = jnp.bfloat16
 F32 = jnp.float32
-VMEM_BYTES = 58 * 2**20
+MIB = 2**20
 
 
 def dot(a, b):
@@ -27,6 +27,10 @@
 def split(x):
     high = x.astype(BF16)
     return high, (x - wide(high)).astype(BF16)
+
+
+def thrice(a, b):
+    return dot(a[0], b[0]) + dot(a[0], b[1]) + dot(a[1], b[0])
 
 
 def factor_tile(groups, emit):
@@ -130,13 +134,13 @@
         at += 2 * h
 
 
-def deal(core_ref, total_ref, sends, keeps):
+def deal(core_ref, total_ref, scale, sends, keeps):
     mine = core_ref[0]
     at = 0
     for send, keep in zip(sends, keeps):
         h = send.shape[0]
-        keep[...] = total_ref[pl.ds(pl.multiple_of(at + mine * h, 8), h)]
-        send[...] = total_ref[pl.ds(pl.multiple_of(at + (1 - mine) * h, 8), h)]
+        keep[...] = total_ref[pl.ds(pl.multiple_of(at + mine * h, 8), h)] * scale
+        send[...] = total_ref[pl.ds(pl.multiple_of(at + (1 - mine) * h, 8), h)] * scale
         at += 2 * h
 
 
@@ -162,8 +166,7 @@
 
     @pl.when(step == pl.num_programs(0) - 1)
     def _():
-        acc[...] = acc[...] * scale
-        deal(core_ref, acc, sends, keeps)
+        deal(core_ref, acc, scale, sends, keeps)
 
 
 def first_kernel(parts, scale, core_ref, *refs):
@@ -216,16 +219,17 @@
     high, low = split(once - dot(e_ref[...], sb_ref[...]))
     hi_ref[...] = high
     lo_ref[...] = low
-    ht, lt = high.T, low.T
-    acc[:p] += dot(ht, high)
-    hl[...] += dot(ht, low)
-    acc[p:] += dot(ht, x_ref[:, p:]) + dot(lt, x_ref[:, p:])
+    both = jnp.concatenate([high.T, low.T], axis=0)
+    square = dot(both, high)
+    acc[:p] += square[:p]
+    hl[...] += square[p:]
+    other_two = dot(both, x_ref[:, p:])
+    acc[p:] += other_two[:p] + other_two[p:]
 
     @pl.when(step == pl.num_programs(0) - 1)
     def _():
         acc[:p] = acc[:p] + hl[...] + hl[...].T
-        acc[...] = acc[...] * scale
-        deal(core_ref, acc, [send], [keep])
+        deal(core_ref, acc, scale, [send], [keep])
 
 
 def second_kernel(parts, scale, core_ref, own, other, z_ref, h_ref, b2_ref, e_ref, u_ref, hi_ref, lo_ref, l_ref, *refs):
@@ -246,16 +250,18 @@
         ih[...] = high
         il[...] = low
         d = full(inv, total[p:])
-        d_b = wide(d.astype(BF16))
-        db[...] = d.astype(BF16)
-        against = h_ref[...]
-        at = against.T
-        upper = (z_ref[...] - full(against, full(invt, d_b))).astype(BF16)
+        d_b = d.astype(BF16)
+        db[...] = d_b
+        inv_s = split(inv)
+        against = split(h_ref[...])
+        at = split(h_ref[...].T)
+        turned = split(dot(high, d_b) + dot(low, d_b))
+        upper = (z_ref[...] - thrice(against, turned)).astype(BF16)
         ub[...] = upper
-        lower = (d - d_b) - full(inv, full(at, wide(b2_ref[...])))
+        lower = (d - wide(d_b)) - thrice(inv_s, split(dot(at[0], b2_ref[...]) + dot(at[1], b2_ref[...])))
         lower_b = lower.astype(BF16)
         lb[...] = lower_b
-        x_ref[...] = (lower - wide(lower_b)) - full(inv, full(at, wide(upper)))
+        x_ref[...] = (lower - wide(lower_b)) - thrice(inv_s, split(dot(at[0], upper) + dot(at[1], upper)))
         acc[...] = jnp.zeros_like(acc)
         hl[...] = jnp.zeros_like(hl)
 
@@ -266,20 +272,21 @@
     high, low = split(once - dot(e_ref[...], ub[...]) - dot(q, lb[...]))
     hi2_ref[...] = high
     lo2_ref[...] = low
-    ht, lt, qt = high.T, low.T, q.T
-    acc[:p] += dot(ht, high)
-    hl[...] += dot(ht, low)
-    acc[p:2 * p] += dot(qt, high) + dot(qt, low)
+    qt = q.T
+    left = jnp.concatenate([high.T, low.T, qt], axis=0)
+    square = dot(left, high)
+    acc[:p] += square[:p]
+    hl[...] += square[p:2 * p]
+    acc[p:2 * p] += square[2 * p:] + dot(qt, low)
     for c in range(2):
-        right = l_ref[:, c * p:(c + 1) * p]
-        acc[(2 + c) * p:(3 + c) * p] += dot(ht, right) + dot(lt, right)
-        acc[(4 + c) * p:(5 + c) * p] += dot(qt, right)
+        mixed = dot(left, l_ref[:, c * p:(c + 1) * p])
+        acc[(2 + c) * p:(3 + c) * p] += mixed[:p] + mixed[p:2 * p]
+        acc[(4 + c) * p:(5 + c) * p] += mixed[2 * p:]
 
     @pl.when(step == pl.num_programs(0) - 1)
     def _():
         acc[:p] = acc[:p] + hl[...] + hl[...].T
-        acc[...] = acc[...] * scale
-        deal(core_ref, acc, sends, keeps)
+        deal(core_ref, acc, scale, sends, keeps)
 
 
 def last_kernel(parts, core_ref, *refs):
@@ -292,23 +299,26 @@
         place(core_ref, list(zip(own, other)), total)
         res = total[p:2 * p]
         off = res - x_ref[...]
-        offt = off.T
-        cut = full(offt, res)
-        r_ref[...] = total[:p] - cut - cut.T + full(offt, off)
+        off_b = off.astype(BF16)
+        offt = off.T.astype(BF16)
+        cut = dot(offt, res.astype(BF16))
+        r_ref[...] = total[:p] - cut - cut.T + dot(offt, off_b)
         factor(r_ref, m_ref)
         inv = m_ref[...]
         invt = inv.T
         high, low = split(invt)
         ih[...] = high
         il[...] = low
-        back[...] = full(off, invt).astype(BF16)
+        back[...] = dot(off_b, high).astype(BF16)
+        inv_s = split(inv)
         factors[0] = r1_ref[...]
         factors[1] = r_ref[...]
         for c in range(2):
             cols = slice(c * p, (c + 1) * p)
             early = total[(4 + c) * p:(5 + c) * p]
             shift[:p, cols] = early
-            shift[p:, cols] = full(inv, total[(2 + c) * p:(3 + c) * p] - full(offt, early))
+            late = total[(2 + c) * p:(3 + c) * p] - dot(offt, early.astype(BF16))
+            shift[p:, cols] = thrice(inv_s, split(late))
 
     high, low = hi_ref[...], lo_ref[...]
     q = dot(high, ih[...]) + dot(high, il[...]) + dot(low, ih[...]) - dot(q_ref[...], back[...])
@@ -348,6 +358,16 @@
     return parts, [exchange(x, "grp", 0) for x in parts]
 
 
+def summed_at_once(send, keep):
+    size = lax.axis_size("rows")
+    x = keep + exchange(send, "grp", 0)
+    got = lax.all_to_all(x, "rows", 0, 0, tiled=True)
+    mine = got.reshape(size, x.shape[0] // size, x.shape[1]).sum(0)
+    same = jnp.broadcast_to(mine[None], (size,) + mine.shape).reshape(x.shape)
+    x = lax.all_to_all(same, "rows", 0, 0, tiled=True)
+    return x, exchange(x, "grp", 0)
+
+
 def body(earlier, snapshots, later):
     n, k = earlier.shape
     p = snapshots.shape[1] // 2
@@ -358,8 +378,7 @@
     rows = (2 * blocks + blocks * (blocks + 1) // 2) * p
     unit = 2 * devices * 8
     parts = 3 if rows % (3 * unit) == 0 else 1
-    tile = 512 if n % 512 == 0 else n
-    tall = 1024 if n % 1024 == 0 else tile
+    tile = 1024 if n % 1024 == 0 else n
 
     def smem():
         return pl.BlockSpec(memory_space=pltpu.SMEM)
@@ -367,16 +386,16 @@
     def whole(*shape):
         return pl.BlockSpec(shape, lambda i: (0,) * len(shape))
 
-    def tiled(cols, height=tile):
-        return pl.BlockSpec((height, cols), lambda i: (i, 0))
+    def tiled(cols):
+        return pl.BlockSpec((tile, cols), lambda i: (i, 0))
 
     def shape(*dims, dtype=F32):
         return jax.ShapeDtypeStruct(dims, dtype)
 
-    def call(kernel, name, steps, ins, outs, scratch, flops, size, *args):
+    def call(kernel, name, room, ins, outs, scratch, flops, size, *args):
         return pl.pallas_call(
             kernel,
-            grid=(steps,),
+            grid=(n // tile,),
             in_specs=[s for s in ins],
             out_specs=[s for s, _ in outs],
             out_shape=[s for _, s in outs],
@@ -384,15 +403,15 @@
             name=name,
             cost_estimate=pl.CostEstimate(flops=flops, bytes_accessed=size, transcendentals=0),
             compiler_params=pltpu.CompilerParams(
-                dimension_semantics=("arbitrary",), vmem_limit_bytes=VMEM_BYTES
+                dimension_semantics=("arbitrary",), vmem_limit_bytes=room * MIB
             ),
         )(*args)
 
     half = rows // parts // 2
     halves = [(whole(half, p), shape(half, p))] * (2 * parts)
     got = call(
-        lambda *r: cross_kernel(parts, scale, *r), "cross", n // tall,
-        [smem(), tiled(k, tall), tiled(2 * p, tall)],
+        lambda *r: cross_kernel(parts, scale, *r), "cross", 32,
+        [smem(), tiled(k), tiled(2 * p)],
         halves,
         [pltpu.VMEM((rows, p), F32)],
         2 * n * rows * p, 2 * n * (k + 2 * p),
@@ -401,7 +420,7 @@
     own, other = summed(got[:parts], got[parts:], 1)
 
     u, hi, lo, z, h, b2, send, keep = call(
-        lambda *r: first_kernel(parts, scale, *r), "first", n // tile,
+        lambda *r: first_kernel(parts, scale, *r), "first", 48,
         [smem()] + [whole(half, p)] * (2 * parts) + [tiled(k), tiled(2 * p)],
         [
             (tiled(p), shape(n, p)),
@@ -425,10 +444,10 @@
         2 * n * p * (3 * k + 4 * p) + 12 * k * k * p, n * (2 * k + 12 * p),
         core, *own, *other, earlier, snapshots,
     )
-    (own,), (other,) = summed([send], [keep], 2)
+    own, other = summed_at_once(send, keep)
 
     got = call(
-        lambda *r: second_kernel(3, scale, *r), "second", n // tile,
+        lambda *r: second_kernel(3, scale, *r), "second", 44,
         [smem(), whole(p, p), whole(p, p), whole(k, p), whole(k, p), whole(k, p),
          tiled(k), tiled(p), tiled(p), tiled(p), tiled(2 * p)],
         [
@@ -456,7 +475,7 @@
     own, other = summed(got[5:8], got[8:], 2)
 
     return tuple(call(
-        lambda *r: last_kernel(3, *r), "last", n // tile,
+        lambda *r: last_kernel(3, *r), "last", 30,
         [smem()] + [whole(p, p)] * 8 + [tiled(p)] * 3,
         [
             (tiled(2 * p), shape(n, 2 * p, dtype=BF16)),

time: 243 us -> 232 us (0.955)
  blocking collectives: 0 us -> 27.4 us
  Pallas kernels: 96.1 us -> 78.5 us
  waiting for transfers between devices: 78.1 us -> 61.3 us
  starting transfers between devices: 54.3 us -> 43 us
  local copies, waits for them, and re-layouts: 4.38 us -> 12.4 us
    all_to_all x0 -> x2, blocking collectives: none -> 27.4 us  [the longest x1 14.7 us: summed_at_once(): got = lax.all_to_all(x, 'rows', 0, 0, tiled=True)]
    pallas_call x4, Pallas kernels: 96.1 us -> 78.5 us  [call(): pl.pallas_call(kernel, grid=(n // tile,), in_specs=[s for s in ins], out_...]
    ppermute x59 -> x53, waiting for transfers between devices: 78.1 us -> 61.3 us  [exchange(): return lax.ppermute(x, axis, [(i, i ^ 1 << bit) for i in range(size)])]
    ppermute x59 -> x53, starting transfers between devices: 54.3 us -> 43 us  [exchange(): return lax.ppermute(x, axis, [(i, i ^ 1 << bit) for i in range(size)])]
    unnamed x32 -> x22, local copies, waits for them, and re-layouts: 3.26 us -> 11.3 us
    add x7 -> x6, other arithmetic: 6.74 us -> 6.65 us  [summed(): keep + exchange(send, 'grp', 0)]
  transfers between devices with their start and end apart: 59 -> 53, of which waited for: 45 -> 38; matrix products, arithmetic and copies ran while one was open for 3% -> 4% of each run, Pallas kernels for 0% -> 0%
where the time goes in v2:
time: 232 us
  Pallas kernels  78.5 us (34%)
  waiting for transfers between devices  61.3 us (26%)
  starting transfers between devices  43 us (19%)
  blocking collectives  27.4 us (12%)
  local copies, waits for them, and re-layouts  12.4 us (5%)
  other arithmetic  7.92 us (3%)
    pallas_call x4, Pallas kernels, call(): pl.pallas_call(kernel, grid=(n // tile,), in_specs=[s for s in ins], out_...  78.5 us
    ppermute x53, waiting for transfers between devices, exchange(): return lax.ppermute(x, axis, [(i, i ^ 1 << bit) for i in range(size)])  61.3 us
    ppermute x53, starting transfers between devices, exchange(): return lax.ppermute(x, axis, [(i, i ^ 1 << bit) for i in range(size)])  43 us
    all_to_all x1, blocking collectives, summed_at_once(): got = lax.all_to_all(x, 'rows', 0, 0, tiled=True)  14.7 us
    all_to_all x1, blocking collectives, summed_at_once(): x = lax.all_to_all(same, 'rows', 0, 0, tiled=True)  12.8 us
    unnamed x22, local copies, waits for them, and re-layouts  11.3 us
    add x6, other arithmetic, summed(): keep + exchange(send, 'grp', 0)  6.65 us
  transfers between devices with their start and end apart: 53, of which 38 were waited for; matrix products, arithmetic and copies ran while one was open for 4% of the time, Pallas kernels for 0%

profile of v2, /device:TPU:0, one launch (start us, length us, event | category | flops | bytes accessed | tf_op | source)
XLA Modules:
  0.0 231.8 jit_solution(12698162910294245125)
XLA Ops:
  0.6 3.4 %copy-done.3 = bf16[4096,1024]{1,0:T(8,128)(2,1)S(1)} copy-done((bf16[4096,1024]{1,0:T(8,128)(2,1)S(1)}, bf16[4096,1024]{1,0:T(8,128)(2,1)}, u32[]{:S(2)}) %copy-start.3) | copy-done | bytes 8388632
  4.0 2.2 copy-done.4
  6.2 12.7 %cross.1 = (f32[768,256]{1,0:T(8,128)S(1)}, f32[768,256]{1,0:T(8,128)}, f32[768,256]{1,0:T(8,128)}, f32[768,256]{1,0:T(8,128)S(1)}, f32[768,256]{1,0:T(8,128)S(1)}, /*index=5*/f32[768,256]{1,0:T(8,128)S(1)}) custom-call(s32[1]{0:T(128)} %bitcast.r_0_, bf16[4096,1024]{1,0:T(8,128)(2,1)S(1)} %copy-done.3, bf16[4096,512]{1,0:T(8,128)(2,1)S(1)} %copy-done.4), custom_call_target="tpu_custom_call" | custom-call | flops 9663676416 | bytes 12582912 | tf_op jit(solution)/shard_map/cross/pallas_call | solution.py:396
  19.9 1.7 collective-permute-done.16
  24.5 2.9 %collective-permute-start.17 = (f32[384,256]{1,0:T(8,128)}, f32[384,256]{1,0:T(8,128)S(1)}, u32[]{:S(2)}, u32[]{:S(2)}) collective-permute-start(f32[384,256]{1,0:T(8,128)} %constant_dynamic-slice_fusion.8), channel_id=1, source_target_pairs={{0,8},{2,10},{4,12},{6,14},{8,0},{10,2},{12,4},{14,6},{16,24},{18,... | collective-permute-start | bytes 1179656 | tf_op jit(solution)/shard_map/ppermute | solution.py:331
  33.2 3.9 %collective-permute-done.17 = f32[384,256]{1,0:T(8,128)S(1)} collective-permute-done((f32[384,256]{1,0:T(8,128)}, f32[384,256]{1,0:T(8,128)S(1)}, u32[]{:S(2)}, u32[]{:S(2)}) %collective-permute-start.17) | collective-permute-done | bytes 393248 | tf_op jit(solution)/shard_map/ppermute | solution.py:331
  40.7 3.1 %collective-permute-done.1 = f32[384,256]{1,0:T(8,128)S(1)} collective-permute-done((f32[384,256]{1,0:T(8,128)S(1)}, f32[384,256]{1,0:T(8,128)S(1)}, u32[]{:S(2)}, u32[]{:S(2)}) %collective-permute-start.1) | collective-permute-done | bytes 393248 | tf_op jit(solution)/shard_map/ppermute | solution.py:331
  44.4 2.1 collective-permute-done.18
  48.8 1.9 collective-permute-done.2
  51.7 2.7 %collective-permute-start.20 = (f32[96,256]{1,0:T(8,128)S(1)}, f32[96,256]{1,0:T(8,128)S(1)}, u32[]{:S(2)}, u32[]{:S(2)}) collective-permute-start(f32[96,256]{1,0:T(8,128)S(1)} %dynamic-slice_add_fusion.9), channel_id=1, source_target_pairs={{0,16},{2,18},{4,20},{6,22},{8,24},{10,26},{12,28},{14,30},{16,0},... | collective-permute-start | bytes 294920 | tf_op jit(solution)/shard_map/ppermute | solution.py:331
  56.4 2.7 %collective-permute-start.4 = (f32[96,256]{1,0:T(8,128)S(1)}, f32[96,256]{1,0:T(8,128)S(1)}, u32[]{:S(2)}, u32[]{:S(2)}) collective-permute-start(f32[96,256]{1,0:T(8,128)S(1)} %dynamic-slice_add_fusion.11), channel_id=1, source_target_pairs={{0,16},{2,18},{4,20},{6,22},{8,24},{10,26},{12,28},{14,30},{16,0},... | collective-permute-start | bytes 294920 | tf_op jit(solution)/shard_map/ppermute | solution.py:331
  59.1 4.4 %collective-permute-done.20 = f32[96,256]{1,0:T(8,128)S(1)} collective-permute-done((f32[96,256]{1,0:T(8,128)S(1)}, f32[96,256]{1,0:T(8,128)S(1)}, u32[]{:S(2)}, u32[]{:S(2)}) %collective-permute-start.20) | collective-permute-done | bytes 98336 | tf_op jit(solution)/shard_map/ppermute | solution.py:331
  63.8 1.7 collective-permute-done.12
  75.1 4.0 %collective-permute-done.14 = f32[192,256]{1,0:T(8,128)S(1)} collective-permute-done((f32[192,256]{1,0:T(8,128)S(1)}, f32[192,256]{1,0:T(8,128)S(1)}, u32[]{:S(2)}, u32[]{:S(2)}) %collective-permute-start.14) | collective-permute-done | bytes 196640 | tf_op jit(solution)/shard_map/ppermute | solution.py:331
  81.8 3.0 %collective-permute-done.23 = f32[384,256]{1,0:T(8,128)S(1)} collective-permute-done((f32[384,256]{1,0:T(8,128)S(1)}, f32[384,256]{1,0:T(8,128)S(1)}, u32[]{:S(2)}, u32[]{:S(2)}) %collective-permute-start.23) | collective-permute-done | bytes 393248 | tf_op jit(solution)/shard_map/ppermute | solution.py:331
  85.0 2.0 collective-permute-done.15
  91.0 21.4 %first.1 = (f32[4096,256]{1,0:T(8,128)}, bf16[4096,256]{1,0:T(8,128)(2,1)}, bf16[4096,256]{1,0:T(8,128)(2,1)}, f32[1024,256]{1,0:T(8,128)}, f32[1024,256]{1,0:T(...) custom-call(s32[1]{0:T(128)} %bitcast.r_0_, ...), custom_call_target="tpu_custom_call" | custom-call | flops 11811160064 | bytes 20971520 | tf_op jit(solution)/shard_map/first/pallas_call | solution.py:396
  114.1 14.7 %all_to_all.17 = f32[16,16,256]{2,1,0:T(8,128)S(1)} all-to-all(f32[16,16,256]{2,1,0:T(8,128)S(1)} %bitcast.5), channel_id=1, replica_groups=mesh['rows'=16,'grp'=2] {'rows'}, dimensions={0} | all-to-all | bytes 524288 | tf_op jit(solution)/shard_map/all_to_all | solution.py:364
  128.8 12.8 %all_to_all.18 = f32[16,16,256]{2,1,0:T(8,128)S(1)} all-to-all(f32[16,16,256]{2,1,0:T(8,128)S(1)} %broadcast_in_dim.2), channel_id=1, replica_groups=mesh['rows'=16,'grp'=2] {'rows'}, dimensions={0} | all-to-all | bytes 524288 | tf_op jit(solution)/shard_map/all_to_all | solution.py:367
  146.6 30.1 %second.1 = (bf16[4096,256]{1,0:T(8,128)(2,1)S(1)}, bf16[4096,256]{1,0:T(8,128)(2,1)S(1)}, bf16[4096,256]{1,0:T(8,128)(2,1)}, f32[256,256]{1,0:T(8,128)S(1)}, f3...) custom-call(s32[1]{0:T(128)} %bitcast.r_0_, ...), custom_call_target="tpu_custom_call" | custom-call | flops 10200547328 | bytes 27262976 | tf_op jit(solution)/shard_map/second/pallas_call | solution.py:396
  204.3 2.2 collective-permute-done.33
  210.9 2.2 collective-permute-done.49
  213.9 2.0 collective-permute-done.35
  217.5 14.3 %last.1 = (bf16[4096,512]{1,0:T(8,128)(2,1)}, f32[2,256,256]{2,1,0:T(8,128)}, f32[512,512]{1,0:T(8,128)}) custom-call(s32[1]{0:T(128)} %bitcast.r_0_, f32[256,256]{1,0:T(8,128)S(1)} %pad_maximum_fusion.6.r_1_, f32[256,256]{1,0:T(8,128)S(1)} %pad_maximum_fusion.7.r_2_, f32[256,256]{1,0:T(8,128)S(1)} %pad_maximum_fusion.8.r_3_, ...), custom_call_target="tpu_custom_call" | custom-call | flops 2147483648 | bytes 10485760 | tf_op jit(solution)/shard_map/last/pallas_call | solution.py:396
  (188 shorter events, 76.6 us)
Async XLA Ops:
  19.4 8.1 %collective-permute-start.8 = (f32[768,256]{1,0:T(8,128)}, f32[768,256]{1,0:T(8,128)}, u32[]{:S(2)}, u32[]{:S(2)}) collective-permute-start(f32[768,256]{1,0:T(8,128)} %get-tuple-element.31), channel_id=1, source_target_pairs={{0,1},{1,0},{2,3},{3,2},{4,5},{5,4},{6,7},{7,6},{8,9},{9,8},{10,11... | collective-permute-start | bytes 2359304 | tf_op jit(solution)/shard_map/ppermute | solution.py:331
  19.5 10.9 %collective-permute-start = (f32[768,256]{1,0:T(8,128)S(1)}, f32[768,256]{1,0:T(8,128)}, u32[]{:S(2)}, u32[]{:S(2)}) collective-permute-start(f32[768,256]{1,0:T(8,128)S(1)} %get-tuple-element.29), channel_id=1, source_target_pairs={{0,1},{1,0},{2,3},{3,2},{4,5},{5,4},{6,7},{7,6},{8,9},{9,8},{10,11... | collective-permute-start | bytes 2359304 | tf_op jit(solution)/shard_map/ppermute | solution.py:331
  24.5 12.6 %collective-permute-start.17 = (f32[384,256]{1,0:T(8,128)}, f32[384,256]{1,0:T(8,128)S(1)}, u32[]{:S(2)}, u32[]{:S(2)}) collective-permute-start(f32[384,256]{1,0:T(8,128)} %constant_dynamic-slice_fusion.8), channel_id=1, source_target_pairs={{0,8},{2,10},{4,12},{6,14},{8,0},{10,2},{12,4},{14,6},{16,24},{18,... | collective-permute-start | bytes 1179656 | tf_op jit(solution)/shard_map/ppermute | solution.py:331
  28.8 10.9 %collective-permute-start.9 = (f32[384,256]{1,0:T(8,128)S(1)}, f32[384,256]{1,0:T(8,128)S(1)}, u32[]{:S(2)}, u32[]{:S(2)}) collective-permute-start(f32[384,256]{1,0:T(8,128)S(1)} %constant_dynamic-slice_fusion.11), channel_id=1, source_target_pairs={{0,4},{2,6},{4,0},{6,2},{8,12},{10,14},{12,8},{14,10},{16,20},{18,... | collective-permute-start | bytes 1179656 | tf_op jit(solution)/shard_map/ppermute | solution.py:331
  31.6 12.1 %collective-permute-start.1 = (f32[384,256]{1,0:T(8,128)S(1)}, f32[384,256]{1,0:T(8,128)S(1)}, u32[]{:S(2)}, u32[]{:S(2)}) collective-permute-start(f32[384,256]{1,0:T(8,128)S(1)} %constant_dynamic-slice_fusion.14), channel_id=1, source_target_pairs={{0,2},{2,0},{4,6},{6,4},{8,10},{10,8},{12,14},{14,12},{16,18},{18,... | collective-permute-start | bytes 1179656 | tf_op jit(solution)/shard_map/ppermute | solution.py:331
  37.2 9.3 %collective-permute-start.18 = (f32[192,256]{1,0:T(8,128)S(1)}, f32[192,256]{1,0:T(8,128)S(1)}, u32[]{:S(2)}, u32[]{:S(2)}) collective-permute-start(f32[192,256]{1,0:T(8,128)S(1)} %constant_dynamic-slice_fusion.7), channel_id=1, source_target_pairs={{0,2},{2,0},{4,6},{6,4},{8,10},{10,8},{12,14},{14,12},{16,18},{18,... | collective-permute-start | bytes 589832 | tf_op jit(solution)/shard_map/ppermute | solution.py:331
  39.8 7.3 %collective-permute-start.10 = (f32[192,256]{1,0:T(8,128)S(1)}, f32[192,256]{1,0:T(8,128)S(1)}, u32[]{:S(2)}, u32[]{:S(2)}) collective-permute-start(f32[192,256]{1,0:T(8,128)S(1)} %constant_dynamic-slice_fusion.10), channel_id=1, source_target_pairs={{0,8},{2,10},{4,12},{6,14},{8,0},{10,2},{12,4},{14,6},{16,24},{18,... | collective-permute-start | bytes 589832 | tf_op jit(solution)/shard_map/ppermute | solution.py:331
  43.8 6.8 %collective-permute-start.2 = (f32[192,256]{1,0:T(8,128)S(1)}, f32[192,256]{1,0:T(8,128)S(1)}, u32[]{:S(2)}, u32[]{:S(2)}) collective-permute-start(f32[192,256]{1,0:T(8,128)S(1)} %constant_dynamic-slice_fusion.13), channel_id=1, source_target_pairs={{0,4},{2,6},{4,0},{6,2},{8,12},{10,14},{12,8},{14,10},{16,20},{18,... | collective-permute-start | bytes 589832 | tf_op jit(solution)/shard_map/ppermute | solution.py:331
  47.2 7.2 %collective-permute-start.11 = (f32[96,256]{1,0:T(8,128)S(1)}, f32[96,256]{1,0:T(8,128)S(1)}, u32[]{:S(2)}, u32[]{:S(2)}) collective-permute-start(f32[96,256]{1,0:T(8,128)S(1)} %constant_dynamic-slice_fusion.9), channel_id=1, source_target_pairs={{0,2},{2,0},{4,6},{6,4},{8,10},{10,8},{12,14},{14,12},{16,18},{18,... | collective-permute-start | bytes 294920 | tf_op jit(solution)/shard_map/ppermute | solution.py:331
  50.7 5.7 %collective-permute-start.3 = (f32[96,256]{1,0:T(8,128)S(1)}, f32[96,256]{1,0:T(8,128)S(1)}, u32[]{:S(2)}, u32[]{:S(2)}) collective-permute-start(f32[96,256]{1,0:T(8,128)S(1)} %constant_dynamic-slice_fusion.12), channel_id=1, source_target_pairs={{0,8},{2,10},{4,12},{6,14},{8,0},{10,2},{12,4},{14,6},{16,24},{18,... | collective-permute-start | bytes 294920 | tf_op jit(solution)/shard_map/ppermute | solution.py:331
  51.7 11.8 %collective-permute-start.20 = (f32[96,256]{1,0:T(8,128)S(1)}, f32[96,256]{1,0:T(8,128)S(1)}, u32[]{:S(2)}, u32[]{:S(2)}) collective-permute-start(f32[96,256]{1,0:T(8,128)S(1)} %dynamic-slice_add_fusion.9), channel_id=1, source_target_pairs={{0,16},{2,18},{4,20},{6,22},{8,24},{10,26},{12,28},{14,30},{16,0},... | collective-permute-start | bytes 294920 | tf_op jit(solution)/shard_map/ppermute | solution.py:331
  54.4 11.1 %collective-permute-start.12 = (f32[96,256]{1,0:T(8,128)S(1)}, f32[96,256]{1,0:T(8,128)S(1)}, u32[]{:S(2)}, u32[]{:S(2)}) collective-permute-start(f32[96,256]{1,0:T(8,128)S(1)} %dynamic-slice_add_fusion.10), channel_id=1, source_target_pairs={{0,16},{2,18},{4,20},{6,22},{8,24},{10,26},{12,28},{14,30},{16,0},... | collective-permute-start | bytes 294920 | tf_op jit(solution)/shard_map/ppermute | solution.py:331
  56.4 10.6 %collective-permute-start.4 = (f32[96,256]{1,0:T(8,128)S(1)}, f32[96,256]{1,0:T(8,128)S(1)}, u32[]{:S(2)}, u32[]{:S(2)}) collective-permute-start(f32[96,256]{1,0:T(8,128)S(1)} %dynamic-slice_add_fusion.11), channel_id=1, source_target_pairs={{0,16},{2,18},{4,20},{6,22},{8,24},{10,26},{12,28},{14,30},{16,0},... | collective-permute-start | bytes 294920 | tf_op jit(solution)/shard_map/ppermute | solution.py:331
  65.5 5.7 %collective-permute-start.13 = (f32[96,256]{1,0:T(8,128)S(1)}, f32[96,256]{1,0:T(8,128)S(1)}, u32[]{:S(2)}, u32[]{:S(2)}) collective-permute-start(f32[96,256]{1,0:T(8,128)S(1)} %add.204), channel_id=1, source_target_pairs={{0,2},{2,0},{4,6},{6,4},{8,10},{10,8},{12,14},{14,12},{16,18},{18,... | collective-permute-start | bytes 294920 | tf_op jit(solution)/shard_map/ppermute | solution.py:331
  68.3 5.7 %collective-permute-start.22 = (f32[192,256]{1,0:T(8,128)S(1)}, f32[192,256]{1,0:T(8,128)S(1)}, u32[]{:S(2)}, u32[]{:S(2)}) collective-permute-start(f32[192,256]{1,0:T(8,128)S(1)} %pad_maximum_fusion.11), channel_id=1, source_target_pairs={{0,2},{2,0},{4,6},{6,4},{8,10},{10,8},{12,14},{14,12},{16,18},{18,... | collective-permute-start | bytes 589832 | tf_op jit(solution)/shard_map/ppermute | solution.py:331
  71.3 7.8 %collective-permute-start.14 = (f32[192,256]{1,0:T(8,128)S(1)}, f32[192,256]{1,0:T(8,128)S(1)}, u32[]{:S(2)}, u32[]{:S(2)}) collective-permute-start(f32[192,256]{1,0:T(8,128)S(1)} %pad_maximum_fusion.10), channel_id=1, source_target_pairs={{0,8},{2,10},{4,12},{6,14},{8,0},{10,2},{12,4},{14,6},{16,24},{18,... | collective-permute-start | bytes 589832 | tf_op jit(solution)/shard_map/ppermute | solution.py:331
  72.8 7.8 %collective-permute-start.6 = (f32[192,256]{1,0:T(8,128)S(1)}, f32[192,256]{1,0:T(8,128)S(1)}, u32[]{:S(2)}, u32[]{:S(2)}) collective-permute-start(f32[192,256]{1,0:T(8,128)S(1)} %pad_maximum_fusion.9), channel_id=1, source_target_pairs={{0,4},{2,6},{4,0},{6,2},{8,12},{10,14},{12,8},{14,10},{16,20},{18,... | collective-permute-start | bytes 589832 | tf_op jit(solution)/shard_map/ppermute | solution.py:331
  74.1 10.7 %collective-permute-start.23 = (f32[384,256]{1,0:T(8,128)S(1)}, f32[384,256]{1,0:T(8,128)S(1)}, u32[]{:S(2)}, u32[]{:S(2)}) collective-permute-start(f32[384,256]{1,0:T(8,128)S(1)} %pad_maximum_fusion.5), channel_id=1, source_target_pairs={{0,8},{2,10},{4,12},{6,14},{8,0},{10,2},{12,4},{14,6},{16,24},{18,... | collective-permute-start | bytes 1179656 | tf_op jit(solution)/shard_map/ppermute | solution.py:331
  79.1 7.8 %collective-permute-start.15 = (f32[384,256]{1,0:T(8,128)S(1)}, f32[384,256]{1,0:T(8,128)S(1)}, u32[]{:S(2)}, u32[]{:S(2)}) collective-permute-start(f32[384,256]{1,0:T(8,128)S(1)} %pad_maximum_fusion.4), channel_id=1, source_target_pairs={{0,4},{2,6},{4,0},{6,2},{8,12},{10,14},{12,8},{14,10},{16,20},{18,... | collective-permute-start | bytes 1179656 | tf_op jit(solution)/shard_map/ppermute | solution.py:331
  80.7 7.8 %collective-permute-start.7 = (f32[384,256]{1,0:T(8,128)S(1)}, f32[384,256]{1,0:T(8,128)S(1)}, u32[]{:S(2)}, u32[]{:S(2)}) collective-permute-start(f32[384,256]{1,0:T(8,128)S(1)} %pad_maximum_fusion.3), channel_id=1, source_target_pairs={{0,2},{2,0},{4,6},{6,4},{8,10},{10,8},{12,14},{14,12},{16,18},{18,... | collective-permute-start | bytes 1179656 | tf_op jit(solution)/shard_map/ppermute | solution.py:331
  184.9 5.7 %collective-permute-start.30 = (f32[128,256]{1,0:T(8,128)S(1)}, f32[128,256]{1,0:T(8,128)S(1)}, u32[]{:S(2)}, u32[]{:S(2)}) collective-permute-start(f32[128,256]{1,0:T(8,128)S(1)} %constant_dynamic-slice_fusion.5), channel_id=1, source_target_pairs={{0,2},{2,0},{4,6},{6,4},{8,10},{10,8},{12,14},{14,12},{16,18},{18,... | collective-permute-start | bytes 393224 | tf_op jit(solution)/shard_map/ppermute | solution.py:331
  196.4 6.0 %collective-permute-start.47 = (f32[64,256]{1,0:T(8,128)S(1)}, f32[64,256]{1,0:T(8,128)S(1)}, u32[]{:S(2)}, u32[]{:S(2)}) collective-permute-start(f32[64,256]{1,0:T(8,128)S(1)} %add.242), channel_id=1, source_target_pairs={{0,16},{2,18},{4,20},{6,22},{8,24},{10,26},{12,28},{14,30},{16,0},... | collective-permute-start | bytes 196616 | tf_op jit(solution)/shard_map/ppermute | solution.py:331
  197.8 6.0 %collective-permute-start.40 = (f32[64,256]{1,0:T(8,128)S(1)}, f32[64,256]{1,0:T(8,128)S(1)}, u32[]{:S(2)}, u32[]{:S(2)}) collective-permute-start(f32[64,256]{1,0:T(8,128)S(1)} %add.233), channel_id=1, source_target_pairs={{0,16},{2,18},{4,20},{6,22},{8,24},{10,26},{12,28},{14,30},{16,0},... | collective-permute-start | bytes 196616 | tf_op jit(solution)/shard_map/ppermute | solution.py:331
  200.6 5.9 %collective-permute-start.33 = (f32[64,256]{1,0:T(8,128)S(1)}, f32[64,256]{1,0:T(8,128)S(1)}, u32[]{:S(2)}, u32[]{:S(2)}) collective-permute-start(f32[64,256]{1,0:T(8,128)S(1)} %add.224), channel_id=1, source_target_pairs={{0,16},{2,18},{4,20},{6,22},{8,24},{10,26},{12,28},{14,30},{16,0},... | collective-permute-start | bytes 196616 | tf_op jit(solution)/shard_map/ppermute | solution.py:331
  (40 other events, 208.3 us)

commit v3 on v2

--- a/solution.py
+++ b/solution.py
@@ -171,8 +171,8 @@
 
 def first_kernel(parts, scale, core_ref, *refs):
     own, other = refs[:parts], refs[parts:2 * parts]
-    (e_ref, x_ref, u_ref, hi_ref, lo_ref, z_ref, h_ref, b2_ref, send, keep,
-     total, b_ref, sb_ref, offh, offl, acc, hl) = refs[2 * parts:]
+    (e_ref, x_ref, u_ref, w_ref, z_ref, h_ref, b2_ref, send, keep,
+     total, b_ref, offh, offl, acc, hl) = refs[2 * parts:]
     k = e_ref.shape[1]
     p = x_ref.shape[1] // 2
     step = pl.program_id(0)
@@ -205,7 +205,7 @@
             after = (coef - wide(b)) - dot(offh[...], b) - dot(offl[...], b)
             if c == 0:
                 sb = after.astype(BF16)
-                sb_ref[...] = sb
+                b_ref[:, 2 * p:] = sb
                 h_ref[...] = (after - wide(sb)) - dot(offh[...], sb) - dot(offl[...], sb)
             else:
                 z_ref[...] = after
@@ -215,10 +215,10 @@
 
     t = dot(e_ref[...], b_ref[...])
     once = wide((wide(x_ref[:, :p]) - t[:, :p]).astype(BF16))
-    u_ref[...] = wide(x_ref[:, p:]) - t[:, p:]
-    high, low = split(once - dot(e_ref[...], sb_ref[...]))
-    hi_ref[...] = high
-    lo_ref[...] = low
+    u_ref[...] = wide(x_ref[:, p:]) - t[:, p:2 * p]
+    high, low = split(once - t[:, 2 * p:])
+    w_ref[:, :p] = high
+    w_ref[:, p:] = low
     both = jnp.concatenate([high.T, low.T], axis=0)
     square = dot(both, high)
     acc[:p] += square[:p]
@@ -232,10 +232,10 @@
         deal(core_ref, acc, scale, [send], [keep])
 
 
-def second_kernel(parts, scale, core_ref, own, other, z_ref, h_ref, b2_ref, e_ref, u_ref, hi_ref, lo_ref, l_ref, *refs):
-    q_ref, hi2_ref, lo2_ref, r_ref, x_ref = refs[:5]
-    sends, keeps = refs[5:5 + parts], refs[5 + parts:5 + 2 * parts]
-    total, m_ref, ih, il, db, ub, lb, acc, hl = refs[5 + 2 * parts:]
+def second_kernel(parts, scale, core_ref, own, other, z_ref, h_ref, b2_ref, e_ref, u_ref, w_ref, l_ref, *refs):
+    q_ref, w2_ref, r_ref, x_ref = refs[:4]
+    sends, keeps = refs[4:4 + parts], refs[4 + parts:4 + 2 * parts]
+    total, m_ref, ih, il, db, ub, lb, acc, hl = refs[4 + 2 * parts:]
     p = r_ref.shape[0]
     step = pl.program_id(0)
 
@@ -247,7 +247,8 @@
         inv = m_ref[...]
         invt = inv.T
         high, low = split(invt)
-        ih[...] = high
+        ih[:p] = high
+        ih[p:] = high
         il[...] = low
         d = full(inv, total[p:])
         d_b = d.astype(BF16)
@@ -265,13 +266,12 @@
         acc[...] = jnp.zeros_like(acc)
         hl[...] = jnp.zeros_like(hl)
 
-    high, low = hi_ref[...], lo_ref[...]
-    q = (dot(high, ih[...]) + dot(high, il[...]) + dot(low, ih[...])).astype(BF16)
+    q = (dot(w_ref[...], ih[...]) + dot(w_ref[:, :p], il[...])).astype(BF16)
     q_ref[...] = q
     once = wide((u_ref[...] - dot(q, db[...])).astype(BF16))
     high, low = split(once - dot(e_ref[...], ub[...]) - dot(q, lb[...]))
-    hi2_ref[...] = high
-    lo2_ref[...] = low
+    w2_ref[:, :p] = high
+    w2_ref[:, p:] = low
     qt = q.T
     left = jnp.concatenate([high.T, low.T, qt], axis=0)
     square = dot(left, high)
@@ -291,7 +291,7 @@
 
 def last_kernel(parts, core_ref, *refs):
     own, other = refs[:parts], refs[parts:2 * parts]
-    x_ref, r1_ref, q_ref, hi_ref, lo_ref, basis, factors, shift, total, r_ref, m_ref, ih, il, back = refs[2 * parts:]
+    x_ref, r1_ref, q_ref, w_ref, basis, factors, shift, total, r_ref, m_ref, ih, il, back = refs[2 * parts:]
     p = r_ref.shape[0]
 
     @pl.when(pl.program_id(0) == 0)
@@ -307,7 +307,8 @@
         inv = m_ref[...]
         invt = inv.T
         high, low = split(invt)
-        ih[...] = high
+        ih[:p] = high
+        ih[p:] = high
         il[...] = low
         back[...] = dot(off_b, high).astype(BF16)
         inv_s = split(inv)
@@ -320,8 +321,7 @@
             late = total[(2 + c) * p:(3 + c) * p] - dot(offt, early.astype(BF16))
             shift[p:, cols] = thrice(inv_s, split(late))
 
-    high, low = hi_ref[...], lo_ref[...]
-    q = dot(high, ih[...]) + dot(high, il[...]) + dot(low, ih[...]) - dot(q_ref[...], back[...])
+    q = dot(w_ref[...], ih[...]) + dot(w_ref[:, :p], il[...]) - dot(q_ref[...], back[...])
     basis[:, :p] = q_ref[...]
     basis[:, p:] = q.astype(BF16)
 
@@ -329,6 +329,10 @@
 def exchange(x, axis, bit):
     size = lax.axis_size(axis)
     return lax.ppermute(x, axis, [(i, i ^ (1 << bit)) for i in range(size)])
+
+
+def swap(x, mask):
+    return lax.ppermute(x, "rows", [(i, i ^ mask) for i in range(lax.axis_size("rows"))])
 
 
 def summed(sends, keeps, tail):
@@ -359,12 +363,33 @@
 
 
 def summed_at_once(send, keep):
-    size = lax.axis_size("rows")
+    bits = lax.axis_size("rows").bit_length() - 1
+    me = lax.axis_index("rows")
     x = keep + exchange(send, "grp", 0)
-    got = lax.all_to_all(x, "rows", 0, 0, tiled=True)
-    mine = got.reshape(size, x.shape[0] // size, x.shape[1]).sum(0)
-    same = jnp.broadcast_to(mine[None], (size,) + mine.shape).reshape(x.shape)
-    x = lax.all_to_all(same, "rows", 0, 0, tiled=True)
+    levels = [(at, min(2, bits - at)) for at in range(0, bits, 2)]
+    for at, width in levels:
+        count = 1 << width
+        block = x.shape[0] // count
+        mine = (me >> at) & (count - 1)
+
+        def piece(m):
+            return lax.dynamic_slice_in_dim(x, (mine ^ m) * block, block, 0)
+
+        got = [piece(0)] + [swap(piece(m), m << at) for m in range(1, count)]
+        while len(got) > 1:
+            got = [a + b for a, b in zip(got[::2], got[1::2])]
+        x = got[0]
+    for at, width in reversed(levels):
+        count = 1 << width
+        mine = (me >> at) & (count - 1)
+        got = [x] + [swap(x, m << at) for m in range(1, count)]
+        order = []
+        for place_at in range(count):
+            pick = got[0]
+            for m in range(1, count):
+                pick = jnp.where((mine ^ m) == place_at, got[m], pick)
+            order.append(pick)
+        x = jnp.concatenate(order, axis=0)
     return x, exchange(x, "grp", 0)
 
 
@@ -391,6 +416,14 @@
 
     def shape(*dims, dtype=F32):
         return jax.ShapeDtypeStruct(dims, dtype)
+
+    def near(*dims, dtype=F32):
+        return pltpu.VMEM(dims, dtype)
+
+    def far(*dims, dtype=F32):
+        return pltpu.HBM(dims, dtype)
+
+    earlier, snapshots, later = (pltpu.with_memory_space_constraint(a, pltpu.HBM) for a in (earlier, snapshots, later))
 
     def call(kernel, name, room, ins, outs, scratch, flops, size, *args):
         return pl.pallas_call(
@@ -408,7 +441,7 @@
         )(*args)
 
     half = rows // parts // 2
-    halves = [(whole(half, p), shape(half, p))] * (2 * parts)
+    halves = [(whole(half, p), near(half, p))] * (2 * parts)
     got = call(
         lambda *r: cross_kernel(parts, scale, *r), "cross", 32,
         [smem(), tiled(k), tiled(2 * p)],
@@ -419,23 +452,21 @@
     )
     own, other = summed(got[:parts], got[parts:], 1)
 
-    u, hi, lo, z, h, b2, send, keep = call(
+    u, w, z, h, b2, send, keep = call(
         lambda *r: first_kernel(parts, scale, *r), "first", 48,
         [smem()] + [whole(half, p)] * (2 * parts) + [tiled(k), tiled(2 * p)],
         [
-            (tiled(p), shape(n, p)),
-            (tiled(p), shape(n, p, dtype=BF16)),
-            (tiled(p), shape(n, p, dtype=BF16)),
-            (whole(k, p), shape(k, p)),
-            (whole(k, p), shape(k, p)),
-            (whole(k, p), shape(k, p, dtype=BF16)),
-            (whole(p, p), shape(p, p)),
-            (whole(p, p), shape(p, p)),
+            (tiled(p), far(n, p)),
+            (tiled(2 * p), far(n, 2 * p, dtype=BF16)),
+            (whole(k, p), near(k, p)),
+            (whole(k, p), near(k, p)),
+            (whole(k, p), near(k, p, dtype=BF16)),
+            (whole(p, p), near(p, p)),
+            (whole(p, p), near(p, p)),
         ],
         [
             pltpu.VMEM((rows, p), F32),
-            pltpu.VMEM((k, 2 * p), BF16),
-            pltpu.VMEM((k, p), BF16),
+            pltpu.VMEM((k, 3 * p), BF16),
             pltpu.VMEM((k, k), BF16),
             pltpu.VMEM((k, k), BF16),
             pltpu.VMEM((2 * p, p), F32),
@@ -449,18 +480,17 @@
     got = call(
         lambda *r: second_kernel(3, scale, *r), "second", 44,
         [smem(), whole(p, p), whole(p, p), whole(k, p), whole(k, p), whole(k, p),
-         tiled(k), tiled(p), tiled(p), tiled(p), tiled(2 * p)],
+         tiled(k), tiled(p), tiled(2 * p), tiled(2 * p)],
         [
-            (tiled(p), shape(n, p, dtype=BF16)),
-            (tiled(p), shape(n, p, dtype=BF16)),
-            (tiled(p), shape(n, p, dtype=BF16)),
-            (whole(p, p), shape(p, p)),
-            (whole(p, p), shape(p, p)),
-        ] + [(whole(p, p), shape(p, p))] * 6,
+            (tiled(p), far(n, p, dtype=BF16)),
+            (tiled(2 * p), far(n, 2 * p, dtype=BF16)),
+            (whole(p, p), near(p, p)),
+            (whole(p, p), near(p, p)),
+        ] + [(whole(p, p), near(p, p))] * 6,
         [
             pltpu.VMEM((2 * p, p), F32),
             pltpu.VMEM((p, p), F32),
-            pltpu.VMEM((p, p), BF16),
+            pltpu.VMEM((2 * p, p), BF16),
             pltpu.VMEM((p, p), BF16),
             pltpu.VMEM((p, p), BF16),
             pltpu.VMEM((k, p), BF16),
@@ -469,14 +499,14 @@
             pltpu.VMEM((p, p), F32),
         ],
         2 * n * p * (k + 15 * p), n * (2 * k + 18 * p),
-        core, own, other, z, h, b2, earlier, u, hi, lo, later,
+        core, own, other, z, h, b2, earlier, u, w, later,
     )
-    q_one, hi2, lo2, r_one, expected = got[:5]
-    own, other = summed(got[5:8], got[8:], 2)
+    q_one, w2, r_one, expected = got[:4]
+    own, other = summed(got[4:7], got[7:], 2)
 
     return tuple(call(
         lambda *r: last_kernel(3, *r), "last", 30,
-        [smem()] + [whole(p, p)] * 8 + [tiled(p)] * 3,
+        [smem()] + [whole(p, p)] * 8 + [tiled(p), tiled(2 * p)],
         [
             (tiled(2 * p), shape(n, 2 * p, dtype=BF16)),
             (whole(2, p, p), shape(2, p, p)),
@@ -486,12 +516,12 @@
             pltpu.VMEM((6 * p, p), F32),
             pltpu.VMEM((p, p), F32),
             pltpu.VMEM((p, p), F32),
-            pltpu.VMEM((p, p), BF16),
+            pltpu.VMEM((2 * p, p), BF16),
             pltpu.VMEM((p, p), BF16),
             pltpu.VMEM((p, p), BF16),
         ],
         2 * n * p * 4 * p, n * 10 * p,
-        core, *own, *other, expected, r_one, q_one, hi2, lo2,
+        core, *own, *other, expected, r_one, q_one, w2,
     ))
 
 

time: 232 us -> 228 us (0.983)
  blocking collectives: 27.4 us -> 0 us
  starting transfers between devices: 43 us -> 65.3 us
  waiting for transfers between devices: 61.3 us -> 68.5 us
  local copies, waits for them, and re-layouts: 12.4 us -> 7.35 us
  other arithmetic: 7.92 us -> 5.15 us
    all_to_all x2 -> x0, blocking collectives: 27.4 us -> none  [the longest x1 14.7 us: summed_at_once(): got = lax.all_to_all(x, 'rows', 0, 0, tiled=True)]
    ppermute x0 -> x12, starting transfers between devices: none -> 16 us  [swap(): lax.ppermute(x, 'rows', [(i, i ^ mask) for i in range(lax.axis_size('rows...]
    ppermute x0 -> x12, waiting for transfers between devices: none -> 12.5 us  [swap(): lax.ppermute(x, 'rows', [(i, i ^ mask) for i in range(lax.axis_size('rows...]
    ppermute x53, starting transfers between devices: 43 us -> 49.2 us  [exchange(): return lax.ppermute(x, axis, [(i, i ^ 1 << bit) for i in range(size)])]
    ppermute x53, waiting for transfers between devices: 61.3 us -> 56.1 us  [exchange(): return lax.ppermute(x, axis, [(i, i ^ 1 << bit) for i in range(size)])]
    unnamed x22 -> x24, local copies, waits for them, and re-layouts: 11.3 us -> 6.24 us
    add x6, other arithmetic: 6.65 us -> 3.8 us  [summed(): keep + exchange(send, 'grp', 0)]
  transfers between devices with their start and end apart: 53 -> 65, of which waited for: 38 -> 49; matrix products, arithmetic and copies ran while one was open for 4% -> 3% of each run, Pallas kernels for 0% -> 0%
where the time goes in v3:
time: 228 us; the launch traced here: 227 us
  Pallas kernels  79.9 us (35%)
  waiting for transfers between devices  68.5 us (30%)
  starting transfers between devices  65.3 us (29%)
  local copies, waits for them, and re-layouts  7.35 us (3%)
  other arithmetic  5.15 us (2%)
    pallas_call x4, Pallas kernels, call(): pl.pallas_call(kernel, grid=(n // tile,), in_specs=[s for s in ins], out_...  79.9 us
    ppermute x53, waiting for transfers between devices, exchange(): return lax.ppermute(x, axis, [(i, i ^ 1 << bit) for i in range(size)])  56.1 us
    ppermute x53, starting transfers between devices, exchange(): return lax.ppermute(x, axis, [(i, i ^ 1 << bit) for i in range(size)])  49.2 us
    ppermute x12, starting transfers between devices, swap(): lax.ppermute(x, 'rows', [(i, i ^ mask) for i in range(lax.axis_size('rows...  16 us
    ppermute x12, waiting for transfers between devices, swap(): lax.ppermute(x, 'rows', [(i, i ^ mask) for i in range(lax.axis_size('rows...  12.5 us
    unnamed x24, local copies, waits for them, and re-layouts  6.24 us
  transfers between devices with their start and end apart: 65, of which 49 were waited for; matrix products, arithmetic and copies ran while one was open for 3% of the time, Pallas kernels for 0%

profile of v3, /device:TPU:0, one launch (start us, length us, event | category | flops | bytes accessed | tf_op | source)
XLA Modules:
  0.0 227.4 jit_solution(3350041925428162856)
XLA Ops:
  0.6 14.5 %cross.1 = (f32[768,256]{1,0:T(8,128)S(1)}, f32[768,256]{1,0:T(8,128)}, f32[768,256]{1,0:T(8,128)}, f32[768,256]{1,0:T(8,128)S(1)}, f32[768,256]{1,0:T(8,128)S(1)}, /*index=5*/f32[768,256]{1,0:T(8,128)S(1)}) custom-call(s32[1]{0:T(128)} %bitcast.r_0_, bf16[4096,1024]{1,0:T(8,128)(2,1)} %r_6_.1, bf16[4096,512]{1,0:T(8,128)(2,1)} %r_8_.1), custom_call_target="tpu_custom_call" | custom-call | flops 9663676416 | bytes 12582912 | tf_op jit(solution)/shard_map/cross/pallas_call | solution.py:429
  20.7 2.9 %collective-permute-start.17 = (f32[384,256]{1,0:T(8,128)}, f32[384,256]{1,0:T(8,128)S(1)}, u32[]{:S(2)}, u32[]{:S(2)}) collective-permute-start(f32[384,256]{1,0:T(8,128)} %constant_dynamic-slice_fusion.14), channel_id=1, source_target_pairs={{0,8},{2,10},{4,12},{6,14},{8,0},{10,2},{12,4},{14,6},{16,24},{18,... | collective-permute-start | bytes 1179656 | tf_op jit(solution)/shard_map/ppermute | solution.py:331
  29.3 3.9 %collective-permute-done.17 = f32[384,256]{1,0:T(8,128)S(1)} collective-permute-done((f32[384,256]{1,0:T(8,128)}, f32[384,256]{1,0:T(8,128)S(1)}, u32[]{:S(2)}, u32[]{:S(2)}) %collective-permute-start.17) | collective-permute-done | bytes 393248 | tf_op jit(solution)/shard_map/ppermute | solution.py:331
  36.8 3.1 %collective-permute-done.1 = f32[384,256]{1,0:T(8,128)S(1)} collective-permute-done((f32[384,256]{1,0:T(8,128)S(1)}, f32[384,256]{1,0:T(8,128)S(1)}, u32[]{:S(2)}, u32[]{:S(2)}) %collective-permute-start.1) | collective-permute-done | bytes 393248 | tf_op jit(solution)/shard_map/ppermute | solution.py:331
  40.6 2.1 collective-permute-done.18
  44.9 1.9 collective-permute-done.2
  47.8 2.7 %collective-permute-start.20 = (f32[96,256]{1,0:T(8,128)S(1)}, f32[96,256]{1,0:T(8,128)S(1)}, u32[]{:S(2)}, u32[]{:S(2)}) collective-permute-start(f32[96,256]{1,0:T(8,128)S(1)} %dynamic-slice_add_fusion.9), channel_id=1, source_target_pairs={{0,16},{2,18},{4,20},{6,22},{8,24},{10,26},{12,28},{14,30},{16,0},... | collective-permute-start | bytes 294920 | tf_op jit(solution)/shard_map/ppermute | solution.py:331
  52.6 2.7 %collective-permute-start.4 = (f32[96,256]{1,0:T(8,128)S(1)}, f32[96,256]{1,0:T(8,128)S(1)}, u32[]{:S(2)}, u32[]{:S(2)}) collective-permute-start(f32[96,256]{1,0:T(8,128)S(1)} %dynamic-slice_add_fusion.11), channel_id=1, source_target_pairs={{0,16},{2,18},{4,20},{6,22},{8,24},{10,26},{12,28},{14,30},{16,0},... | collective-permute-start | bytes 294920 | tf_op jit(solution)/shard_map/ppermute | solution.py:331
  55.2 4.4 %collective-permute-done.20 = f32[96,256]{1,0:T(8,128)S(1)} collective-permute-done((f32[96,256]{1,0:T(8,128)S(1)}, f32[96,256]{1,0:T(8,128)S(1)}, u32[]{:S(2)}, u32[]{:S(2)}) %collective-permute-start.20) | collective-permute-done | bytes 98336 | tf_op jit(solution)/shard_map/ppermute | solution.py:331
  71.2 4.0 %collective-permute-done.14 = f32[192,256]{1,0:T(8,128)S(1)} collective-permute-done((f32[192,256]{1,0:T(8,128)S(1)}, f32[192,256]{1,0:T(8,128)S(1)}, u32[]{:S(2)}, u32[]{:S(2)}) %collective-permute-start.14) | collective-permute-done | bytes 196640 | tf_op jit(solution)/shard_map/ppermute | solution.py:331
  77.9 3.0 %collective-permute-done.23 = f32[384,256]{1,0:T(8,128)S(1)} collective-permute-done((f32[384,256]{1,0:T(8,128)S(1)}, f32[384,256]{1,0:T(8,128)S(1)}, u32[]{:S(2)}, u32[]{:S(2)}) %collective-permute-start.23) | collective-permute-done | bytes 393248 | tf_op jit(solution)/shard_map/ppermute | solution.py:331
  81.2 2.0 collective-permute-done.15
  88.1 21.4 %first.1 = (f32[4096,256]{1,0:T(8,128)}, bf16[4096,512]{1,0:T(8,128)(2,1)}, f32[1024,256]{1,0:T(8,128)S(1)}, f32[1024,256]{1,0:T(8,128)S(1)}, bf16[1024,256]{1,0...) custom-call(s32[1]{0:T(128)} %bitcast.r_0_, f32[768,256]{1,0:T(8,128)S(1)} %pad_maximum_fusion.r_1_, ...), custom_call_target="tpu_custom_call" | custom-call | flops 11811160064 | bytes 20971520 | tf_op jit(solution)/shard_map/first/pallas_call | solution.py:429
  118.9 2.6 %collective-permute-start.32 = (f32[16,256]{1,0:T(8,128)S(1)}, f32[16,256]{1,0:T(8,128)S(1)}, u32[]{:S(2)}, u32[]{:S(2)}) collective-permute-start(f32[16,256]{1,0:T(8,128)S(1)} %get-tuple-element.92), channel_id=1, source_target_pairs={{0,16},{2,18},{4,20},{6,22},{8,24},{10,26},{12,28},{14,30},{16,0},... | collective-permute-start | bytes 49160 | tf_op jit(solution)/shard_map/ppermute | solution.py:335
  123.5 3.5 %collective-permute-done.33 = f32[16,256]{1,0:T(8,128)S(1)} collective-permute-done((f32[16,256]{1,0:T(8,128)S(1)}, f32[16,256]{1,0:T(8,128)S(1)}, u32[]{:S(2)}, u32[]{:S(2)}) %collective-permute-start.33) | collective-permute-done | bytes 16416 | tf_op jit(solution)/shard_map/ppermute | solution.py:335
  128.5 2.9 %collective-permute-start.36 = (f32[16,256]{1,0:T(8,128)S(1)}, f32[16,256]{1,0:T(8,128)S(1)}, u32[]{:S(2)}, u32[]{:S(2)}) collective-permute-start(f32[16,256]{1,0:T(8,128)S(1)} %add_add_fusion.1), channel_id=1, source_target_pairs={{0,8},{2,10},{4,12},{6,14},{8,0},{10,2},{12,4},{14,6},{16,24},{18,... | collective-permute-start | bytes 49160 | tf_op jit(solution)/shard_map/ppermute | solution.py:335
  141.4 2.2 copy-done.2
  145.9 29.9 %second.1 = (bf16[4096,256]{1,0:T(8,128)(2,1)}, bf16[4096,512]{1,0:T(8,128)(2,1)}, f32[256,256]{1,0:T(8,128)S(1)}, f32[256,256]{1,0:T(8,128)S(1)}, f32[256,256]{...) custom-call(s32[1]{0:T(128)} %bitcast.r_0_, ...), custom_call_target="tpu_custom_call" | custom-call | flops 10200547328 | bytes 27262976 | tf_op jit(solution)/shard_map/second/pallas_call | solution.py:429
  177.4 1.9 collective-permute-start.56
  184.8 1.8 collective-permute-start.50
  196.8 2.4 %collective-permute-done.59 = f32[64,256]{1,0:T(8,128)S(1)} collective-permute-done((f32[64,256]{1,0:T(8,128)S(1)}, f32[64,256]{1,0:T(8,128)S(1)}, u32[]{:S(2)}, u32[]{:S(2)}) %collective-permute-start.59) | collective-permute-done | bytes 65568 | tf_op jit(solution)/shard_map/ppermute | solution.py:331
  199.2 2.1 collective-permute-start.60
  208.7 2.0 collective-permute-done.54
  213.4 14.0 %last.1 = (bf16[4096,512]{1,0:T(8,128)(2,1)}, f32[2,256,256]{2,1,0:T(8,128)}, f32[512,512]{1,0:T(8,128)}) custom-call(s32[1]{0:T(128)} %bitcast.r_0_, f32[256,256]{1,0:T(8,128)S(1)} %pad_maximum_fusion.7.r_1_, f32[256,256]{1,0:T(8,128)S(1)} %pad_maximum_fusion.8.r_2_, f32[256,256]{1,0:T(8,128)S(1)} %pad_maximum_fusion.9.r_3_, ...), custom_call_target="tpu_custom_call" | custom-call | flops 2147483648 | bytes 10485760 | tf_op jit(solution)/shard_map/last/pallas_call | solution.py:429
  (219 shorter events, 92.3 us)
Async XLA Ops:
  15.5 8.1 %collective-permute-start.8 = (f32[768,256]{1,0:T(8,128)}, f32[768,256]{1,0:T(8,128)}, u32[]{:S(2)}, u32[]{:S(2)}) collective-permute-start(f32[768,256]{1,0:T(8,128)} %get-tuple-element.29), channel_id=1, source_target_pairs={{0,1},{1,0},{2,3},{3,2},{4,5},{5,4},{6,7},{7,6},{8,9},{9,8},{10,11... | collective-permute-start | bytes 2359304 | tf_op jit(solution)/shard_map/ppermute | solution.py:331
  15.6 10.9 %collective-permute-start = (f32[768,256]{1,0:T(8,128)S(1)}, f32[768,256]{1,0:T(8,128)}, u32[]{:S(2)}, u32[]{:S(2)}) collective-permute-start(f32[768,256]{1,0:T(8,128)S(1)} %get-tuple-element.27), channel_id=1, source_target_pairs={{0,1},{1,0},{2,3},{3,2},{4,5},{5,4},{6,7},{7,6},{8,9},{9,8},{10,11... | collective-permute-start | bytes 2359304 | tf_op jit(solution)/shard_map/ppermute | solution.py:331
  20.7 12.6 %collective-permute-start.17 = (f32[384,256]{1,0:T(8,128)}, f32[384,256]{1,0:T(8,128)S(1)}, u32[]{:S(2)}, u32[]{:S(2)}) collective-permute-start(f32[384,256]{1,0:T(8,128)} %constant_dynamic-slice_fusion.14), channel_id=1, source_target_pairs={{0,8},{2,10},{4,12},{6,14},{8,0},{10,2},{12,4},{14,6},{16,24},{18,... | collective-permute-start | bytes 1179656 | tf_op jit(solution)/shard_map/ppermute | solution.py:331
  24.9 10.9 %collective-permute-start.9 = (f32[384,256]{1,0:T(8,128)S(1)}, f32[384,256]{1,0:T(8,128)S(1)}, u32[]{:S(2)}, u32[]{:S(2)}) collective-permute-start(f32[384,256]{1,0:T(8,128)S(1)} %constant_dynamic-slice_fusion.17), channel_id=1, source_target_pairs={{0,4},{2,6},{4,0},{6,2},{8,12},{10,14},{12,8},{14,10},{16,20},{18,... | collective-permute-start | bytes 1179656 | tf_op jit(solution)/shard_map/ppermute | solution.py:331
  27.8 12.1 %collective-permute-start.1 = (f32[384,256]{1,0:T(8,128)S(1)}, f32[384,256]{1,0:T(8,128)S(1)}, u32[]{:S(2)}, u32[]{:S(2)}) collective-permute-start(f32[384,256]{1,0:T(8,128)S(1)} %constant_dynamic-slice_fusion.20), channel_id=1, source_target_pairs={{0,2},{2,0},{4,6},{6,4},{8,10},{10,8},{12,14},{14,12},{16,18},{18,... | collective-permute-start | bytes 1179656 | tf_op jit(solution)/shard_map/ppermute | solution.py:331
  33.4 9.3 %collective-permute-start.18 = (f32[192,256]{1,0:T(8,128)S(1)}, f32[192,256]{1,0:T(8,128)S(1)}, u32[]{:S(2)}, u32[]{:S(2)}) collective-permute-start(f32[192,256]{1,0:T(8,128)S(1)} %constant_dynamic-slice_fusion.13), channel_id=1, source_target_pairs={{0,2},{2,0},{4,6},{6,4},{8,10},{10,8},{12,14},{14,12},{16,18},{18,... | collective-permute-start | bytes 589832 | tf_op jit(solution)/shard_map/ppermute | solution.py:331
  36.0 7.3 %collective-permute-start.10 = (f32[192,256]{1,0:T(8,128)S(1)}, f32[192,256]{1,0:T(8,128)S(1)}, u32[]{:S(2)}, u32[]{:S(2)}) collective-permute-start(f32[192,256]{1,0:T(8,128)S(1)} %constant_dynamic-slice_fusion.16), channel_id=1, source_target_pairs={{0,8},{2,10},{4,12},{6,14},{8,0},{10,2},{12,4},{14,6},{16,24},{18,... | collective-permute-start | bytes 589832 | tf_op jit(solution)/shard_map/ppermute | solution.py:331
  40.0 6.8 %collective-permute-start.2 = (f32[192,256]{1,0:T(8,128)S(1)}, f32[192,256]{1,0:T(8,128)S(1)}, u32[]{:S(2)}, u32[]{:S(2)}) collective-permute-start(f32[192,256]{1,0:T(8,128)S(1)} %constant_dynamic-slice_fusion.19), channel_id=1, source_target_pairs={{0,4},{2,6},{4,0},{6,2},{8,12},{10,14},{12,8},{14,10},{16,20},{18,... | collective-permute-start | bytes 589832 | tf_op jit(solution)/shard_map/ppermute | solution.py:331
  43.4 7.1 %collective-permute-start.11 = (f32[96,256]{1,0:T(8,128)S(1)}, f32[96,256]{1,0:T(8,128)S(1)}, u32[]{:S(2)}, u32[]{:S(2)}) collective-permute-start(f32[96,256]{1,0:T(8,128)S(1)} %constant_dynamic-slice_fusion.15), channel_id=1, source_target_pairs={{0,2},{2,0},{4,6},{6,4},{8,10},{10,8},{12,14},{14,12},{16,18},{18,... | collective-permute-start | bytes 294920 | tf_op jit(solution)/shard_map/ppermute | solution.py:331
  46.8 5.7 %collective-permute-start.3 = (f32[96,256]{1,0:T(8,128)S(1)}, f32[96,256]{1,0:T(8,128)S(1)}, u32[]{:S(2)}, u32[]{:S(2)}) collective-permute-start(f32[96,256]{1,0:T(8,128)S(1)} %constant_dynamic-slice_fusion.18), channel_id=1, source_target_pairs={{0,8},{2,10},{4,12},{6,14},{8,0},{10,2},{12,4},{14,6},{16,24},{18,... | collective-permute-start | bytes 294920 | tf_op jit(solution)/shard_map/ppermute | solution.py:331
  47.8 11.8 %collective-permute-start.20 = (f32[96,256]{1,0:T(8,128)S(1)}, f32[96,256]{1,0:T(8,128)S(1)}, u32[]{:S(2)}, u32[]{:S(2)}) collective-permute-start(f32[96,256]{1,0:T(8,128)S(1)} %dynamic-slice_add_fusion.9), channel_id=1, source_target_pairs={{0,16},{2,18},{4,20},{6,22},{8,24},{10,26},{12,28},{14,30},{16,0},... | collective-permute-start | bytes 294920 | tf_op jit(solution)/shard_map/ppermute | solution.py:331
  50.5 11.1 %collective-permute-start.12 = (f32[96,256]{1,0:T(8,128)S(1)}, f32[96,256]{1,0:T(8,128)S(1)}, u32[]{:S(2)}, u32[]{:S(2)}) collective-permute-start(f32[96,256]{1,0:T(8,128)S(1)} %dynamic-slice_add_fusion.10), channel_id=1, source_target_pairs={{0,16},{2,18},{4,20},{6,22},{8,24},{10,26},{12,28},{14,30},{16,0},... | collective-permute-start | bytes 294920 | tf_op jit(solution)/shard_map/ppermute | solution.py:331
  52.6 10.6 %collective-permute-start.4 = (f32[96,256]{1,0:T(8,128)S(1)}, f32[96,256]{1,0:T(8,128)S(1)}, u32[]{:S(2)}, u32[]{:S(2)}) collective-permute-start(f32[96,256]{1,0:T(8,128)S(1)} %dynamic-slice_add_fusion.11), channel_id=1, source_target_pairs={{0,16},{2,18},{4,20},{6,22},{8,24},{10,26},{12,28},{14,30},{16,0},... | collective-permute-start | bytes 294920 | tf_op jit(solution)/shard_map/ppermute | solution.py:331
  61.7 5.7 %collective-permute-start.13 = (f32[96,256]{1,0:T(8,128)S(1)}, f32[96,256]{1,0:T(8,128)S(1)}, u32[]{:S(2)}, u32[]{:S(2)}) collective-permute-start(f32[96,256]{1,0:T(8,128)S(1)} %add.246), channel_id=1, source_target_pairs={{0,2},{2,0},{4,6},{6,4},{8,10},{10,8},{12,14},{14,12},{16,18},{18,... | collective-permute-start | bytes 294920 | tf_op jit(solution)/shard_map/ppermute | solution.py:331
  64.4 5.7 %collective-permute-start.22 = (f32[192,256]{1,0:T(8,128)S(1)}, f32[192,256]{1,0:T(8,128)S(1)}, u32[]{:S(2)}, u32[]{:S(2)}) collective-permute-start(f32[192,256]{1,0:T(8,128)S(1)} %pad_maximum_fusion.12), channel_id=1, source_target_pairs={{0,2},{2,0},{4,6},{6,4},{8,10},{10,8},{12,14},{14,12},{16,18},{18,... | collective-permute-start | bytes 589832 | tf_op jit(solution)/shard_map/ppermute | solution.py:331
  67.4 7.8 %collective-permute-start.14 = (f32[192,256]{1,0:T(8,128)S(1)}, f32[192,256]{1,0:T(8,128)S(1)}, u32[]{:S(2)}, u32[]{:S(2)}) collective-permute-start(f32[192,256]{1,0:T(8,128)S(1)} %pad_maximum_fusion.11), channel_id=1, source_target_pairs={{0,8},{2,10},{4,12},{6,14},{8,0},{10,2},{12,4},{14,6},{16,24},{18,... | collective-permute-start | bytes 589832 | tf_op jit(solution)/shard_map/ppermute | solution.py:331
  69.0 7.8 %collective-permute-start.6 = (f32[192,256]{1,0:T(8,128)S(1)}, f32[192,256]{1,0:T(8,128)S(1)}, u32[]{:S(2)}, u32[]{:S(2)}) collective-permute-start(f32[192,256]{1,0:T(8,128)S(1)} %pad_maximum_fusion.10), channel_id=1, source_target_pairs={{0,4},{2,6},{4,0},{6,2},{8,12},{10,14},{12,8},{14,10},{16,20},{18,... | collective-permute-start | bytes 589832 | tf_op jit(solution)/shard_map/ppermute | solution.py:331
  70.2 10.8 %collective-permute-start.23 = (f32[384,256]{1,0:T(8,128)S(1)}, f32[384,256]{1,0:T(8,128)S(1)}, u32[]{:S(2)}, u32[]{:S(2)}) collective-permute-start(f32[384,256]{1,0:T(8,128)S(1)} %pad_maximum_fusion.5), channel_id=1, source_target_pairs={{0,8},{2,10},{4,12},{6,14},{8,0},{10,2},{12,4},{14,6},{16,24},{18,... | collective-permute-start | bytes 1179656 | tf_op jit(solution)/shard_map/ppermute | solution.py:331
  75.3 7.8 %collective-permute-start.15 = (f32[384,256]{1,0:T(8,128)S(1)}, f32[384,256]{1,0:T(8,128)S(1)}, u32[]{:S(2)}, u32[]{:S(2)}) collective-permute-start(f32[384,256]{1,0:T(8,128)S(1)} %pad_maximum_fusion.4), channel_id=1, source_target_pairs={{0,4},{2,6},{4,0},{6,2},{8,12},{10,14},{12,8},{14,10},{16,20},{18,... | collective-permute-start | bytes 1179656 | tf_op jit(solution)/shard_map/ppermute | solution.py:331
  76.9 7.8 %collective-permute-start.7 = (f32[384,256]{1,0:T(8,128)S(1)}, f32[384,256]{1,0:T(8,128)S(1)}, u32[]{:S(2)}, u32[]{:S(2)}) collective-permute-start(f32[384,256]{1,0:T(8,128)S(1)} %pad_maximum_fusion.3), channel_id=1, source_target_pairs={{0,2},{2,0},{4,6},{6,4},{8,10},{10,8},{12,14},{14,12},{16,18},{18,... | collective-permute-start | bytes 1179656 | tf_op jit(solution)/shard_map/ppermute | solution.py:331
  180.8 5.8 %collective-permute-start.42 = (f32[128,256]{1,0:T(8,128)S(1)}, f32[128,256]{1,0:T(8,128)S(1)}, u32[]{:S(2)}, u32[]{:S(2)}) collective-permute-start(f32[128,256]{1,0:T(8,128)S(1)} %constant_dynamic-slice_fusion.5), channel_id=1, source_target_pairs={{0,2},{2,0},{4,6},{6,4},{8,10},{10,8},{12,14},{14,12},{16,18},{18,... | collective-permute-start | bytes 393224 | tf_op jit(solution)/shard_map/ppermute | solution.py:331
  192.0 7.1 %collective-permute-start.59 = (f32[64,256]{1,0:T(8,128)S(1)}, f32[64,256]{1,0:T(8,128)S(1)}, u32[]{:S(2)}, u32[]{:S(2)}) collective-permute-start(f32[64,256]{1,0:T(8,128)S(1)} %add.298), channel_id=1, source_target_pairs={{0,16},{2,18},{4,20},{6,22},{8,24},{10,26},{12,28},{14,30},{16,0},... | collective-permute-start | bytes 196616 | tf_op jit(solution)/shard_map/ppermute | solution.py:331
  193.7 7.6 %collective-permute-start.52 = (f32[64,256]{1,0:T(8,128)S(1)}, f32[64,256]{1,0:T(8,128)S(1)}, u32[]{:S(2)}, u32[]{:S(2)}) collective-permute-start(f32[64,256]{1,0:T(8,128)S(1)} %add.289), channel_id=1, source_target_pairs={{0,16},{2,18},{4,20},{6,22},{8,24},{10,26},{12,28},{14,30},{16,0},... | collective-permute-start | bytes 196616 | tf_op jit(solution)/shard_map/ppermute | solution.py:331
  196.0 5.9 %collective-permute-start.45 = (f32[64,256]{1,0:T(8,128)S(1)}, f32[64,256]{1,0:T(8,128)S(1)}, u32[]{:S(2)}, u32[]{:S(2)}) collective-permute-start(f32[64,256]{1,0:T(8,128)S(1)} %add.280), channel_id=1, source_target_pairs={{0,16},{2,18},{4,20},{6,22},{8,24},{10,26},{12,28},{14,30},{16,0},... | collective-permute-start | bytes 196616 | tf_op jit(solution)/shard_map/ppermute | solution.py:331
  (53 other events, 322.5 us)

commit v4 on v3

--- a/solution.py
+++ b/solution.py
@@ -144,8 +144,7 @@
         at += 2 * h
 
 
-def cross_kernel(parts, scale, core_ref, e_ref, x_ref, *refs):
-    sends, keeps, acc = refs[:parts], refs[parts:2 * parts], refs[-1]
+def cross_kernel(scale, core_ref, e_ref, x_ref, send, keep, acc):
     k = e_ref.shape[1]
     p = x_ref.shape[1] // 2
     step = pl.program_id(0)
@@ -155,10 +154,26 @@
         acc[...] = jnp.zeros_like(acc)
 
     et = e_ref[...].T
+    for c in range(2):
+        acc[c * k:(c + 1) * k] += dot(et, x_ref[:, c * p:(c + 1) * p])
+
+    @pl.when(step == pl.num_programs(0) - 1)
+    def _():
+        deal(core_ref, acc, scale, [send], [keep])
+
+
+def square_kernel(parts, scale, core_ref, e_ref, *refs):
+    sends, keeps, acc = refs[:parts], refs[parts:2 * parts], refs[-1]
+    k = e_ref.shape[1]
+    p = acc.shape[1]
+    step = pl.program_id(0)
+
+    @pl.when(step == 0)
+    def _():
+        acc[...] = jnp.zeros_like(acc)
+
+    et = e_ref[...].T
     at = 0
-    for c in range(2):
-        acc[at:at + k] += dot(et, x_ref[:, c * p:(c + 1) * p])
-        at += k
     for j in range(k // p):
         m = (j + 1) * p
         acc[at:at + m] += dot(et[:m], e_ref[:, j * p:(j + 1) * p])
@@ -169,12 +184,27 @@
         deal(core_ref, acc, scale, sends, keeps)
 
 
+def once_kernel(core_ref, own, other, e_ref, x_ref, o_ref, u_ref, total, b_ref):
+    k = e_ref.shape[1]
+    p = o_ref.shape[1]
+
+    @pl.when(pl.program_id(0) == 0)
+    def _():
+        place(core_ref, [(own, other)], total)
+        for c in range(2):
+            b_ref[:, c * p:(c + 1) * p] = total[c * k:(c + 1) * k].astype(BF16)
+
+    t = dot(e_ref[...], b_ref[...])
+    o_ref[...] = (wide(x_ref[:, :p]) - t[:, :p]).astype(BF16)
+    u_ref[...] = wide(x_ref[:, p:]) - t[:, p:]
+
+
 def first_kernel(parts, scale, core_ref, *refs):
     own, other = refs[:parts], refs[parts:2 * parts]
-    (e_ref, x_ref, u_ref, w_ref, z_ref, h_ref, b2_ref, send, keep,
-     total, b_ref, offh, offl, acc, hl) = refs[2 * parts:]
+    (e_ref, x_ref, o_ref, w_ref, z_ref, h_ref, t_ref, send, keep,
+     total, sb_ref, offh, offl, acc, hl) = refs[2 * parts:]
     k = e_ref.shape[1]
-    p = x_ref.shape[1] // 2
+    p = o_ref.shape[1]
     step = pl.program_id(0)
 
     @pl.when(step == 0)
@@ -197,33 +227,29 @@
                 if i < j:
                     offh[cols, rows] = high.T
                     offl[cols, rows] = low.T
-        for c in range(2):
-            cols = slice(c * p, (c + 1) * p)
-            coef = total[c * k:(c + 1) * k]
-            b = coef.astype(BF16)
-            b_ref[:, cols] = b
-            after = (coef - wide(b)) - dot(offh[...], b) - dot(offl[...], b)
-            if c == 0:
-                sb = after.astype(BF16)
-                b_ref[:, 2 * p:] = sb
-                h_ref[...] = (after - wide(sb)) - dot(offh[...], sb) - dot(offl[...], sb)
-            else:
-                z_ref[...] = after
-                b2_ref[...] = b
+        coef = total[:k]
+        b = coef.astype(BF16)
+        after = (coef - wide(b)) - dot(offh[...], b) - dot(offl[...], b)
+        sb = after.astype(BF16)
+        sb_ref[...] = sb
+        against = (after - wide(sb)) - dot(offh[...], sb) - dot(offl[...], sb)
+        h_ref[...] = against
+        coef = total[k:2 * k]
+        b = coef.astype(BF16)
+        z_ref[...] = (coef - wide(b)) - dot(offh[...], b) - dot(offl[...], b)
+        high, low = split(against.T)
+        t_ref[...] = dot(high, b) + dot(low, b)
         acc[...] = jnp.zeros_like(acc)
         hl[...] = jnp.zeros_like(hl)
 
-    t = dot(e_ref[...], b_ref[...])
-    once = wide((wide(x_ref[:, :p]) - t[:, :p]).astype(BF16))
-    u_ref[...] = wide(x_ref[:, p:]) - t[:, p:2 * p]
-    high, low = split(once - t[:, 2 * p:])
+    high, low = split(wide(o_ref[...]) - dot(e_ref[...], sb_ref[...]))
     w_ref[:, :p] = high
     w_ref[:, p:] = low
     both = jnp.concatenate([high.T, low.T], axis=0)
     square = dot(both, high)
     acc[:p] += square[:p]
     hl[...] += square[p:]
-    other_two = dot(both, x_ref[:, p:])
+    other_two = dot(both, x_ref[...])
     acc[p:] += other_two[:p] + other_two[p:]
 
     @pl.when(step == pl.num_programs(0) - 1)
@@ -232,7 +258,7 @@
         deal(core_ref, acc, scale, [send], [keep])
 
 
-def second_kernel(parts, scale, core_ref, own, other, z_ref, h_ref, b2_ref, e_ref, u_ref, w_ref, l_ref, *refs):
+def second_kernel(parts, scale, core_ref, own, other, z_ref, h_ref, t_ref, e_ref, u_ref, w_ref, l_ref, *refs):
     q_ref, w2_ref, r_ref, x_ref = refs[:4]
     sends, keeps = refs[4:4 + parts], refs[4 + parts:4 + 2 * parts]
     total, m_ref, ih, il, db, ub, lb, acc, hl = refs[4 + 2 * parts:]
@@ -259,7 +285,7 @@
         turned = split(dot(high, d_b) + dot(low, d_b))
         upper = (z_ref[...] - thrice(against, turned)).astype(BF16)
         ub[...] = upper
-        lower = (d - wide(d_b)) - thrice(inv_s, split(dot(at[0], b2_ref[...]) + dot(at[1], b2_ref[...])))
+        lower = (d - wide(d_b)) - thrice(inv_s, split(t_ref[...]))
         lower_b = lower.astype(BF16)
         lb[...] = lower_b
         x_ref[...] = (lower - wide(lower_b)) - thrice(inv_s, split(dot(at[0], upper) + dot(at[1], upper)))
@@ -331,65 +357,41 @@
     return lax.ppermute(x, axis, [(i, i ^ (1 << bit)) for i in range(size)])
 
 
-def swap(x, mask):
-    return lax.ppermute(x, "rows", [(i, i ^ mask) for i in range(lax.axis_size("rows"))])
-
-
-def summed(sends, keeps, tail):
-    bits = list(range(lax.axis_size("rows").bit_length() - 1))
-    turn, last = bits[:-1], bits[-1:]
-    orders = [turn[n % len(turn):] + turn[:n % len(turn)] + last for n in range(len(sends))]
+def summed(sends, keeps, tail, orders):
     me = lax.axis_index("rows")
-    parts = [keep + exchange(send, "grp", 0) for send, keep in zip(sends, keeps)]
-    halving = len(bits) - tail
-    for step in range(halving):
-        for n, order in enumerate(orders):
-            x, bit = parts[n], order[step]
+    parts = list(keeps)
+    for n, order in enumerate(orders):
+        x = keeps[n] + sends[n]
+        halving = len(order) - tail
+        for bit in order[:halving]:
             half = x.shape[0] // 2
             mine = (me >> bit) & 1
             send = lax.dynamic_slice_in_dim(x, (1 - mine) * half, half, 0)
             keep = lax.dynamic_slice_in_dim(x, mine * half, half, 0)
-            parts[n] = keep + exchange(send, "rows", bit)
-    for step in range(halving, len(bits)):
-        for n, order in enumerate(orders):
-            parts[n] = parts[n] + exchange(parts[n], "rows", order[step])
-    for step in reversed(range(halving)):
-        for n, order in enumerate(orders):
-            x, bit = parts[n], order[step]
+            x = keep + exchange(send, "rows", bit)
+        for bit in order[halving:]:
+            x = x + exchange(x, "rows", bit)
+        for bit in reversed(order[:halving]):
             other = exchange(x, "rows", bit)
             mine = ((me >> bit) & 1) == 1
-            parts[n] = jnp.concatenate([jnp.where(mine, other, x), jnp.where(mine, x, other)], axis=0)
+            x = jnp.concatenate([jnp.where(mine, other, x), jnp.where(mine, x, other)], axis=0)
+        parts[n] = x
     return parts, [exchange(x, "grp", 0) for x in parts]
 
 
+def turned(bits, n):
+    most = bits[:-1]
+    n = n % len(most)
+    return most[n:] + most[:n] + bits[-1:]
+
+
 def summed_at_once(send, keep):
-    bits = lax.axis_size("rows").bit_length() - 1
-    me = lax.axis_index("rows")
+    size = lax.axis_size("rows")
     x = keep + exchange(send, "grp", 0)
-    levels = [(at, min(2, bits - at)) for at in range(0, bits, 2)]
-    for at, width in levels:
-        count = 1 << width
-        block = x.shape[0] // count
-        mine = (me >> at) & (count - 1)
-
-        def piece(m):
-            return lax.dynamic_slice_in_dim(x, (mine ^ m) * block, block, 0)
-
-        got = [piece(0)] + [swap(piece(m), m << at) for m in range(1, count)]
-        while len(got) > 1:
-            got = [a + b for a, b in zip(got[::2], got[1::2])]
-        x = got[0]
-    for at, width in reversed(levels):
-        count = 1 << width
-        mine = (me >> at) & (count - 1)
-        got = [x] + [swap(x, m << at) for m in range(1, count)]
-        order = []
-        for place_at in range(count):
-            pick = got[0]
-            for m in range(1, count):
-                pick = jnp.where((mine ^ m) == place_at, got[m], pick)
-            order.append(pick)
-        x = jnp.concatenate(order, axis=0)
+    got = lax.all_to_all(x, "rows", 0, 0, tiled=True)
+    mine = got.reshape(size, x.shape[0] // size, x.shape[1]).sum(0)
+    same = jnp.broadcast_to(mine[None], (size,) + mine.shape).reshape(x.shape)
+    x = lax.all_to_all(same, "rows", 0, 0, tiled=True)
     return x, exchange(x, "grp", 0)
 
 
@@ -400,9 +402,7 @@
     scale = 1.0 / (n * devices)
     core = lax.axis_index("grp").astype(jnp.int32).reshape(1)
     blocks = k // p
-    rows = (2 * blocks + blocks * (blocks + 1) // 2) * p
-    unit = 2 * devices * 8
-    parts = 3 if rows % (3 * unit) == 0 else 1
+    parts = 2
     tile = 1024 if n % 1024 == 0 else n
 
     def smem():
@@ -423,7 +423,10 @@
     def far(*dims, dtype=F32):
         return pltpu.HBM(dims, dtype)
 
-    earlier, snapshots, later = (pltpu.with_memory_space_constraint(a, pltpu.HBM) for a in (earlier, snapshots, later))
+    def fixed(x):
+        return pltpu.with_memory_space_constraint(x, pltpu.HBM)
+
+    earlier, snapshots, later = fixed(earlier), fixed(snapshots), fixed(later)
 
     def call(kernel, name, room, ins, outs, scratch, flops, size, *args):
         return pl.pallas_call(
@@ -440,46 +443,73 @@
             ),
         )(*args)
 
+    bits = list(range(lax.axis_size("rows").bit_length() - 1))
+    send, keep = call(
+        lambda *r: cross_kernel(scale, *r), "cross", 24,
+        [smem(), tiled(k), tiled(2 * p)],
+        [(whole(k, p), near(k, p))] * 2,
+        [pltpu.VMEM((2 * k, p), F32)],
+        4 * n * k * p, 2 * n * (k + 2 * p),
+        core, earlier, snapshots,
+    )
+    got = exchange(send, "grp", 0)
+    got, core_too = lax.optimization_barrier((got, core))
+    (c_own,), (c_other,) = summed([got], [keep], 1, [turned(bits, 0)])
+
+    rows = blocks * (blocks + 1) // 2 * p
     half = rows // parts // 2
-    halves = [(whole(half, p), near(half, p))] * (2 * parts)
     got = call(
-        lambda *r: cross_kernel(parts, scale, *r), "cross", 32,
-        [smem(), tiled(k), tiled(2 * p)],
-        halves,
+        lambda *r: square_kernel(parts, scale, *r), "square", 28,
+        [smem(), tiled(k)],
+        [(whole(half, p), near(half, p))] * (2 * parts),
         [pltpu.VMEM((rows, p), F32)],
-        2 * n * rows * p, 2 * n * (k + 2 * p),
-        core, earlier, snapshots,
-    )
-    own, other = summed(got[:parts], got[parts:], 1)
-
-    u, w, z, h, b2, send, keep = call(
-        lambda *r: first_kernel(parts, scale, *r), "first", 48,
-        [smem()] + [whole(half, p)] * (2 * parts) + [tiled(k), tiled(2 * p)],
+        2 * n * rows * p, 2 * n * k,
+        core_too, earlier,
+    )
+    g_own, g_other = summed(
+        [exchange(x, "grp", 0) for x in got[:parts]], got[parts:], 1,
+        [turned(bits, t + 1) for t in range(parts)],
+    )
+
+    once, u = call(
+        once_kernel, "once", 28,
+        [smem(), whole(k, p), whole(k, p), tiled(k), tiled(2 * p)],
+        [(tiled(p), far(n, p, dtype=BF16)), (tiled(p), far(n, p))],
+        [pltpu.VMEM((2 * k, p), F32), pltpu.VMEM((k, 2 * p), BF16)],
+        4 * n * k * p, 2 * n * (k + 5 * p),
+        core, c_own, c_other, earlier, snapshots,
+    )
+    once, u = fixed(once), fixed(u)
+
+    w, z, h, t, send, keep = call(
+        lambda *r: first_kernel(1 + parts, scale, *r), "first", 36,
+        [smem()] + ([whole(k, p)] + [whole(half, p)] * parts) * 2
+        + [tiled(k), pl.BlockSpec((tile, p), lambda i: (i, 1)), tiled(p)],
         [
-            (tiled(p), far(n, p)),
             (tiled(2 * p), far(n, 2 * p, dtype=BF16)),
             (whole(k, p), near(k, p)),
             (whole(k, p), near(k, p)),
-            (whole(k, p), near(k, p, dtype=BF16)),
+            (whole(p, p), near(p, p)),
             (whole(p, p), near(p, p)),
             (whole(p, p), near(p, p)),
         ],
         [
-            pltpu.VMEM((rows, p), F32),
-            pltpu.VMEM((k, 3 * p), BF16),
+            pltpu.VMEM((2 * k + rows, p), F32),
+            pltpu.VMEM((k, p), BF16),
             pltpu.VMEM((k, k), BF16),
             pltpu.VMEM((k, k), BF16),
             pltpu.VMEM((2 * p, p), F32),
             pltpu.VMEM((p, p), F32),
         ],
-        2 * n * p * (3 * k + 4 * p) + 12 * k * k * p, n * (2 * k + 12 * p),
-        core, *own, *other, earlier, snapshots,
-    )
+        2 * n * p * (k + 4 * p) + 12 * k * k * p, n * (2 * k + 8 * p),
+        core, c_own, *g_own, c_other, *g_other, earlier, snapshots, once,
+    )
+    w = fixed(w)
     own, other = summed_at_once(send, keep)
 
     got = call(
-        lambda *r: second_kernel(3, scale, *r), "second", 44,
-        [smem(), whole(p, p), whole(p, p), whole(k, p), whole(k, p), whole(k, p),
+        lambda *r: second_kernel(3, scale, *r), "second", 32,
+        [smem(), whole(p, p), whole(p, p), whole(k, p), whole(k, p), whole(p, p),
          tiled(k), tiled(p), tiled(2 * p), tiled(2 * p)],
         [
             (tiled(p), far(n, p, dtype=BF16)),
@@ -499,13 +529,17 @@
             pltpu.VMEM((p, p), F32),
         ],
         2 * n * p * (k + 15 * p), n * (2 * k + 18 * p),
-        core, own, other, z, h, b2, earlier, u, w, later,
+        core, own, other, z, h, t, earlier, u, w, later,
     )
     q_one, w2, r_one, expected = got[:4]
-    own, other = summed(got[4:7], got[7:], 2)
+    q_one, w2 = fixed(q_one), fixed(w2)
+    own, other = summed(
+        [exchange(x, "grp", 0) for x in got[4:7]], got[7:], 2,
+        [turned(bits, t) for t in range(3)],
+    )
 
     return tuple(call(
-        lambda *r: last_kernel(3, *r), "last", 30,
+        lambda *r: last_kernel(3, *r), "last", 28,
         [smem()] + [whole(p, p)] * 8 + [tiled(p), tiled(2 * p)],
         [
             (tiled(2 * p), shape(n, 2 * p, dtype=BF16)),

time: 228 us -> 242 us (1.061)
  blocking collectives: 0 us -> 30.1 us
  starting transfers between devices: 65.3 us -> 44 us
  Pallas kernels: 79.9 us -> 89.8 us
  local copies, waits for them, and re-layouts: 7.35 us -> 3.45 us
    all_to_all x0 -> x2, blocking collectives: none -> 30.1 us  [the longest x1 17.2 us: summed_at_once(): got = lax.all_to_all(x, 'rows', 0, 0, tiled=True)]
    ppermute x12 -> x0, starting transfers between devices: 16 us -> none  [swap(): lax.ppermute(x, 'rows', [(i, i ^ mask) for i in range(lax.axis_size('rows...]
    ppermute x12 -> x0, waiting for transfers between devices: 12.5 us -> none  [swap(): lax.ppermute(x, 'rows', [(i, i ^ mask) for i in range(lax.axis_size('rows...]
    ppermute x53, waiting for transfers between devices: 56.1 us -> 66.6 us  [exchange(): return lax.ppermute(x, axis, [(i, i ^ 1 << bit) for i in range(size)])]
    pallas_call x4 -> x6, Pallas kernels: 79.9 us -> 89.8 us  [call(): pl.pallas_call(kernel, grid=(n // tile,), in_specs=[s for s in ins], out_...]
    ppermute x53, starting transfers between devices: 49.2 us -> 44 us  [exchange(): return lax.ppermute(x, axis, [(i, i ^ 1 << bit) for i in range(size)])]
    unnamed x24 -> x6, local copies, waits for them, and re-layouts: 6.24 us -> 3.11 us
    add x32 -> x30, other arithmetic: 4.27 us -> 5.17 us  [the longest x6 2.58 us: summed(): x = keeps[n] + sends[n]]
  transfers between devices with their start and end apart: 65 -> 53, of which waited for: 49 -> 33; matrix products, arithmetic and copies ran while one was open for 3% -> 3% of each run, Pallas kernels for 0% -> 8%
where the time goes in v4:
time: 242 us; the launch traced here: 241 us
  Pallas kernels  89.8 us (37%)
  waiting for transfers between devices  66.6 us (28%)
  starting transfers between devices  44 us (18%)
  blocking collectives  30.1 us (12%)
  other arithmetic  5.99 us (2%)
  local copies, waits for them, and re-layouts  3.45 us (1%)
    pallas_call x6, Pallas kernels, call(): pl.pallas_call(kernel, grid=(n // tile,), in_specs=[s for s in ins], out_...  89.8 us
    ppermute x53, waiting for transfers between devices, exchange(): return lax.ppermute(x, axis, [(i, i ^ 1 << bit) for i in range(size)])  66.6 us
    ppermute x53, starting transfers between devices, exchange(): return lax.ppermute(x, axis, [(i, i ^ 1 << bit) for i in range(size)])  44 us
    all_to_all x1, blocking collectives, summed_at_once(): got = lax.all_to_all(x, 'rows', 0, 0, tiled=True)  17.2 us
    all_to_all x1, blocking collectives, summed_at_once(): x = lax.all_to_all(same, 'rows', 0, 0, tiled=True)  12.8 us
  transfers between devices with their start and end apart: 53, of which 33 were waited for; matrix products, arithmetic and copies ran while one was open for 3% of the time, Pallas kernels for 8%

profile of v4, /device:TPU:0, one launch (start us, length us, event | category | flops | bytes accessed | tf_op | source)
XLA Modules:
  0.0 241.2 jit_solution(7050074195651991582)
XLA Ops:
  0.6 8.0 %cross.1 = (f32[1024,256]{1,0:T(8,128)S(1)}, f32[1024,256]{1,0:T(8,128)S(1)}) custom-call(s32[1]{0:T(128)} %bitcast.r_0_.core_ref, bf16[4096,1024]{1,0:T(8,128)(2,1)} %r_6_.1, bf16[4096,512]{1,0:T(8,128)(2,1)} %r_8_.1), custom_call_target="tpu_custom_call" | custom-call | flops 4294967296 | bytes 12582912 | tf_op jit(solution)/shard_map/cross/pallas_call | solution.py:432
  9.2 2.3 collective-permute-done
  12.6 2.9 %collective-permute-start.1 = (f32[512,256]{1,0:T(8,128)S(1)}, f32[512,256]{1,0:T(8,128)}, u32[]{:S(2)}, u32[]{:S(2)}) collective-permute-start(f32[512,256]{1,0:T(8,128)S(1)} %constant_dynamic-slice_fusion.14), channel_id=1, source_target_pairs={{0,2},{2,0},{4,6},{6,4},{8,10},{10,8},{12,14},{14,12},{16,18},{18,... | collective-permute-start | bytes 1572872 | tf_op jit(solution)/shard_map/ppermute | solution.py:357
  15.5 8.3 %square.1 = (f32[640,256]{1,0:T(8,128)S(1)}, f32[640,256]{1,0:T(8,128)S(1)}, f32[640,256]{1,0:T(8,128)S(1)}, f32[640,256]{1,0:T(8,128)S(1)}) custom-call(s32[1]{0:T(128)} %bitcast.r_0_.core_ref, bf16[4096,1024]{1,0:T(8,128)(2,1)} %r_6_.1), custom_call_target="tpu_custom_call" | custom-call | flops 5368709120 | bytes 8388608 | tf_op jit(solution)/shard_map/square/pallas_call | solution.py:432
  23.8 4.0 %collective-permute-done.1 = f32[512,256]{1,0:T(8,128)} collective-permute-done((f32[512,256]{1,0:T(8,128)S(1)}, f32[512,256]{1,0:T(8,128)}, u32[]{:S(2)}, u32[]{:S(2)}) %collective-permute-start.1) | collective-permute-done | bytes 524320 | tf_op jit(solution)/shard_map/ppermute | solution.py:357
  32.1 5.0 %collective-permute-done.2 = f32[256,256]{1,0:T(8,128)} collective-permute-done((f32[256,256]{1,0:T(8,128)S(1)}, f32[256,256]{1,0:T(8,128)}, u32[]{:S(2)}, u32[]{:S(2)}) %collective-permute-start.2) | collective-permute-done | bytes 262176 | tf_op jit(solution)/shard_map/ppermute | solution.py:357
  43.0 3.0 %collective-permute-done.3 = f32[128,256]{1,0:T(8,128)S(1)} collective-permute-done((f32[128,256]{1,0:T(8,128)S(1)}, f32[128,256]{1,0:T(8,128)S(1)}, u32[]{:S(2)}, u32[]{:S(2)}) %collective-permute-start.3) | collective-permute-done | bytes 131104 | tf_op jit(solution)/shard_map/ppermute | solution.py:357
  47.2 3.7 %collective-permute-done.17 = f32[320,256]{1,0:T(8,128)S(1)} collective-permute-done((f32[320,256]{1,0:T(8,128)S(1)}, f32[320,256]{1,0:T(8,128)S(1)}, u32[]{:S(2)}, u32[]{:S(2)}) %collective-permute-start.17) | collective-permute-done | bytes 327712 | tf_op jit(solution)/shard_map/ppermute | solution.py:357
  54.4 1.9 collective-permute-done.18
  60.9 2.1 collective-permute-start.20
  64.6 2.6 %collective-permute-done.20 = f32[80,256]{1,0:T(8,128)S(1)} collective-permute-done((f32[80,256]{1,0:T(8,128)S(1)}, f32[80,256]{1,0:T(8,128)S(1)}, u32[]{:S(2)}, u32[]{:S(2)}) %collective-permute-start.20) | collective-permute-done | bytes 81952 | tf_op jit(solution)/shard_map/ppermute | solution.py:357
  67.4 2.0 collective-permute-start.6
  71.9 3.0 %collective-permute-done.13 = f32[80,256]{1,0:T(8,128)S(1)} collective-permute-done((f32[80,256]{1,0:T(8,128)S(1)}, f32[80,256]{1,0:T(8,128)S(1)}, u32[]{:S(2)}, u32[]{:S(2)}) %collective-permute-start.13) | collective-permute-done | bytes 81952 | tf_op jit(solution)/shard_map/ppermute | solution.py:357
  80.3 4.6 %collective-permute-done.7 = f32[512,256]{1,0:T(8,128)S(1)} collective-permute-done((f32[512,256]{1,0:T(8,128)S(1)}, f32[512,256]{1,0:T(8,128)S(1)}, u32[]{:S(2)}, u32[]{:S(2)}) %collective-permute-start.7) | collective-permute-done | bytes 524320 | tf_op jit(solution)/shard_map/ppermute | solution.py:357
  87.1 8.2 %collective-permute-done.15 = f32[320,256]{1,0:T(8,128)S(1)} collective-permute-done((f32[320,256]{1,0:T(8,128)S(1)}, f32[320,256]{1,0:T(8,128)S(1)}, u32[]{:S(2)}, u32[]{:S(2)}) %collective-permute-start.15) | collective-permute-done | bytes 327712 | tf_op jit(solution)/shard_map/ppermute | solution.py:357
  95.5 10.0 %once.1 = (bf16[4096,256]{1,0:T(8,128)(2,1)}, f32[4096,256]{1,0:T(8,128)}) custom-call(s32[1]{0:T(128)} %bitcast.r_0_.core_ref, f32[1024,256]{1,0:T(8,128)S(1)} %pad_maximum_fusion.own.r_1_, f32[1024,256]{1,0:T(8,128)S(1)} %collective-permute-done.24.other.r_4_, bf16[4096,1024]{1,0:T(8,128)(2,1)} %r_6_.1, bf16[4096,512]{1,0:T(8,128)(2,1)} %r_8_.1), custom_call_target="tpu_custom_call" | custom-call | flops 4294967296 | bytes 18874368 | tf_op jit(solution)/shard_map/once/pallas_call | solution.py:432
  105.6 16.8 %first.1 = (bf16[4096,512]{1,0:T(8,128)(2,1)}, f32[1024,256]{1,0:T(8,128)S(1)}, f32[1024,256]{1,0:T(8,128)S(1)}, f32[256,256]{1,0:T(8,128)S(1)}, f32[256,256]{1,0:T(8,128)S(1)}, /*index=5*/f32[256,256]{1,0:T(8,128)S(1)}) custom-call(s32[1]{0:T(128)} %bitcast.r_0_.core_ref, f32[1024,256]{1,0:T(8,128)S(1)} %pad_maximum_fusion.own.r_1_, ...), custom_call_target="tpu_custom_call" | custom-call | flops 7516192768 | bytes 16777216 | tf_op jit(solution)/shard_map/first/pallas_call | solution.py:432
  125.0 17.2 %all_to_all.17 = f32[16,16,256]{2,1,0:T(8,128)S(1)} all-to-all(f32[16,16,256]{2,1,0:T(8,128)S(1)} %bitcast.5), channel_id=1, replica_groups=mesh['rows'=16,'grp'=2] {'rows'}, dimensions={0} | all-to-all | bytes 524288 | tf_op jit(solution)/shard_map/all_to_all | solution.py:391
  142.3 12.8 %all_to_all.18 = f32[16,16,256]{2,1,0:T(8,128)S(1)} all-to-all(f32[16,16,256]{2,1,0:T(8,128)S(1)} %broadcast_in_dim.2), channel_id=1, replica_groups=mesh['rows'=16,'grp'=2] {'rows'}, dimensions={0} | all-to-all | bytes 524288 | tf_op jit(solution)/shard_map/all_to_all | solution.py:394
  157.9 30.2 %second.1 = (bf16[4096,256]{1,0:T(8,128)(2,1)}, bf16[4096,512]{1,0:T(8,128)(2,1)}, f32[256,256]{1,0:T(8,128)S(1)}, f32[256,256]{1,0:T(8,128)S(1)}, f32[256,256]{...) custom-call(s32[1]{0:T(128)} %bitcast.r_0_.core_ref, ...), custom_call_target="tpu_custom_call" | custom-call | flops 10200547328 | bytes 27262976 | tf_op jit(solution)/shard_map/second/pallas_call | solution.py:432
  192.5 2.9 %collective-permute-done.44 = f32[128,256]{1,0:T(8,128)S(1)} collective-permute-done((f32[128,256]{1,0:T(8,128)S(1)}, f32[128,256]{1,0:T(8,128)S(1)}, u32[]{:S(2)}, u32[]{:S(2)}) %collective-permute-start.44) | collective-permute-done | bytes 131104 | tf_op jit(solution)/shard_map/ppermute | solution.py:357
  205.1 2.1 collective-permute-start.40
  208.2 3.4 %collective-permute-done.47 = f32[64,256]{1,0:T(8,128)S(1)} collective-permute-done((f32[64,256]{1,0:T(8,128)S(1)}, f32[64,256]{1,0:T(8,128)S(1)}, u32[]{:S(2)}, u32[]{:S(2)}) %collective-permute-start.47) | collective-permute-done | bytes 65568 | tf_op jit(solution)/shard_map/ppermute | solution.py:357
  224.8 16.5 %last.1 = (bf16[4096,512]{1,0:T(8,128)(2,1)}, f32[2,256,256]{2,1,0:T(8,128)}, f32[512,512]{1,0:T(8,128)}) custom-call(s32[1]{0:T(128)} %bitcast.r_0_.core_ref, f32[256,256]{1,0:T(8,128)S(1)} %pad_maximum_fusion.7.r_1_, f32[256,256]{1,0:T(8,128)S(1)} %pad_maximum_fusion.8.r_2_, f32[256,256]{1,0:T(8,128)S(1)} %pad_maximum_fusion.9.r_3_, ...), custom_call_target="tpu_custom_call" | custom-call | flops 2147483648 | bytes 10485760 | tf_op jit(solution)/shard_map/last/pallas_call | solution.py:432
  (174 shorter events, 66.5 us)
Async XLA Ops:
  12.6 15.2 %collective-permute-start.1 = (f32[512,256]{1,0:T(8,128)S(1)}, f32[512,256]{1,0:T(8,128)}, u32[]{:S(2)}, u32[]{:S(2)}) collective-permute-start(f32[512,256]{1,0:T(8,128)S(1)} %constant_dynamic-slice_fusion.14), channel_id=1, source_target_pairs={{0,2},{2,0},{4,6},{6,4},{8,10},{10,8},{12,14},{14,12},{16,18},{18,... | collective-permute-start | bytes 1572872 | tf_op jit(solution)/shard_map/ppermute | solution.py:357
  23.7 7.2 %collective-permute-start.16 = (f32[640,256]{1,0:T(8,128)S(1)}, f32[640,256]{1,0:T(8,128)}, u32[]{:S(2)}, u32[]{:S(2)}) collective-permute-start(f32[640,256]{1,0:T(8,128)S(1)} %get-tuple-element.36), channel_id=1, source_target_pairs={{0,1},{1,0},{2,3},{3,2},{4,5},{5,4},{6,7},{7,6},{8,9},{9,8},{10,11... | collective-permute-start | bytes 1966088 | tf_op jit(solution)/shard_map/ppermute | solution.py:357
  29.1 8.0 %collective-permute-start.2 = (f32[256,256]{1,0:T(8,128)S(1)}, f32[256,256]{1,0:T(8,128)}, u32[]{:S(2)}, u32[]{:S(2)}) collective-permute-start(f32[256,256]{1,0:T(8,128)S(1)} %constant_dynamic-slice_fusion.13), channel_id=1, source_target_pairs={{0,4},{2,6},{4,0},{6,2},{8,12},{10,14},{12,8},{14,10},{16,20},{18,... | collective-permute-start | bytes 786440 | tf_op jit(solution)/shard_map/ppermute | solution.py:357
  30.9 9.4 %collective-permute-start.8 = (f32[640,256]{1,0:T(8,128)S(1)}, f32[640,256]{1,0:T(8,128)}, u32[]{:S(2)}, u32[]{:S(2)}) collective-permute-start(f32[640,256]{1,0:T(8,128)S(1)} %get-tuple-element.34), channel_id=1, source_target_pairs={{0,1},{1,0},{2,3},{3,2},{4,5},{5,4},{6,7},{7,6},{8,9},{9,8},{10,11... | collective-permute-start | bytes 1966088 | tf_op jit(solution)/shard_map/ppermute | solution.py:357
  38.1 7.9 %collective-permute-start.3 = (f32[128,256]{1,0:T(8,128)S(1)}, f32[128,256]{1,0:T(8,128)S(1)}, u32[]{:S(2)}, u32[]{:S(2)}) collective-permute-start(f32[128,256]{1,0:T(8,128)S(1)} %constant_dynamic-slice_fusion.12), channel_id=1, source_target_pairs={{0,8},{2,10},{4,12},{6,14},{8,0},{10,2},{12,4},{14,6},{16,24},{18,... | collective-permute-start | bytes 393224 | tf_op jit(solution)/shard_map/ppermute | solution.py:357
  39.7 11.2 %collective-permute-start.17 = (f32[320,256]{1,0:T(8,128)S(1)}, f32[320,256]{1,0:T(8,128)S(1)}, u32[]{:S(2)}, u32[]{:S(2)}) collective-permute-start(f32[320,256]{1,0:T(8,128)S(1)} %constant_dynamic-slice_fusion.8), channel_id=1, source_target_pairs={{0,8},{2,10},{4,12},{6,14},{8,0},{10,2},{12,4},{14,6},{16,24},{18,... | collective-permute-start | bytes 983048 | tf_op jit(solution)/shard_map/ppermute | solution.py:357
  41.5 10.4 %collective-permute-start.9 = (f32[320,256]{1,0:T(8,128)S(1)}, f32[320,256]{1,0:T(8,128)S(1)}, u32[]{:S(2)}, u32[]{:S(2)}) collective-permute-start(f32[320,256]{1,0:T(8,128)S(1)} %constant_dynamic-slice_fusion.11), channel_id=1, source_target_pairs={{0,4},{2,6},{4,0},{6,2},{8,12},{10,14},{12,8},{14,10},{16,20},{18,... | collective-permute-start | bytes 983048 | tf_op jit(solution)/shard_map/ppermute | solution.py:357
  46.0 7.6 %collective-permute-start.4 = (f32[128,256]{1,0:T(8,128)S(1)}, f32[128,256]{1,0:T(8,128)S(1)}, u32[]{:S(2)}, u32[]{:S(2)}) collective-permute-start(f32[128,256]{1,0:T(8,128)S(1)} %dynamic-slice_add_fusion.9), channel_id=1, source_target_pairs={{0,16},{2,18},{4,20},{6,22},{8,24},{10,26},{12,28},{14,30},{16,0},... | collective-permute-start | bytes 393224 | tf_op jit(solution)/shard_map/ppermute | solution.py:357
  57.5 5.5 %collective-permute-start.11 = (f32[80,256]{1,0:T(8,128)S(1)}, f32[80,256]{1,0:T(8,128)S(1)}, u32[]{:S(2)}, u32[]{:S(2)}) collective-permute-start(f32[80,256]{1,0:T(8,128)S(1)} %constant_dynamic-slice_fusion.9), channel_id=1, source_target_pairs={{0,2},{2,0},{4,6},{6,4},{8,10},{10,8},{12,14},{14,12},{16,18},{18,... | collective-permute-start | bytes 245768 | tf_op jit(solution)/shard_map/ppermute | solution.py:357
  60.9 6.3 %collective-permute-start.20 = (f32[80,256]{1,0:T(8,128)S(1)}, f32[80,256]{1,0:T(8,128)S(1)}, u32[]{:S(2)}, u32[]{:S(2)}) collective-permute-start(f32[80,256]{1,0:T(8,128)S(1)} %dynamic-slice_add_fusion.10), channel_id=1, source_target_pairs={{0,16},{2,18},{4,20},{6,22},{8,24},{10,26},{12,28},{14,30},{16,0},... | collective-permute-start | bytes 245768 | tf_op jit(solution)/shard_map/ppermute | solution.py:357
  63.0 6.4 %collective-permute-start.12 = (f32[80,256]{1,0:T(8,128)S(1)}, f32[80,256]{1,0:T(8,128)S(1)}, u32[]{:S(2)}, u32[]{:S(2)}) collective-permute-start(f32[80,256]{1,0:T(8,128)S(1)} %dynamic-slice_add_fusion.11), channel_id=1, source_target_pairs={{0,16},{2,18},{4,20},{6,22},{8,24},{10,26},{12,28},{14,30},{16,0},... | collective-permute-start | bytes 245768 | tf_op jit(solution)/shard_map/ppermute | solution.py:357
  67.4 8.2 %collective-permute-start.6 = (f32[256,256]{1,0:T(8,128)S(1)}, f32[256,256]{1,0:T(8,128)S(1)}, u32[]{:S(2)}, u32[]{:S(2)}) collective-permute-start(f32[256,256]{1,0:T(8,128)S(1)} %pad_maximum_fusion.6), channel_id=1, source_target_pairs={{0,4},{2,6},{4,0},{6,2},{8,12},{10,14},{12,8},{14,10},{16,20},{18,... | collective-permute-start | bytes 786440 | tf_op jit(solution)/shard_map/ppermute | solution.py:357
  71.8 7.2 %collective-permute-start.22 = (f32[160,256]{1,0:T(8,128)S(1)}, f32[160,256]{1,0:T(8,128)S(1)}, u32[]{:S(2)}, u32[]{:S(2)}) collective-permute-start(f32[160,256]{1,0:T(8,128)S(1)} %pad_maximum_fusion.11), channel_id=1, source_target_pairs={{0,2},{2,0},{4,6},{6,4},{8,10},{10,8},{12,14},{14,12},{16,18},{18,... | collective-permute-start | bytes 491528 | tf_op jit(solution)/shard_map/ppermute | solution.py:357
  75.7 9.2 %collective-permute-start.7 = (f32[512,256]{1,0:T(8,128)S(1)}, f32[512,256]{1,0:T(8,128)S(1)}, u32[]{:S(2)}, u32[]{:S(2)}) collective-permute-start(f32[512,256]{1,0:T(8,128)S(1)} %pad_maximum_fusion.3), channel_id=1, source_target_pairs={{0,2},{2,0},{4,6},{6,4},{8,10},{10,8},{12,14},{14,12},{16,18},{18,... | collective-permute-start | bytes 1572872 | tf_op jit(solution)/shard_map/ppermute | solution.py:357
  79.0 7.7 %collective-permute-start.23 = (f32[320,256]{1,0:T(8,128)S(1)}, f32[320,256]{1,0:T(8,128)S(1)}, u32[]{:S(2)}, u32[]{:S(2)}) collective-permute-start(f32[320,256]{1,0:T(8,128)S(1)} %pad_maximum_fusion.5), channel_id=1, source_target_pairs={{0,8},{2,10},{4,12},{6,14},{8,0},{10,2},{12,4},{14,6},{16,24},{18,... | collective-permute-start | bytes 983048 | tf_op jit(solution)/shard_map/ppermute | solution.py:357
  85.1 10.5 %collective-permute-start.24 = (f32[1024,256]{1,0:T(8,128)S(1)}, f32[1024,256]{1,0:T(8,128)S(1)}, u32[]{:S(2)}, u32[]{:S(2)}) collective-permute-start(f32[1024,256]{1,0:T(8,128)S(1)} %pad_maximum_fusion.own.r_1_), channel_id=1, source_target_pairs={{0,1},{1,0},{2,3},{3,2},{4,5},{5,4},{6,7},{7,6},{8,9},{9,8},{10,11... | collective-permute-start | bytes 3145736 | tf_op jit(solution)/shard_map/ppermute | solution.py:357
  85.2 10.2 %collective-permute-start.15 = (f32[320,256]{1,0:T(8,128)S(1)}, f32[320,256]{1,0:T(8,128)S(1)}, u32[]{:S(2)}, u32[]{:S(2)}) collective-permute-start(f32[320,256]{1,0:T(8,128)S(1)} %pad_maximum_fusion.4), channel_id=1, source_target_pairs={{0,4},{2,6},{4,0},{6,2},{8,12},{10,14},{12,8},{14,10},{16,20},{18,... | collective-permute-start | bytes 983048 | tf_op jit(solution)/shard_map/ppermute | solution.py:357
  86.9 18.7 %collective-permute-start.26 = (f32[640,256]{1,0:T(8,128)S(1)}, f32[640,256]{1,0:T(8,128)S(1)}, u32[]{:S(2)}, u32[]{:S(2)}) collective-permute-start(f32[640,256]{1,0:T(8,128)S(1)} %pad_maximum_fusion.2.r_3_), channel_id=1, source_target_pairs={{0,1},{1,0},{2,3},{3,2},{4,5},{5,4},{6,7},{7,6},{8,9},{9,8},{10,11... | collective-permute-start | bytes 1966088 | tf_op jit(solution)/shard_map/ppermute | solution.py:357
  95.4 10.1 %collective-permute-start.25 = (f32[640,256]{1,0:T(8,128)S(1)}, f32[640,256]{1,0:T(8,128)S(1)}, u32[]{:S(2)}, u32[]{:S(2)}) collective-permute-start(f32[640,256]{1,0:T(8,128)S(1)} %pad_maximum_fusion.1.r_2_), channel_id=1, source_target_pairs={{0,1},{1,0},{2,3},{3,2},{4,5},{5,4},{6,7},{7,6},{8,9},{9,8},{10,11... | collective-permute-start | bytes 1966088 | tf_op jit(solution)/shard_map/ppermute | solution.py:357
  189.8 5.6 %collective-permute-start.44 = (f32[128,256]{1,0:T(8,128)S(1)}, f32[128,256]{1,0:T(8,128)S(1)}, u32[]{:S(2)}, u32[]{:S(2)}) collective-permute-start(f32[128,256]{1,0:T(8,128)S(1)} %constant_dynamic-slice_fusion.1), channel_id=1, source_target_pairs={{0,8},{2,10},{4,12},{6,14},{8,0},{10,2},{12,4},{14,6},{16,24},{18,... | collective-permute-start | bytes 393224 | tf_op jit(solution)/shard_map/ppermute | solution.py:357
  191.9 5.5 %collective-permute-start.30 = (f32[128,256]{1,0:T(8,128)S(1)}, f32[128,256]{1,0:T(8,128)S(1)}, u32[]{:S(2)}, u32[]{:S(2)}) collective-permute-start(f32[128,256]{1,0:T(8,128)S(1)} %constant_dynamic-slice_fusion.5), channel_id=1, source_target_pairs={{0,2},{2,0},{4,6},{6,4},{8,10},{10,8},{12,14},{14,12},{16,18},{18,... | collective-permute-start | bytes 393224 | tf_op jit(solution)/shard_map/ppermute | solution.py:357
  204.1 7.5 %collective-permute-start.47 = (f32[64,256]{1,0:T(8,128)S(1)}, f32[64,256]{1,0:T(8,128)S(1)}, u32[]{:S(2)}, u32[]{:S(2)}) collective-permute-start(f32[64,256]{1,0:T(8,128)S(1)} %add.236), channel_id=1, source_target_pairs={{0,16},{2,18},{4,20},{6,22},{8,24},{10,26},{12,28},{14,30},{16,0},... | collective-permute-start | bytes 196616 | tf_op jit(solution)/shard_map/ppermute | solution.py:357
  205.1 7.3 %collective-permute-start.40 = (f32[64,256]{1,0:T(8,128)S(1)}, f32[64,256]{1,0:T(8,128)S(1)}, u32[]{:S(2)}, u32[]{:S(2)}) collective-permute-start(f32[64,256]{1,0:T(8,128)S(1)} %add.229), channel_id=1, source_target_pairs={{0,16},{2,18},{4,20},{6,22},{8,24},{10,26},{12,28},{14,30},{16,0},... | collective-permute-start | bytes 196616 | tf_op jit(solution)/shard_map/ppermute | solution.py:357
  207.2 6.5 %collective-permute-start.33 = (f32[64,256]{1,0:T(8,128)S(1)}, f32[64,256]{1,0:T(8,128)S(1)}, u32[]{:S(2)}, u32[]{:S(2)}) collective-permute-start(f32[64,256]{1,0:T(8,128)S(1)} %add.220), channel_id=1, source_target_pairs={{0,16},{2,18},{4,20},{6,22},{8,24},{10,26},{12,28},{14,30},{16,0},... | collective-permute-start | bytes 196616 | tf_op jit(solution)/shard_map/ppermute | solution.py:357
  (32 other events, 118.7 us)

commit v5 on v2

v5 whole, which is shorter than its diff:
```python
import jax
import jax.numpy as jnp
from jax import lax
from jax.experimental import pallas as pl
from jax.experimental.pallas import tpu as pltpu
from jax.sharding import PartitionSpec as P

AXES = ("rows", "grp")
HIGHEST = lax.Precision.HIGHEST
BF16 = jnp.bfloat16
F32 = jnp.float32
MIB = 2**20


def dot(a, b):
    return jnp.dot(a, b, preferred_element_type=F32)


def full(a, b):
    return jnp.dot(a, b, precision=HIGHEST, preferred_element_type=F32)


def wide(x):
    return x.astype(F32)


def split(x):
    high = x.astype(BF16)
    return high, (x - wide(high)).astype(BF16)


def thrice(a, b):
    return dot(a[0], b[0]) + dot(a[0], b[1]) + dot(a[1], b[0])


def factor_tile(groups, emit):
    count = len(groups)
    lane = lax.broadcasted_iota(jnp.int32, (8, 128), 1)
    sub = lax.broadcasted_iota(jnp.int32, (8, 128), 0)
    rows = list(groups)
    for k in range(count):
        base = 8 * k
        strip = rows[k]
        inside = (lane >= base) & (lane < base + 8)
        eye = jnp.where(lane == base + sub, 1.0, 0.0).astype(F32)
        mixed = jnp.where(inside, eye, strip)
        cols = [jnp.broadcast_to(strip[:, base + j:base + j + 1], (8, 128)) for j in range(8)]
        entry = {}
        for j in range(8):
            for i in range(j, 8):
                entry[i, j] = jnp.broadcast_to(cols[j][i:i + 1, :], (8, 128))
        scale = []
        low = {}
        for j in range(8):
            r = lax.rsqrt(entry[j, j])
            scale.append(r)
            for i in range(j + 1, 8):
                low[i, j] = entry[i, j] * r
            for c in range(j + 1, 8):
                for i in range(c, 8):
                    entry[i, c] = entry[i, c] - low[i, j] * low[c, j]
        upper, both = [], []
        for j in range(8):
            u = jnp.broadcast_to(strip[j:j + 1, :], (8, 128))
            v = jnp.broadcast_to(mixed[j:j + 1, :], (8, 128))
            for i in range(j):
                u = u - low[j, i] * upper[i]
                v = v - low[j, i] * both[i]
            upper.append(u * scale[j])
            both.append(v * scale[j])
        out_r = upper[0]
        out_m = both[0]
        for j in range(1, 8):
            out_r = jnp.where(sub == j, upper[j], out_r)
            out_m = jnp.where(sub == j, both[j], out_m)
        emit(
            k,
            jnp.where(lane >= base + sub, out_r, 0.0),
            jnp.where(lane <= base + sub, out_m, 0.0),
        )
        for g in range(k + 1, count):
            w = rows[g]
            new = jnp.where(inside, 0.0, w)
            left = []
            for j in range(8):
                c = jnp.broadcast_to(w[:, base + j:base + j + 1], (8, 128))
                for i in range(j):
                    c = c - left[i] * low[j, i]
                c = c * scale[j]
                left.append(c)
                new = new - c * both[j]
            rows[g] = new


def factor(r_ref, m_ref):
    n = r_ref.shape[0]
    h = 128

    def step(t, carry):
        top = pl.multiple_of(t * h, h)
        groups = [r_ref[pl.ds(pl.multiple_of(top + 8 * g, 8), 8), pl.ds(top, h)] for g in range(h // 8)]

        def emit(k, r, m):
            at = pl.ds(pl.multiple_of(top + 8 * k, 8), 8)
            r_ref[at, pl.ds(top, h)] = r
            m_ref[at, pl.ds(top, h)] = m

        factor_tile(groups, emit)

        @pl.when(t == 0)
        def _():
            inv = m_ref[:h, :h]
            u = full(inv, r_ref[:h, h:])
            ut = u.T
            r_ref[:h, h:] = u
            r_ref[h:, h:] = r_ref[h:, h:] - full(ut, u)
            m_ref[h:, :h] = full(ut, inv)
            r_ref[h:, :h] = jnp.zeros((n - h, h), F32)
            m_ref[:h, h:] = jnp.zeros((h, n - h), F32)

        return carry

    lax.fori_loop(0, n // h, step, 0)
    m_ref[h:, :h] = -full(m_ref[h:, h:], m_ref[h:, :h])


def begin(copies, sems):
    for n, (source, target) in enumerate(copies):
        pltpu.make_async_copy(source, target, sems.at[n]).start()


def finish(copies, sems):
    for n, (source, target) in enumerate(copies):
        pltpu.make_async_copy(source, target, sems.at[n]).wait()


def places(core_ref, own, other, total_ref):
    mine = core_ref[0]
    copies = []
    at = 0
    for a, b in zip(own, other):
        h = a.shape[0]
        copies.append((a, total_ref.at[pl.ds(pl.multiple_of(at + mine * h, 8), h)]))
        copies.append((b, total_ref.at[pl.ds(pl.multiple_of(at + (1 - mine) * h, 8), h)]))
        at += 2 * h
    return copies


def tile_rows(i, tile):
    return pl.ds(pl.multiple_of(i * tile, tile), tile)


def at_tile(pairs, i, tile):
    rows = tile_rows(i, tile)
    return [(a.at[rows], b.at[rows]) for a, b in pairs]


def deal(core_ref, total_ref, scale, sends, keeps):
    mine = core_ref[0]
    at = 0
    for send, keep in zip(sends, keeps):
        h = send.shape[0]
        keep[...] = total_ref[pl.ds(pl.multiple_of(at + mine * h, 8), h)] * scale
        send[...] = total_ref[pl.ds(pl.multiple_of(at + (1 - mine) * h, 8), h)] * scale
        at += 2 * h


def cross_kernel(parts, scale, core_ref, e_ref, x_ref, *refs):
    sends, keeps, acc = refs[:parts], refs[parts:2 * parts], refs[-1]
    k = e_ref.shape[1]
    p = x_ref.shape[1] // 2
    step = pl.program_id(0)

    @pl.when(step == 0)
    def _():
        acc[...] = jnp.zeros_like(acc)

    et = e_ref[...].T
    at = 0
    for c in range(2):
        acc[at:at + k] += dot(et, x_ref[:, c * p:(c + 1) * p])
        at += k
    for j in range(k // p):
        m = (j + 1) * p
        acc[at:at + m] += dot(et[:m], e_ref[:, j * p:(j + 1) * p])
        at += m

    @pl.when(step == pl.num_programs(0) - 1)
    def _():
        deal(core_ref, acc, scale, sends, keeps)


def first_kernel(parts, tile, scale, core_ref, *refs):
    own, other = refs[:parts], refs[parts:2 * parts]
    (e_in, x_in, u_out, w_out, z_out, h_out, t_ref, send, keep,
     total, e_ref, x_ref, u_ref, w_ref, z_ref, h_ref, b_ref, offh, offl, acc, hl,
     sum_sems, in_sems, out_sems, small_sems) = refs[2 * parts:]
    n, k = e_ref.shape
    p = u_ref.shape[1]
    tiles = n // tile
    sums = places(core_ref, own, other, total)
    inputs = [(e_in, e_ref), (x_in, x_ref)]
    outputs = [(u_ref, u_out), (w_ref, w_out)]
    small = [(z_ref, z_out), (h_ref, h_out)]
    begin(sums, sum_sems)
    for i in range(tiles):
        begin(at_tile(inputs, i, tile), in_sems.at[i])
    acc[...] = jnp.zeros_like(acc)
    hl[...] = jnp.zeros_like(hl)
    finish(sums, sum_sems)

    at = 2 * k
    for j in range(k // p):
        cols = slice(j * p, (j + 1) * p)
        for i in range(j + 1):
            block = total[at:at + p]
            at += p
            if i == j:
                a = lax.broadcasted_iota(jnp.int32, (p, p), 0)
                b = lax.broadcasted_iota(jnp.int32, (p, p), 1)
                block = block - jnp.where(a == b, 1.0, 0.0)
            high, low = split(block)
            rows = slice(i * p, (i + 1) * p)
            offh[rows, cols] = high
            offl[rows, cols] = low
            if i < j:
                offh[cols, rows] = high.T
                offl[cols, rows] = low.T
    for c in range(2):
        coef = total[c * k:(c + 1) * k]
        b = coef.astype(BF16)
        b_ref[:, c * p:(c + 1) * p] = b
        after = (coef - wide(b)) - dot(offh[...], b) - dot(offl[...], b)
        if c == 0:
            sb = after.astype(BF16)
            b_ref[:, 2 * p:] = sb
            against = (after - wide(sb)) - dot(offh[...], sb) - dot(offl[...], sb)
            h_ref[...] = against
        else:
            z_ref[...] = after
            high, low = split(against.T)
            t_ref[...] = dot(high, b) + dot(low, b)
    begin(small, small_sems)

    def step(i, carry):
        rows = tile_rows(i, tile)
        finish(at_tile(inputs, i, tile), in_sems.at[i])
        t = dot(e_ref[rows, :], b_ref[...])
        once = wide((wide(x_ref[rows, :p]) - t[:, :p]).astype(BF16))
        x_two = x_ref[rows, p:]
        u_ref[rows, :] = wide(x_two) - t[:, p:2 * p]
        high, low = split(once - t[:, 2 * p:])
        w_ref[rows, :p] = high
        w_ref[rows, p:] = low
        begin(at_tile(outputs, i, tile), out_sems.at[i])
        both = jnp.concatenate([high.T, low.T], axis=0)
        square = dot(both, high)
        acc[:p] += square[:p]
        hl[...] += square[p:]
        other_two = dot(both, x_two)
        acc[p:] += other_two[:p] + other_two[p:]
        return carry

    lax.fori_loop(0, tiles, step, 0)
    acc[:p] = acc[:p] + hl[...] + hl[...].T
    deal(core_ref, acc, scale, [send], [keep])
    for i in range(tiles):
        finish(at_tile(outputs, i, tile), out_sems.at[i])
    finish(small, small_sems)


def second_kernel(parts, tile, scale, core_ref, own, other, z_in, h_in, t_ref, e_in, u_in, w_in, l_in, *refs):
    q_out, w2_out, r_ref, x_ref = refs[:4]
    sends, keeps = refs[4:4 + parts], refs[4 + parts:4 + 2 * parts]
    (total, z_ref, h_ref, e_ref, u_ref, w_ref, l_ref, q_ref, w2_ref, m_ref, ih, il, db, ub, lb, acc, hl,
     sum_sems, small_sems, in_sems, out_sems) = refs[4 + 2 * parts:]
    p = r_ref.shape[0]
    n = e_ref.shape[0]
    tiles = n // tile
    sums = places(core_ref, [own], [other], total)
    small = [(z_in, z_ref), (h_in, h_ref)]
    inputs = [(e_in, e_ref), (u_in, u_ref), (w_in, w_ref), (l_in, l_ref)]
    outputs = [(q_ref, q_out), (w2_ref, w2_out)]
    begin(sums, sum_sems)
    begin(small, small_sems)
    for i in range(tiles):
        begin(at_tile(inputs, i, tile), in_sems.at[i])
    acc[...] = jnp.zeros_like(acc)
    hl[...] = jnp.zeros_like(hl)
    finish(sums, sum_sems)

    r_ref[...] = total[:p]
    factor(r_ref, m_ref)
    inv = m_ref[...]
    high, low = split(inv.T)
    ih[:p] = high
    ih[p:] = high
    il[...] = low
    d = full(inv, total[p:])
    d_b = d.astype(BF16)
    db[...] = d_b
    finish(small, small_sems)
    inv_s = split(inv)
    against = split(h_ref[...])
    at = split(h_ref[...].T)
    turned = split(dot(high, d_b) + dot(low, d_b))
    upper = (z_ref[...] - thrice(against, turned)).astype(BF16)
    ub[...] = upper
    lower = (d - wide(d_b)) - thrice(inv_s, split(t_ref[...]))
    lower_b = lower.astype(BF16)
    lb[...] = lower_b
    x_ref[...] = (lower - wide(lower_b)) - thrice(inv_s, split(dot(at[0], upper) + dot(at[1], upper)))

    def step(i, carry):
        rows = tile_rows(i, tile)
        finish(at_tile(inputs, i, tile), in_sems.at[i])
        q = (dot(w_ref[rows, :], ih[...]) + dot(w_ref[rows, :p], il[...])).astype(BF16)
        q_ref[rows, :] = q
        once = wide((u_ref[rows, :] - dot(q, db[...])).astype(BF16))
        high, low = split(once - dot(e_ref[rows, :], ub[...]) - dot(q, lb[...]))
        w2_ref[rows, :p] = high
        w2_ref[rows, p:] = low
        begin(at_tile(outputs, i, tile), out_sems.at[i])
        qt = q.T
        left = jnp.concatenate([high.T, low.T, qt], axis=0)
        square = dot(left, high)
        acc[:p] += square[:p]
        hl[...] += square[p:2 * p]
        acc[p:2 * p] += square[2 * p:] + dot(qt, low)
        for c in range(2):
            mixed = dot(left, l_ref[rows, c * p:(c + 1) * p])
            acc[(2 + c) * p:(3 + c) * p] += mixed[:p] + mixed[p:2 * p]
            acc[(4 + c) * p:(5 + c) * p] += mixed[2 * p:]
        return carry

    lax.fori_loop(0, tiles, step, 0)
    acc[:p] = acc[:p] + hl[...] + hl[...].T
    deal(core_ref, acc, scale, sends, keeps)
    for i in range(tiles):
        finish(at_tile(outputs, i, tile), out_sems.at[i])


def last_kernel(parts, tile, core_ref, *refs):
    own, other = refs[:parts], refs[parts:2 * parts]
    (x_ref, r1_ref, q_in, w_in, basis_out, factors, shift,
     total, q_ref, w_ref, basis, r_ref, m_ref, ih, il, back, sum_sems, in_sems, out_sems) = refs[2 * parts:]
    p = r_ref.shape[0]
    tiles = q_ref.shape[0] // tile
    sums = places(core_ref, own, other, total)
    inputs = [(q_in, q_ref), (w_in, w_ref)]
    outputs = [(basis, basis_out)]
    begin(sums, sum_sems)
    for i in range(tiles):
        begin(at_tile(inputs, i, tile), in_sems.at[i])
    finish(sums, sum_sems)

    res = total[p:2 * p]
    off = res - x_ref[...]
    off_b = off.astype(BF16)
    offt = off.T.astype(BF16)
    cut = dot(offt, res.astype(BF16))
    r_ref[...] = total[:p] - cut - cut.T + dot(offt, off_b)
    factor(r_ref, m_ref)
    inv = m_ref[...]
    high, low = split(inv.T)
    ih[:p] = high
    ih[p:] = high
    il[...] = low
    back[...] = dot(off_b, high).astype(BF16)

    def step(i, carry):
        rows = tile_rows(i, tile)
        finish(at_tile(inputs, i, tile), in_sems.at[i])
        q = dot(w_ref[rows, :], ih[...]) + dot(w_ref[rows, :p], il[...]) - dot(q_ref[rows, :], back[...])
        basis[rows, :p] = q_ref[rows, :]
        basis[rows, p:] = q.astype(BF16)
        begin(at_tile(outputs, i, tile), out_sems.at[i])
        return carry

    lax.fori_loop(0, tiles, step, 0)
    inv_s = split(m_ref[...])
    factors[0] = r1_ref[...]
    factors[1] = r_ref[...]
    for c in range(2):
        cols = slice(c * p, (c + 1) * p)
        early = total[(4 + c) * p:(5 + c) * p]
        shift[:p, cols] = early
        late = total[(2 + c) * p:(3 + c) * p] - dot(offt, early.astype(BF16))
        shift[p:, cols] = thrice(inv_s, split(late))
    for i in range(tiles):
        finish(at_tile(outputs, i, tile), out_sems.at[i])


def exchange(x, axis, bit):
    size = lax.axis_size(axis)
    return lax.ppermute(x, axis, [(i, i ^ (1 << bit)) for i in range(size)])


def summed(sends, keeps, tail):
    bits = list(range(lax.axis_size("rows").bit_length() - 1))
    turn, last = bits[:-1], bits[-1:]
    orders = [turn[n % len(turn):] + turn[:n % len(turn)] + last for n in range(len(sends))]
    me = lax.axis_index("rows")
    parts = [keep + exchange(send, "grp", 0) for send, keep in zip(sends, keeps)]
    halving = len(bits) - tail
    for step in range(halving):
        for n, order in enumerate(orders):
            x, bit = parts[n], order[step]
            half = x.shape[0] // 2
            mine = (me >> bit) & 1
            send = lax.dynamic_slice_in_dim(x, (1 - mine) * half, half, 0)
            keep = lax.dynamic_slice_in_dim(x, mine * half, half, 0)
            parts[n] = keep + exchange(send, "rows", bit)
    for step in range(halving, len(bits)):
        for n, order in enumerate(orders):
            parts[n] = parts[n] + exchange(parts[n], "rows", order[step])
    for step in reversed(range(halving)):
        for n, order in enumerate(orders):
            x, bit = parts[n], order[step]
            other = exchange(x, "rows", bit)
            mine = ((me >> bit) & 1) == 1
            parts[n] = jnp.concatenate([jnp.where(mine, other, x), jnp.where(mine, x, other)], axis=0)
    return parts, [exchange(x, "grp", 0) for x in parts]


def summed_at_once(send, keep):
    size = lax.axis_size("rows")
    x = keep + exchange(send, "grp", 0)
    got = lax.all_to_all(x, "rows", 0, 0, tiled=True)
    mine = got.reshape(size, x.shape[0] // size, x.shape[1]).sum(0)
    same = jnp.broadcast_to(mine[None], (size,) + mine.shape).reshape(x.shape)
    x = lax.all_to_all(same, "rows", 0, 0, tiled=True)
    return x, exchange(x, "grp", 0)


def body(earlier, snapshots, later):
    n, k = earlier.shape
    p = snapshots.shape[1] // 2
    devices = lax.axis_size(AXES)
    scale = 1.0 / (n * devices)
    core = lax.axis_index("grp").astype(jnp.int32).reshape(1)
    blocks = k // p
    rows = (2 * blocks + blocks * (blocks + 1) // 2) * p
    unit = 2 * devices * 8
    parts = 3 if rows % (3 * unit) == 0 else 1
    tile = 1024 if n % 1024 == 0 else n

    def smem():
        return pl.BlockSpec(memory_space=pltpu.SMEM)

    def whole(*shape):
        return pl.BlockSpec(shape, lambda i: (0,) * len(shape))

    def tiled(cols):
        return pl.BlockSpec((tile, cols), lambda i: (i, 0))

    def shape(*dims, dtype=F32):
        return jax.ShapeDtypeStruct(dims, dtype)

    def near(*dims, dtype=F32):
        return pltpu.VMEM(dims, dtype)

    def far(*dims, dtype=F32):
        return pltpu.HBM(dims, dtype)

    apart = pl.BlockSpec(memory_space=pl.ANY)
    inside = pl.BlockSpec(memory_space=pltpu.VMEM)

    def fixed(x):
        return pltpu.with_memory_space_constraint(x, pltpu.HBM)

    earlier, snapshots, later = fixed(earlier), fixed(snapshots), fixed(later)

    def call(kernel, name, room, ins, outs, scratch, flops, size, *args, grid=None):
        return pl.pallas_call(
            kernel,
            grid=(n // tile,) if grid is None else grid,
            in_specs=[s for s in ins],
            out_specs=[s for s, _ in outs],
            out_shape=[s for _, s in outs],
            scratch_shapes=scratch,
            name=name,
            cost_estimate=pl.CostEstimate(flops=flops, bytes_accessed=size, transcendentals=0),
            compiler_params=pltpu.CompilerParams(
                vmem_limit_bytes=room * MIB
            ),
        )(*args)

    half = rows // parts // 2
    halves = [(whole(half, p), near(half, p))] * (2 * parts)
    got = call(
        lambda *r: cross_kernel(parts, scale, *r), "cross", 32,
        [smem(), tiled(k), tiled(2 * p)],
        halves,
        [pltpu.VMEM((rows, p), F32)],
        2 * n * rows * p, 2 * n * (k + 2 * p),
        core, earlier, snapshots,
    )
    own, other = summed(got[:parts], got[parts:], 1)

    tiles = n // tile
    dma = pltpu.SemaphoreType.DMA

    def held(*dims, dtype=F32):
        return pltpu.VMEM(dims, dtype)

    u, w, z, h, t, send, keep = call(
        lambda *r: first_kernel(parts, tile, scale, *r), "first", 50,
        [smem()] + [apart] * (2 * parts + 2),
        [
            (apart, far(n, p)),
            (apart, far(n, 2 * p, dtype=BF16)),
            (apart, far(k, p)),
            (apart, far(k, p)),
            (inside, near(p, p)),
            (inside, near(p, p)),
            (inside, near(p, p)),
        ],
        [
            held(rows, p),
            held(n, k, dtype=BF16),
            held(n, 2 * p, dtype=BF16),
            held(n, p),
            held(n, 2 * p, dtype=BF16),
            held(k, p),
            held(k, p),
            held(k, 3 * p, dtype=BF16),
            held(k, k, dtype=BF16),
            held(k, k, dtype=BF16),
            held(2 * p, p),
            held(p, p),
            dma((2 * parts,)), dma((tiles, 2)), dma((tiles, 2)), dma((2,)),
        ],
        2 * n * p * (3 * k + 4 * p) + 12 * k * k * p, n * (2 * k + 12 * p),
        core, *own, *other, earlier, snapshots, grid=(),
    )
    own, other = summed_at_once(send, keep)

    got = call(
        lambda *r: second_kernel(3, tile, scale, *r), "second", 46,
        [smem()] + [apart] * 4 + [inside] + [apart] * 4,
        [
            (apart, far(n, p, dtype=BF16)),
            (apart, far(n, 2 * p, dtype=BF16)),
            (inside, near(p, p)),
            (inside, near(p, p)),
        ] + [(inside, near(p, p))] * 6,
        [
            held(2 * p, p),
            held(k, p),
            held(k, p),
            held(n, k, dtype=BF16),
            held(n, p),
            held(n, 2 * p, dtype=BF16),
            held(n, 2 * p, dtype=BF16),
            held(n, p, dtype=BF16),
            held(n, 2 * p, dtype=BF16),
            held(p, p),
            held(2 * p, p, dtype=BF16),
            held(p, p, dtype=BF16),
            held(p, p, dtype=BF16),
            held(k, p, dtype=BF16),
            held(p, p, dtype=BF16),
            held(6 * p, p),
            held(p, p),
            dma((2,)), dma((2,)), dma((tiles, 4)), dma((tiles, 2)),
        ],
        2 * n * p * (k + 15 * p), n * (2 * k + 18 * p),
        core, own, other, fixed(z), fixed(h), t, earlier, fixed(u), fixed(w), later, grid=(),
    )
    q_one, w2, r_one, expected = got[:4]
    own, other = summed(got[4:7], got[7:], 2)

    return tuple(call(
        lambda *r: last_kernel(3, tile, *r), "last", 26,
        [smem()] + [apart] * 6 + [inside] * 2 + [apart] * 2,
        [
            (apart, far(n, 2 * p, dtype=BF16)),
            (inside, shape(2, p, p)),
            (inside, shape(2 * p, 2 * p)),
        ],
        [
            held(6 * p, p),
            held(n, p, dtype=BF16),
            held(n, 2 * p, dtype=BF16),
            held(n, 2 * p, dtype=BF16),
            held(p, p),
            held(p, p),
            held(2 * p, p, dtype=BF16),
            held(p, p, dtype=BF16),
            held(p, p, dtype=BF16),
            dma((6,)), dma((tiles, 2)), dma((tiles, 1)),
        ],
        2 * n * p * 4 * p, n * 10 * p,
        core, *own, *other, expected, r_one, fixed(q_one), fixed(w2), grid=(),
    ))


def solution(mesh):
    spec = P(("rows", "grp"), None)
    return jax.shard_map(
        body,
        mesh=mesh,
        in_specs=(spec, spec, spec),
        out_specs=(spec, P(), P()),
        check_vma=False,
    )
```

time: 232 us -> 220 us (0.948)
  local copies, waits for them, and re-layouts: 12.4 us -> 1.98 us
  other arithmetic: 7.92 us -> 5.07 us
    unnamed x22 -> x8, local copies, waits for them, and re-layouts: 11.3 us -> 0.89 us
    add x6, other arithmetic: 6.65 us -> 3.8 us  [summed(): keep + exchange(send, 'grp', 0)]
  transfers between devices with their start and end apart: 53 -> 53, of which waited for: 38 -> 40; matrix products, arithmetic and copies ran while one was open for 4% -> 3% of each run, Pallas kernels for 0% -> 0%
where the time goes in v5:
time: 220 us; the launch traced here: 219 us
  Pallas kernels  79 us (36%)
  waiting for transfers between devices  62.6 us (28%)
  starting transfers between devices  41.7 us (19%)
  blocking collectives  27.4 us (12%)
  other arithmetic  5.07 us (2%)
    pallas_call x4, Pallas kernels, call(): pl.pallas_call(kernel, grid=(n // tile,) if grid is None else grid, in_sp...  79 us
    ppermute x53, waiting for transfers between devices, exchange(): return lax.ppermute(x, axis, [(i, i ^ 1 << bit) for i in range(size)])  62.6 us
    ppermute x53, starting transfers between devices, exchange(): return lax.ppermute(x, axis, [(i, i ^ 1 << bit) for i in range(size)])  41.7 us
    all_to_all x1, blocking collectives, summed_at_once(): got = lax.all_to_all(x, 'rows', 0, 0, tiled=True)  14.7 us
    all_to_all x1, blocking collectives, summed_at_once(): x = lax.all_to_all(same, 'rows', 0, 0, tiled=True)  12.8 us
  transfers between devices with their start and end apart: 53, of which 40 were waited for; matrix products, arithmetic and copies ran while one was open for 3% of the time, Pallas kernels for 0%

profile of v5, /device:TPU:0, one launch (start us, length us, event | category | flops | bytes accessed | tf_op | source)
XLA Modules:
  0.0 219.2 jit_solution(5859205716563370844)
XLA Ops:
  0.6 14.5 %cross.1 = (f32[768,256]{1,0:T(8,128)S(1)}, f32[768,256]{1,0:T(8,128)}, f32[768,256]{1,0:T(8,128)}, f32[768,256]{1,0:T(8,128)S(1)}, f32[768,256]{1,0:T(8,128)S(1)}, /*index=5*/f32[768,256]{1,0:T(8,128)S(1)}) custom-call(s32[1]{0:T(128)} %bitcast.r_0_, bf16[4096,1024]{1,0:T(8,128)(2,1)} %r_6_.1, bf16[4096,512]{1,0:T(8,128)(2,1)} %r_8_.1), custom_call_target="tpu_custom_call" | custom-call | flops 9663676416 | bytes 12582912 | tf_op jit(solution)/shard_map/cross/pallas_call | solution.py:475
  16.1 1.7 collective-permute-done.16
  20.7 2.9 %collective-permute-start.17 = (f32[384,256]{1,0:T(8,128)}, f32[384,256]{1,0:T(8,128)S(1)}, u32[]{:S(2)}, u32[]{:S(2)}) collective-permute-start(f32[384,256]{1,0:T(8,128)} %constant_dynamic-slice_fusion.8), channel_id=1, source_target_pairs={{0,8},{2,10},{4,12},{6,14},{8,0},{10,2},{12,4},{14,6},{16,24},{18,... | collective-permute-start | bytes 1179656 | tf_op jit(solution)/shard_map/ppermute | solution.py:396
  29.3 3.9 %collective-permute-done.17 = f32[384,256]{1,0:T(8,128)S(1)} collective-permute-done((f32[384,256]{1,0:T(8,128)}, f32[384,256]{1,0:T(8,128)S(1)}, u32[]{:S(2)}, u32[]{:S(2)}) %collective-permute-start.17) | collective-permute-done | bytes 393248 | tf_op jit(solution)/shard_map/ppermute | solution.py:396
  33.4 1.7 collective-permute-start.18
  36.8 3.1 %collective-permute-done.1 = f32[384,256]{1,0:T(8,128)S(1)} collective-permute-done((f32[384,256]{1,0:T(8,128)S(1)}, f32[384,256]{1,0:T(8,128)S(1)}, u32[]{:S(2)}, u32[]{:S(2)}) %collective-permute-start.1) | collective-permute-done | bytes 393248 | tf_op jit(solution)/shard_map/ppermute | solution.py:396
  40.6 2.1 collective-permute-done.18
  44.9 1.9 collective-permute-done.2
  47.8 2.7 %collective-permute-start.20 = (f32[96,256]{1,0:T(8,128)S(1)}, f32[96,256]{1,0:T(8,128)S(1)}, u32[]{:S(2)}, u32[]{:S(2)}) collective-permute-start(f32[96,256]{1,0:T(8,128)S(1)} %dynamic-slice_add_fusion.9), channel_id=1, source_target_pairs={{0,16},{2,18},{4,20},{6,22},{8,24},{10,26},{12,28},{14,30},{16,0},... | collective-permute-start | bytes 294920 | tf_op jit(solution)/shard_map/ppermute | solution.py:396
  52.6 2.7 %collective-permute-start.4 = (f32[96,256]{1,0:T(8,128)S(1)}, f32[96,256]{1,0:T(8,128)S(1)}, u32[]{:S(2)}, u32[]{:S(2)}) collective-permute-start(f32[96,256]{1,0:T(8,128)S(1)} %dynamic-slice_add_fusion.11), channel_id=1, source_target_pairs={{0,16},{2,18},{4,20},{6,22},{8,24},{10,26},{12,28},{14,30},{16,0},... | collective-permute-start | bytes 294920 | tf_op jit(solution)/shard_map/ppermute | solution.py:396
  55.2 4.4 %collective-permute-done.20 = f32[96,256]{1,0:T(8,128)S(1)} collective-permute-done((f32[96,256]{1,0:T(8,128)S(1)}, f32[96,256]{1,0:T(8,128)S(1)}, u32[]{:S(2)}, u32[]{:S(2)}) %collective-permute-start.20) | collective-permute-done | bytes 98336 | tf_op jit(solution)/shard_map/ppermute | solution.py:396
  59.9 1.7 collective-permute-done.12
  71.2 4.0 %collective-permute-done.14 = f32[192,256]{1,0:T(8,128)S(1)} collective-permute-done((f32[192,256]{1,0:T(8,128)S(1)}, f32[192,256]{1,0:T(8,128)S(1)}, u32[]{:S(2)}, u32[]{:S(2)}) %collective-permute-start.14) | collective-permute-done | bytes 196640 | tf_op jit(solution)/shard_map/ppermute | solution.py:396
  77.9 3.0 %collective-permute-done.23 = f32[384,256]{1,0:T(8,128)S(1)} collective-permute-done((f32[384,256]{1,0:T(8,128)S(1)}, f32[384,256]{1,0:T(8,128)S(1)}, u32[]{:S(2)}, u32[]{:S(2)}) %collective-permute-start.23) | collective-permute-done | bytes 393248 | tf_op jit(solution)/shard_map/ppermute | solution.py:396
  81.2 2.0 collective-permute-done.15
  87.2 23.0 %first.1 = (f32[4096,256]{1,0:T(8,128)}, bf16[4096,512]{1,0:T(8,128)(2,1)}, f32[1024,256]{1,0:T(8,128)}, f32[1024,256]{1,0:T(8,128)}, f32[256,256]{1,0:T(8,128)S...) custom-call(s32[1]{0:T(128)} %bitcast.r_0_, f32[768,256]{1,0:T(8,128)S(1)} %pad_maximum_fusion.r_1_, ...), custom_call_target="tpu_custom_call" | custom-call | flops 11811160064 | bytes 20971520 | tf_op jit(solution)/shard_map/first/pallas_call | solution.py:475
  111.8 14.7 %all_to_all.17 = f32[16,16,256]{2,1,0:T(8,128)S(1)} all-to-all(f32[16,16,256]{2,1,0:T(8,128)S(1)} %bitcast.5), channel_id=1, replica_groups=mesh['rows'=16,'grp'=2] {'rows'}, dimensions={0} | all-to-all | bytes 524288 | tf_op jit(solution)/shard_map/all_to_all | solution.py:429
  126.5 12.8 %all_to_all.18 = f32[16,16,256]{2,1,0:T(8,128)S(1)} all-to-all(f32[16,16,256]{2,1,0:T(8,128)S(1)} %broadcast_in_dim.2), channel_id=1, replica_groups=mesh['rows'=16,'grp'=2] {'rows'}, dimensions={0} | all-to-all | bytes 524288 | tf_op jit(solution)/shard_map/all_to_all | solution.py:432
  140.8 26.8 %second.1 = (bf16[4096,256]{1,0:T(8,128)(2,1)}, bf16[4096,512]{1,0:T(8,128)(2,1)}, f32[256,256]{1,0:T(8,128)S(1)}, f32[256,256]{1,0:T(8,128)S(1)}, f32[256,256]{...) custom-call(s32[1]{0:T(128)} %bitcast.r_0_, ...), custom_call_target="tpu_custom_call" | custom-call | flops 10200547328 | bytes 27262976 | tf_op jit(solution)/shard_map/second/pallas_call | solution.py:475
  172.0 2.9 %collective-permute-done.44 = f32[128,256]{1,0:T(8,128)S(1)} collective-permute-done((f32[128,256]{1,0:T(8,128)S(1)}, f32[128,256]{1,0:T(8,128)S(1)}, u32[]{:S(2)}, u32[]{:S(2)}) %collective-permute-start.44) | collective-permute-done | bytes 131104 | tf_op jit(solution)/shard_map/ppermute | solution.py:396
  184.7 2.1 collective-permute-start.40
  187.7 3.4 %collective-permute-done.47 = f32[64,256]{1,0:T(8,128)S(1)} collective-permute-done((f32[64,256]{1,0:T(8,128)S(1)}, f32[64,256]{1,0:T(8,128)S(1)}, u32[]{:S(2)}, u32[]{:S(2)}) %collective-permute-start.47) | collective-permute-done | bytes 65568 | tf_op jit(solution)/shard_map/ppermute | solution.py:396
  198.7 1.8 collective-permute-done.49
  204.3 14.7 %last.1 = (bf16[4096,512]{1,0:T(8,128)(2,1)}, f32[2,256,256]{2,1,0:T(8,128)}, f32[512,512]{1,0:T(8,128)}) custom-call(s32[1]{0:T(128)} %bitcast.r_0_, f32[256,256]{1,0:T(8,128)S(1)} %pad_maximum_fusion.6.r_1_, f32[256,256]{1,0:T(8,128)S(1)} %pad_maximum_fusion.7.r_2_, f32[256,256]{1,0:T(8,128)S(1)} %pad_maximum_fusion.8.r_3_, ...), custom_call_target="tpu_custom_call" | custom-call | flops 2147483648 | bytes 10485760 | tf_op jit(solution)/shard_map/last/pallas_call | solution.py:475
  (174 shorter events, 63.4 us)
Async XLA Ops:
  15.5 8.1 %collective-permute-start.8 = (f32[768,256]{1,0:T(8,128)}, f32[768,256]{1,0:T(8,128)}, u32[]{:S(2)}, u32[]{:S(2)}) collective-permute-start(f32[768,256]{1,0:T(8,128)} %get-tuple-element.29), channel_id=1, source_target_pairs={{0,1},{1,0},{2,3},{3,2},{4,5},{5,4},{6,7},{7,6},{8,9},{9,8},{10,11... | collective-permute-start | bytes 2359304 | tf_op jit(solution)/shard_map/ppermute | solution.py:396
  15.6 10.9 %collective-permute-start = (f32[768,256]{1,0:T(8,128)S(1)}, f32[768,256]{1,0:T(8,128)}, u32[]{:S(2)}, u32[]{:S(2)}) collective-permute-start(f32[768,256]{1,0:T(8,128)S(1)} %get-tuple-element.27), channel_id=1, source_target_pairs={{0,1},{1,0},{2,3},{3,2},{4,5},{5,4},{6,7},{7,6},{8,9},{9,8},{10,11... | collective-permute-start | bytes 2359304 | tf_op jit(solution)/shard_map/ppermute | solution.py:396
  20.7 12.6 %collective-permute-start.17 = (f32[384,256]{1,0:T(8,128)}, f32[384,256]{1,0:T(8,128)S(1)}, u32[]{:S(2)}, u32[]{:S(2)}) collective-permute-start(f32[384,256]{1,0:T(8,128)} %constant_dynamic-slice_fusion.8), channel_id=1, source_target_pairs={{0,8},{2,10},{4,12},{6,14},{8,0},{10,2},{12,4},{14,6},{16,24},{18,... | collective-permute-start | bytes 1179656 | tf_op jit(solution)/shard_map/ppermute | solution.py:396
  24.9 10.9 %collective-permute-start.9 = (f32[384,256]{1,0:T(8,128)S(1)}, f32[384,256]{1,0:T(8,128)S(1)}, u32[]{:S(2)}, u32[]{:S(2)}) collective-permute-start(f32[384,256]{1,0:T(8,128)S(1)} %constant_dynamic-slice_fusion.11), channel_id=1, source_target_pairs={{0,4},{2,6},{4,0},{6,2},{8,12},{10,14},{12,8},{14,10},{16,20},{18,... | collective-permute-start | bytes 1179656 | tf_op jit(solution)/shard_map/ppermute | solution.py:396
  27.8 12.1 %collective-permute-start.1 = (f32[384,256]{1,0:T(8,128)S(1)}, f32[384,256]{1,0:T(8,128)S(1)}, u32[]{:S(2)}, u32[]{:S(2)}) collective-permute-start(f32[384,256]{1,0:T(8,128)S(1)} %constant_dynamic-slice_fusion.14), channel_id=1, source_target_pairs={{0,2},{2,0},{4,6},{6,4},{8,10},{10,8},{12,14},{14,12},{16,18},{18,... | collective-permute-start | bytes 1179656 | tf_op jit(solution)/shard_map/ppermute | solution.py:396
  33.4 9.3 %collective-permute-start.18 = (f32[192,256]{1,0:T(8,128)S(1)}, f32[192,256]{1,0:T(8,128)S(1)}, u32[]{:S(2)}, u32[]{:S(2)}) collective-permute-start(f32[192,256]{1,0:T(8,128)S(1)} %constant_dynamic-slice_fusion.7), channel_id=1, source_target_pairs={{0,2},{2,0},{4,6},{6,4},{8,10},{10,8},{12,14},{14,12},{16,18},{18,... | collective-permute-start | bytes 589832 | tf_op jit(solution)/shard_map/ppermute | solution.py:396
  36.0 7.3 %collective-permute-start.10 = (f32[192,256]{1,0:T(8,128)S(1)}, f32[192,256]{1,0:T(8,128)S(1)}, u32[]{:S(2)}, u32[]{:S(2)}) collective-permute-start(f32[192,256]{1,0:T(8,128)S(1)} %constant_dynamic-slice_fusion.10), channel_id=1, source_target_pairs={{0,8},{2,10},{4,12},{6,14},{8,0},{10,2},{12,4},{14,6},{16,24},{18,... | collective-permute-start | bytes 589832 | tf_op jit(solution)/shard_map/ppermute | solution.py:396
  40.0 6.8 %collective-permute-start.2 = (f32[192,256]{1,0:T(8,128)S(1)}, f32[192,256]{1,0:T(8,128)S(1)}, u32[]{:S(2)}, u32[]{:S(2)}) collective-permute-start(f32[192,256]{1,0:T(8,128)S(1)} %constant_dynamic-slice_fusion.13), channel_id=1, source_target_pairs={{0,4},{2,6},{4,0},{6,2},{8,12},{10,14},{12,8},{14,10},{16,20},{18,... | collective-permute-start | bytes 589832 | tf_op jit(solution)/shard_map/ppermute | solution.py:396
  43.4 7.1 %collective-permute-start.11 = (f32[96,256]{1,0:T(8,128)S(1)}, f32[96,256]{1,0:T(8,128)S(1)}, u32[]{:S(2)}, u32[]{:S(2)}) collective-permute-start(f32[96,256]{1,0:T(8,128)S(1)} %constant_dynamic-slice_fusion.9), channel_id=1, source_target_pairs={{0,2},{2,0},{4,6},{6,4},{8,10},{10,8},{12,14},{14,12},{16,18},{18,... | collective-permute-start | bytes 294920 | tf_op jit(solution)/shard_map/ppermute | solution.py:396
  46.8 5.7 %collective-permute-start.3 = (f32[96,256]{1,0:T(8,128)S(1)}, f32[96,256]{1,0:T(8,128)S(1)}, u32[]{:S(2)}, u32[]{:S(2)}) collective-permute-start(f32[96,256]{1,0:T(8,128)S(1)} %constant_dynamic-slice_fusion.12), channel_id=1, source_target_pairs={{0,8},{2,10},{4,12},{6,14},{8,0},{10,2},{12,4},{14,6},{16,24},{18,... | collective-permute-start | bytes 294920 | tf_op jit(solution)/shard_map/ppermute | solution.py:396
  47.8 11.8 %collective-permute-start.20 = (f32[96,256]{1,0:T(8,128)S(1)}, f32[96,256]{1,0:T(8,128)S(1)}, u32[]{:S(2)}, u32[]{:S(2)}) collective-permute-start(f32[96,256]{1,0:T(8,128)S(1)} %dynamic-slice_add_fusion.9), channel_id=1, source_target_pairs={{0,16},{2,18},{4,20},{6,22},{8,24},{10,26},{12,28},{14,30},{16,0},... | collective-permute-start | bytes 294920 | tf_op jit(solution)/shard_map/ppermute | solution.py:396
  50.5 11.1 %collective-permute-start.12 = (f32[96,256]{1,0:T(8,128)S(1)}, f32[96,256]{1,0:T(8,128)S(1)}, u32[]{:S(2)}, u32[]{:S(2)}) collective-permute-start(f32[96,256]{1,0:T(8,128)S(1)} %dynamic-slice_add_fusion.10), channel_id=1, source_target_pairs={{0,16},{2,18},{4,20},{6,22},{8,24},{10,26},{12,28},{14,30},{16,0},... | collective-permute-start | bytes 294920 | tf_op jit(solution)/shard_map/ppermute | solution.py:396
  52.6 10.6 %collective-permute-start.4 = (f32[96,256]{1,0:T(8,128)S(1)}, f32[96,256]{1,0:T(8,128)S(1)}, u32[]{:S(2)}, u32[]{:S(2)}) collective-permute-start(f32[96,256]{1,0:T(8,128)S(1)} %dynamic-slice_add_fusion.11), channel_id=1, source_target_pairs={{0,16},{2,18},{4,20},{6,22},{8,24},{10,26},{12,28},{14,30},{16,0},... | collective-permute-start | bytes 294920 | tf_op jit(solution)/shard_map/ppermute | solution.py:396
  61.7 5.7 %collective-permute-start.13 = (f32[96,256]{1,0:T(8,128)S(1)}, f32[96,256]{1,0:T(8,128)S(1)}, u32[]{:S(2)}, u32[]{:S(2)}) collective-permute-start(f32[96,256]{1,0:T(8,128)S(1)} %add.204), channel_id=1, source_target_pairs={{0,2},{2,0},{4,6},{6,4},{8,10},{10,8},{12,14},{14,12},{16,18},{18,... | collective-permute-start | bytes 294920 | tf_op jit(solution)/shard_map/ppermute | solution.py:396
  63.2 5.7 %collective-permute-start.5 = (f32[96,256]{1,0:T(8,128)S(1)}, f32[96,256]{1,0:T(8,128)S(1)}, u32[]{:S(2)}, u32[]{:S(2)}) collective-permute-start(f32[96,256]{1,0:T(8,128)S(1)} %add.193), channel_id=1, source_target_pairs={{0,8},{2,10},{4,12},{6,14},{8,0},{10,2},{12,4},{14,6},{16,24},{18,... | collective-permute-start | bytes 294920 | tf_op jit(solution)/shard_map/ppermute | solution.py:396
  64.4 5.7 %collective-permute-start.22 = (f32[192,256]{1,0:T(8,128)S(1)}, f32[192,256]{1,0:T(8,128)S(1)}, u32[]{:S(2)}, u32[]{:S(2)}) collective-permute-start(f32[192,256]{1,0:T(8,128)S(1)} %pad_maximum_fusion.11), channel_id=1, source_target_pairs={{0,2},{2,0},{4,6},{6,4},{8,10},{10,8},{12,14},{14,12},{16,18},{18,... | collective-permute-start | bytes 589832 | tf_op jit(solution)/shard_map/ppermute | solution.py:396
  67.4 7.8 %collective-permute-start.14 = (f32[192,256]{1,0:T(8,128)S(1)}, f32[192,256]{1,0:T(8,128)S(1)}, u32[]{:S(2)}, u32[]{:S(2)}) collective-permute-start(f32[192,256]{1,0:T(8,128)S(1)} %pad_maximum_fusion.10), channel_id=1, source_target_pairs={{0,8},{2,10},{4,12},{6,14},{8,0},{10,2},{12,4},{14,6},{16,24},{18,... | collective-permute-start | bytes 589832 | tf_op jit(solution)/shard_map/ppermute | solution.py:396
  69.0 7.8 %collective-permute-start.6 = (f32[192,256]{1,0:T(8,128)S(1)}, f32[192,256]{1,0:T(8,128)S(1)}, u32[]{:S(2)}, u32[]{:S(2)}) collective-permute-start(f32[192,256]{1,0:T(8,128)S(1)} %pad_maximum_fusion.9), channel_id=1, source_target_pairs={{0,4},{2,6},{4,0},{6,2},{8,12},{10,14},{12,8},{14,10},{16,20},{18,... | collective-permute-start | bytes 589832 | tf_op jit(solution)/shard_map/ppermute | solution.py:396
  70.2 10.8 %collective-permute-start.23 = (f32[384,256]{1,0:T(8,128)S(1)}, f32[384,256]{1,0:T(8,128)S(1)}, u32[]{:S(2)}, u32[]{:S(2)}) collective-permute-start(f32[384,256]{1,0:T(8,128)S(1)} %pad_maximum_fusion.5), channel_id=1, source_target_pairs={{0,8},{2,10},{4,12},{6,14},{8,0},{10,2},{12,4},{14,6},{16,24},{18,... | collective-permute-start | bytes 1179656 | tf_op jit(solution)/shard_map/ppermute | solution.py:396
  75.3 7.8 %collective-permute-start.15 = (f32[384,256]{1,0:T(8,128)S(1)}, f32[384,256]{1,0:T(8,128)S(1)}, u32[]{:S(2)}, u32[]{:S(2)}) collective-permute-start(f32[384,256]{1,0:T(8,128)S(1)} %pad_maximum_fusion.4), channel_id=1, source_target_pairs={{0,4},{2,6},{4,0},{6,2},{8,12},{10,14},{12,8},{14,10},{16,20},{18,... | collective-permute-start | bytes 1179656 | tf_op jit(solution)/shard_map/ppermute | solution.py:396
  76.9 7.8 %collective-permute-start.7 = (f32[384,256]{1,0:T(8,128)S(1)}, f32[384,256]{1,0:T(8,128)S(1)}, u32[]{:S(2)}, u32[]{:S(2)}) collective-permute-start(f32[384,256]{1,0:T(8,128)S(1)} %pad_maximum_fusion.3), channel_id=1, source_target_pairs={{0,2},{2,0},{4,6},{6,4},{8,10},{10,8},{12,14},{14,12},{16,18},{18,... | collective-permute-start | bytes 1179656 | tf_op jit(solution)/shard_map/ppermute | solution.py:396
  183.7 7.5 %collective-permute-start.47 = (f32[64,256]{1,0:T(8,128)S(1)}, f32[64,256]{1,0:T(8,128)S(1)}, u32[]{:S(2)}, u32[]{:S(2)}) collective-permute-start(f32[64,256]{1,0:T(8,128)S(1)} %add.242), channel_id=1, source_target_pairs={{0,16},{2,18},{4,20},{6,22},{8,24},{10,26},{12,28},{14,30},{16,0},... | collective-permute-start | bytes 196616 | tf_op jit(solution)/shard_map/ppermute | solution.py:396
  184.7 7.3 %collective-permute-start.40 = (f32[64,256]{1,0:T(8,128)S(1)}, f32[64,256]{1,0:T(8,128)S(1)}, u32[]{:S(2)}, u32[]{:S(2)}) collective-permute-start(f32[64,256]{1,0:T(8,128)S(1)} %add.233), channel_id=1, source_target_pairs={{0,16},{2,18},{4,20},{6,22},{8,24},{10,26},{12,28},{14,30},{16,0},... | collective-permute-start | bytes 196616 | tf_op jit(solution)/shard_map/ppermute | solution.py:396
  186.7 6.5 %collective-permute-start.33 = (f32[64,256]{1,0:T(8,128)S(1)}, f32[64,256]{1,0:T(8,128)S(1)}, u32[]{:S(2)}, u32[]{:S(2)}) collective-permute-start(f32[64,256]{1,0:T(8,128)S(1)} %add.224), channel_id=1, source_target_pairs={{0,16},{2,18},{4,20},{6,22},{8,24},{10,26},{12,28},{14,30},{16,0},... | collective-permute-start | bytes 196616 | tf_op jit(solution)/shard_map/ppermute | solution.py:396
  (33 other events, 126.2 us)

commit v6 on v5

--- a/solution.py
+++ b/solution.py
@@ -203,11 +203,11 @@
     outputs = [(u_ref, u_out), (w_ref, w_out)]
     small = [(z_ref, z_out), (h_ref, h_out)]
     begin(sums, sum_sems)
-    for i in range(tiles):
-        begin(at_tile(inputs, i, tile), in_sems.at[i])
     acc[...] = jnp.zeros_like(acc)
     hl[...] = jnp.zeros_like(hl)
     finish(sums, sum_sems)
+    for i in range(tiles):
+        begin(at_tile(inputs, i, tile), in_sems.at[i])
 
     at = 2 * k
     for j in range(k // p):
@@ -242,26 +242,38 @@
             t_ref[...] = dot(high, b) + dot(low, b)
     begin(small, small_sems)
 
-    def step(i, carry):
+    for i in range(tiles):
+        finish(at_tile(inputs, i, tile), in_sems.at[i])
+
+    def project(i):
         rows = tile_rows(i, tile)
-        finish(at_tile(inputs, i, tile), in_sems.at[i])
         t = dot(e_ref[rows, :], b_ref[...])
         once = wide((wide(x_ref[rows, :p]) - t[:, :p]).astype(BF16))
-        x_two = x_ref[rows, p:]
-        u_ref[rows, :] = wide(x_two) - t[:, p:2 * p]
+        u_ref[rows, :] = wide(x_ref[rows, p:]) - t[:, p:2 * p]
         high, low = split(once - t[:, 2 * p:])
         w_ref[rows, :p] = high
         w_ref[rows, p:] = low
-        begin(at_tile(outputs, i, tile), out_sems.at[i])
-        both = jnp.concatenate([high.T, low.T], axis=0)
+
+    def gather(i):
+        rows = tile_rows(i, tile)
+        high = w_ref[rows, :p]
+        both = jnp.concatenate([high.T, w_ref[rows, p:].T], axis=0)
         square = dot(both, high)
         acc[:p] += square[:p]
         hl[...] += square[p:]
-        other_two = dot(both, x_two)
+        other_two = dot(both, x_ref[rows, p:])
         acc[p:] += other_two[:p] + other_two[p:]
+
+    def step(i, carry):
+        gather(i)
+        project(i + 1)
+        begin(at_tile(outputs, i + 1, tile), out_sems.at[i + 1])
         return carry
 
-    lax.fori_loop(0, tiles, step, 0)
+    project(0)
+    begin(at_tile(outputs, 0, tile), out_sems.at[0])
+    lax.fori_loop(0, tiles - 1, step, 0)
+    gather(tiles - 1)
     acc[:p] = acc[:p] + hl[...] + hl[...].T
     deal(core_ref, acc, scale, [send], [keep])
     for i in range(tiles):
@@ -282,12 +294,12 @@
     inputs = [(e_in, e_ref), (u_in, u_ref), (w_in, w_ref), (l_in, l_ref)]
     outputs = [(q_ref, q_out), (w2_ref, w2_out)]
     begin(sums, sum_sems)
-    begin(small, small_sems)
-    for i in range(tiles):
-        begin(at_tile(inputs, i, tile), in_sems.at[i])
     acc[...] = jnp.zeros_like(acc)
     hl[...] = jnp.zeros_like(hl)
     finish(sums, sum_sems)
+    begin(small, small_sems)
+    for i in range(tiles):
+        begin(at_tile(inputs, i, tile), in_sems.at[i])
 
     r_ref[...] = total[:p]
     factor(r_ref, m_ref)
@@ -311,17 +323,22 @@
     lb[...] = lower_b
     x_ref[...] = (lower - wide(lower_b)) - thrice(inv_s, split(dot(at[0], upper) + dot(at[1], upper)))
 
-    def step(i, carry):
+    for i in range(tiles):
+        finish(at_tile(inputs, i, tile), in_sems.at[i])
+
+    def project(i):
         rows = tile_rows(i, tile)
-        finish(at_tile(inputs, i, tile), in_sems.at[i])
         q = (dot(w_ref[rows, :], ih[...]) + dot(w_ref[rows, :p], il[...])).astype(BF16)
         q_ref[rows, :] = q
         once = wide((u_ref[rows, :] - dot(q, db[...])).astype(BF16))
         high, low = split(once - dot(e_ref[rows, :], ub[...]) - dot(q, lb[...]))
         w2_ref[rows, :p] = high
         w2_ref[rows, p:] = low
-        begin(at_tile(outputs, i, tile), out_sems.at[i])
-        qt = q.T
+
+    def gather(i):
+        rows = tile_rows(i, tile)
+        high, low = w2_ref[rows, :p], w2_ref[rows, p:]
+        qt = q_ref[rows, :].T
         left = jnp.concatenate([high.T, low.T, qt], axis=0)
         square = dot(left, high)
         acc[:p] += square[:p]
@@ -331,9 +348,17 @@
             mixed = dot(left, l_ref[rows, c * p:(c + 1) * p])
             acc[(2 + c) * p:(3 + c) * p] += mixed[:p] + mixed[p:2 * p]
             acc[(4 + c) * p:(5 + c) * p] += mixed[2 * p:]
+
+    def step(i, carry):
+        gather(i)
+        project(i + 1)
+        begin(at_tile(outputs, i + 1, tile), out_sems.at[i + 1])
         return carry
 
-    lax.fori_loop(0, tiles, step, 0)
+    project(0)
+    begin(at_tile(outputs, 0, tile), out_sems.at[0])
+    lax.fori_loop(0, tiles - 1, step, 0)
+    gather(tiles - 1)
     acc[:p] = acc[:p] + hl[...] + hl[...].T
     deal(core_ref, acc, scale, sends, keeps)
     for i in range(tiles):
@@ -350,9 +375,9 @@
     inputs = [(q_in, q_ref), (w_in, w_ref)]
     outputs = [(basis, basis_out)]
     begin(sums, sum_sems)
+    finish(sums, sum_sems)
     for i in range(tiles):
         begin(at_tile(inputs, i, tile), in_sems.at[i])
-    finish(sums, sum_sems)
 
     res = total[p:2 * p]
     off = res - x_ref[...]
@@ -486,6 +511,13 @@
             ),
         )(*args)
 
+    short = 512 if n % 512 == 0 else n
+    tiles = n // short
+    dma = pltpu.SemaphoreType.DMA
+
+    def held(*dims, dtype=F32):
+        return pltpu.VMEM(dims, dtype)
+
     half = rows // parts // 2
     halves = [(whole(half, p), near(half, p))] * (2 * parts)
     got = call(
@@ -498,14 +530,15 @@
     )
     own, other = summed(got[:parts], got[parts:], 1)
 
-    tiles = n // tile
+    short = 512 if n % 512 == 0 else n
+    tiles = n // short
     dma = pltpu.SemaphoreType.DMA
 
     def held(*dims, dtype=F32):
         return pltpu.VMEM(dims, dtype)
 
     u, w, z, h, t, send, keep = call(
-        lambda *r: first_kernel(parts, tile, scale, *r), "first", 50,
+        lambda *r: first_kernel(parts, short, scale, *r), "first", 50,
         [smem()] + [apart] * (2 * parts + 2),
         [
             (apart, far(n, p)),
@@ -537,7 +570,7 @@
     own, other = summed_at_once(send, keep)
 
     got = call(
-        lambda *r: second_kernel(3, tile, scale, *r), "second", 46,
+        lambda *r: second_kernel(3, short, scale, *r), "second", 46,
         [smem()] + [apart] * 4 + [inside] + [apart] * 4,
         [
             (apart, far(n, p, dtype=BF16)),
@@ -572,7 +605,7 @@
     own, other = summed(got[4:7], got[7:], 2)
 
     return tuple(call(
-        lambda *r: last_kernel(3, tile, *r), "last", 26,
+        lambda *r: last_kernel(3, short, *r), "last", 26,
         [smem()] + [apart] * 6 + [inside] * 2 + [apart] * 2,
         [
             (apart, far(n, 2 * p, dtype=BF16)),

time: 220 us -> 213 us (0.968)
  Pallas kernels: 79 us -> 72.3 us
    pallas_call x4, Pallas kernels: 79 us -> 72.3 us  [call(): pl.pallas_call(kernel, grid=(n // tile,) if grid is None else grid, in_sp...]
where the time goes in v6:
time: 213 us
  Pallas kernels  72.3 us (34%)
  waiting for transfers between devices  62.6 us (29%)
  starting transfers between devices  41.7 us (20%)
  blocking collectives  27.5 us (13%)
  other arithmetic  5.07 us (2%)
    pallas_call x4, Pallas kernels, call(): pl.pallas_call(kernel, grid=(n // tile,) if grid is None else grid, in_sp...  72.3 us
    ppermute x53, waiting for transfers between devices, exchange(): return lax.ppermute(x, axis, [(i, i ^ 1 << bit) for i in range(size)])  62.6 us
    ppermute x53, starting transfers between devices, exchange(): return lax.ppermute(x, axis, [(i, i ^ 1 << bit) for i in range(size)])  41.7 us
    all_to_all x1, blocking collectives, summed_at_once(): got = lax.all_to_all(x, 'rows', 0, 0, tiled=True)  14.7 us
    all_to_all x1, blocking collectives, summed_at_once(): x = lax.all_to_all(same, 'rows', 0, 0, tiled=True)  12.8 us
  transfers between devices with their start and end apart: 53, of which 40 were waited for; matrix products, arithmetic and copies ran while one was open for 3% of the time, Pallas kernels for 0%

profile of v6, /device:TPU:0, one launch (start us, length us, event | category | flops | bytes accessed | tf_op | source)
XLA Modules:
  0.0 212.5 jit_solution(12264872951772958744)
XLA Ops:
  0.6 14.5 %cross.1 = (f32[768,256]{1,0:T(8,128)S(1)}, f32[768,256]{1,0:T(8,128)}, f32[768,256]{1,0:T(8,128)}, f32[768,256]{1,0:T(8,128)S(1)}, f32[768,256]{1,0:T(8,128)S(1)}, /*index=5*/f32[768,256]{1,0:T(8,128)S(1)}) custom-call(s32[1]{0:T(128)} %bitcast.r_0_, bf16[4096,1024]{1,0:T(8,128)(2,1)} %r_6_.1, bf16[4096,512]{1,0:T(8,128)(2,1)} %r_8_.1), custom_call_target="tpu_custom_call" | custom-call | flops 9663676416 | bytes 12582912 | tf_op jit(solution)/shard_map/cross/pallas_call | solution.py:500
  16.1 1.7 collective-permute-done.16
  20.7 2.9 %collective-permute-start.17 = (f32[384,256]{1,0:T(8,128)}, f32[384,256]{1,0:T(8,128)S(1)}, u32[]{:S(2)}, u32[]{:S(2)}) collective-permute-start(f32[384,256]{1,0:T(8,128)} %constant_dynamic-slice_fusion.8), channel_id=1, source_target_pairs={{0,8},{2,10},{4,12},{6,14},{8,0},{10,2},{12,4},{14,6},{16,24},{18,... | collective-permute-start | bytes 1179656 | tf_op jit(solution)/shard_map/ppermute | solution.py:421
  29.3 3.9 %collective-permute-done.17 = f32[384,256]{1,0:T(8,128)S(1)} collective-permute-done((f32[384,256]{1,0:T(8,128)}, f32[384,256]{1,0:T(8,128)S(1)}, u32[]{:S(2)}, u32[]{:S(2)}) %collective-permute-start.17) | collective-permute-done | bytes 393248 | tf_op jit(solution)/shard_map/ppermute | solution.py:421
  33.4 1.7 collective-permute-start.18
  36.8 3.1 %collective-permute-done.1 = f32[384,256]{1,0:T(8,128)S(1)} collective-permute-done((f32[384,256]{1,0:T(8,128)S(1)}, f32[384,256]{1,0:T(8,128)S(1)}, u32[]{:S(2)}, u32[]{:S(2)}) %collective-permute-start.1) | collective-permute-done | bytes 393248 | tf_op jit(solution)/shard_map/ppermute | solution.py:421
  40.6 2.1 collective-permute-done.18
  44.9 1.9 collective-permute-done.2
  47.8 2.7 %collective-permute-start.20 = (f32[96,256]{1,0:T(8,128)S(1)}, f32[96,256]{1,0:T(8,128)S(1)}, u32[]{:S(2)}, u32[]{:S(2)}) collective-permute-start(f32[96,256]{1,0:T(8,128)S(1)} %dynamic-slice_add_fusion.9), channel_id=1, source_target_pairs={{0,16},{2,18},{4,20},{6,22},{8,24},{10,26},{12,28},{14,30},{16,0},... | collective-permute-start | bytes 294920 | tf_op jit(solution)/shard_map/ppermute | solution.py:421
  52.6 2.7 %collective-permute-start.4 = (f32[96,256]{1,0:T(8,128)S(1)}, f32[96,256]{1,0:T(8,128)S(1)}, u32[]{:S(2)}, u32[]{:S(2)}) collective-permute-start(f32[96,256]{1,0:T(8,128)S(1)} %dynamic-slice_add_fusion.11), channel_id=1, source_target_pairs={{0,16},{2,18},{4,20},{6,22},{8,24},{10,26},{12,28},{14,30},{16,0},... | collective-permute-start | bytes 294920 | tf_op jit(solution)/shard_map/ppermute | solution.py:421
  55.2 4.4 %collective-permute-done.20 = f32[96,256]{1,0:T(8,128)S(1)} collective-permute-done((f32[96,256]{1,0:T(8,128)S(1)}, f32[96,256]{1,0:T(8,128)S(1)}, u32[]{:S(2)}, u32[]{:S(2)}) %collective-permute-start.20) | collective-permute-done | bytes 98336 | tf_op jit(solution)/shard_map/ppermute | solution.py:421
  59.9 1.7 collective-permute-done.12
  71.2 4.0 %collective-permute-done.14 = f32[192,256]{1,0:T(8,128)S(1)} collective-permute-done((f32[192,256]{1,0:T(8,128)S(1)}, f32[192,256]{1,0:T(8,128)S(1)}, u32[]{:S(2)}, u32[]{:S(2)}) %collective-permute-start.14) | collective-permute-done | bytes 196640 | tf_op jit(solution)/shard_map/ppermute | solution.py:421
  77.9 3.0 %collective-permute-done.23 = f32[384,256]{1,0:T(8,128)S(1)} collective-permute-done((f32[384,256]{1,0:T(8,128)S(1)}, f32[384,256]{1,0:T(8,128)S(1)}, u32[]{:S(2)}, u32[]{:S(2)}) %collective-permute-start.23) | collective-permute-done | bytes 393248 | tf_op jit(solution)/shard_map/ppermute | solution.py:421
  81.2 2.0 collective-permute-done.15
  87.2 18.1 %first.1 = (f32[4096,256]{1,0:T(8,128)}, bf16[4096,512]{1,0:T(8,128)(2,1)}, f32[1024,256]{1,0:T(8,128)}, f32[1024,256]{1,0:T(8,128)}, f32[256,256]{1,0:T(8,128)S...) custom-call(s32[1]{0:T(128)} %bitcast.r_0_, f32[768,256]{1,0:T(8,128)S(1)} %pad_maximum_fusion.r_1_, ...), custom_call_target="tpu_custom_call" | custom-call | flops 11811160064 | bytes 20971520 | tf_op jit(solution)/shard_map/first/pallas_call | solution.py:500
  106.9 14.7 %all_to_all.17 = f32[16,16,256]{2,1,0:T(8,128)S(1)} all-to-all(f32[16,16,256]{2,1,0:T(8,128)S(1)} %bitcast.5), channel_id=1, replica_groups=mesh['rows'=16,'grp'=2] {'rows'}, dimensions={0} | all-to-all | bytes 524288 | tf_op jit(solution)/shard_map/all_to_all | solution.py:454
  121.6 12.8 %all_to_all.18 = f32[16,16,256]{2,1,0:T(8,128)S(1)} all-to-all(f32[16,16,256]{2,1,0:T(8,128)S(1)} %broadcast_in_dim.2), channel_id=1, replica_groups=mesh['rows'=16,'grp'=2] {'rows'}, dimensions={0} | all-to-all | bytes 524288 | tf_op jit(solution)/shard_map/all_to_all | solution.py:457
  135.9 24.4 %second.1 = (bf16[4096,256]{1,0:T(8,128)(2,1)}, bf16[4096,512]{1,0:T(8,128)(2,1)}, f32[256,256]{1,0:T(8,128)S(1)}, f32[256,256]{1,0:T(8,128)S(1)}, f32[256,256]{...) custom-call(s32[1]{0:T(128)} %bitcast.r_0_, ...), custom_call_target="tpu_custom_call" | custom-call | flops 10200547328 | bytes 27262976 | tf_op jit(solution)/shard_map/second/pallas_call | solution.py:500
  164.8 2.9 %collective-permute-done.44 = f32[128,256]{1,0:T(8,128)S(1)} collective-permute-done((f32[128,256]{1,0:T(8,128)S(1)}, f32[128,256]{1,0:T(8,128)S(1)}, u32[]{:S(2)}, u32[]{:S(2)}) %collective-permute-start.44) | collective-permute-done | bytes 131104 | tf_op jit(solution)/shard_map/ppermute | solution.py:421
  177.4 2.1 collective-permute-start.40
  180.4 3.4 %collective-permute-done.47 = f32[64,256]{1,0:T(8,128)S(1)} collective-permute-done((f32[64,256]{1,0:T(8,128)S(1)}, f32[64,256]{1,0:T(8,128)S(1)}, u32[]{:S(2)}, u32[]{:S(2)}) %collective-permute-start.47) | collective-permute-done | bytes 65568 | tf_op jit(solution)/shard_map/ppermute | solution.py:421
  191.5 1.8 collective-permute-done.49
  197.0 15.3 %last.1 = (bf16[4096,512]{1,0:T(8,128)(2,1)}, f32[2,256,256]{2,1,0:T(8,128)}, f32[512,512]{1,0:T(8,128)}) custom-call(s32[1]{0:T(128)} %bitcast.r_0_, f32[256,256]{1,0:T(8,128)S(1)} %pad_maximum_fusion.6.r_1_, f32[256,256]{1,0:T(8,128)S(1)} %pad_maximum_fusion.7.r_2_, f32[256,256]{1,0:T(8,128)S(1)} %pad_maximum_fusion.8.r_3_, ...), custom_call_target="tpu_custom_call" | custom-call | flops 2147483648 | bytes 10485760 | tf_op jit(solution)/shard_map/last/pallas_call | solution.py:500
  (174 shorter events, 63.4 us)
Async XLA Ops:
  15.5 8.1 %collective-permute-start.8 = (f32[768,256]{1,0:T(8,128)}, f32[768,256]{1,0:T(8,128)}, u32[]{:S(2)}, u32[]{:S(2)}) collective-permute-start(f32[768,256]{1,0:T(8,128)} %get-tuple-element.29), channel_id=1, source_target_pairs={{0,1},{1,0},{2,3},{3,2},{4,5},{5,4},{6,7},{7,6},{8,9},{9,8},{10,11... | collective-permute-start | bytes 2359304 | tf_op jit(solution)/shard_map/ppermute | solution.py:421
  15.6 10.9 %collective-permute-start = (f32[768,256]{1,0:T(8,128)S(1)}, f32[768,256]{1,0:T(8,128)}, u32[]{:S(2)}, u32[]{:S(2)}) collective-permute-start(f32[768,256]{1,0:T(8,128)S(1)} %get-tuple-element.27), channel_id=1, source_target_pairs={{0,1},{1,0},{2,3},{3,2},{4,5},{5,4},{6,7},{7,6},{8,9},{9,8},{10,11... | collective-permute-start | bytes 2359304 | tf_op jit(solution)/shard_map/ppermute | solution.py:421
  20.7 12.6 %collective-permute-start.17 = (f32[384,256]{1,0:T(8,128)}, f32[384,256]{1,0:T(8,128)S(1)}, u32[]{:S(2)}, u32[]{:S(2)}) collective-permute-start(f32[384,256]{1,0:T(8,128)} %constant_dynamic-slice_fusion.8), channel_id=1, source_target_pairs={{0,8},{2,10},{4,12},{6,14},{8,0},{10,2},{12,4},{14,6},{16,24},{18,... | collective-permute-start | bytes 1179656 | tf_op jit(solution)/shard_map/ppermute | solution.py:421
  24.9 10.9 %collective-permute-start.9 = (f32[384,256]{1,0:T(8,128)S(1)}, f32[384,256]{1,0:T(8,128)S(1)}, u32[]{:S(2)}, u32[]{:S(2)}) collective-permute-start(f32[384,256]{1,0:T(8,128)S(1)} %constant_dynamic-slice_fusion.11), channel_id=1, source_target_pairs={{0,4},{2,6},{4,0},{6,2},{8,12},{10,14},{12,8},{14,10},{16,20},{18,... | collective-permute-start | bytes 1179656 | tf_op jit(solution)/shard_map/ppermute | solution.py:421
  27.8 12.1 %collective-permute-start.1 = (f32[384,256]{1,0:T(8,128)S(1)}, f32[384,256]{1,0:T(8,128)S(1)}, u32[]{:S(2)}, u32[]{:S(2)}) collective-permute-start(f32[384,256]{1,0:T(8,128)S(1)} %constant_dynamic-slice_fusion.14), channel_id=1, source_target_pairs={{0,2},{2,0},{4,6},{6,4},{8,10},{10,8},{12,14},{14,12},{16,18},{18,... | collective-permute-start | bytes 1179656 | tf_op jit(solution)/shard_map/ppermute | solution.py:421
  33.4 9.3 %collective-permute-start.18 = (f32[192,256]{1,0:T(8,128)S(1)}, f32[192,256]{1,0:T(8,128)S(1)}, u32[]{:S(2)}, u32[]{:S(2)}) collective-permute-start(f32[192,256]{1,0:T(8,128)S(1)} %constant_dynamic-slice_fusion.7), channel_id=1, source_target_pairs={{0,2},{2,0},{4,6},{6,4},{8,10},{10,8},{12,14},{14,12},{16,18},{18,... | collective-permute-start | bytes 589832 | tf_op jit(solution)/shard_map/ppermute | solution.py:421
  36.0 7.3 %collective-permute-start.10 = (f32[192,256]{1,0:T(8,128)S(1)}, f32[192,256]{1,0:T(8,128)S(1)}, u32[]{:S(2)}, u32[]{:S(2)}) collective-permute-start(f32[192,256]{1,0:T(8,128)S(1)} %constant_dynamic-slice_fusion.10), channel_id=1, source_target_pairs={{0,8},{2,10},{4,12},{6,14},{8,0},{10,2},{12,4},{14,6},{16,24},{18,... | collective-permute-start | bytes 589832 | tf_op jit(solution)/shard_map/ppermute | solution.py:421
  40.0 6.8 %collective-permute-start.2 = (f32[192,256]{1,0:T(8,128)S(1)}, f32[192,256]{1,0:T(8,128)S(1)}, u32[]{:S(2)}, u32[]{:S(2)}) collective-permute-start(f32[192,256]{1,0:T(8,128)S(1)} %constant_dynamic-slice_fusion.13), channel_id=1, source_target_pairs={{0,4},{2,6},{4,0},{6,2},{8,12},{10,14},{12,8},{14,10},{16,20},{18,... | collective-permute-start | bytes 589832 | tf_op jit(solution)/shard_map/ppermute | solution.py:421
  43.4 7.1 %collective-permute-start.11 = (f32[96,256]{1,0:T(8,128)S(1)}, f32[96,256]{1,0:T(8,128)S(1)}, u32[]{:S(2)}, u32[]{:S(2)}) collective-permute-start(f32[96,256]{1,0:T(8,128)S(1)} %constant_dynamic-slice_fusion.9), channel_id=1, source_target_pairs={{0,2},{2,0},{4,6},{6,4},{8,10},{10,8},{12,14},{14,12},{16,18},{18,... | collective-permute-start | bytes 294920 | tf_op jit(solution)/shard_map/ppermute | solution.py:421
  46.8 5.7 %collective-permute-start.3 = (f32[96,256]{1,0:T(8,128)S(1)}, f32[96,256]{1,0:T(8,128)S(1)}, u32[]{:S(2)}, u32[]{:S(2)}) collective-permute-start(f32[96,256]{1,0:T(8,128)S(1)} %constant_dynamic-slice_fusion.12), channel_id=1, source_target_pairs={{0,8},{2,10},{4,12},{6,14},{8,0},{10,2},{12,4},{14,6},{16,24},{18,... | collective-permute-start | bytes 294920 | tf_op jit(solution)/shard_map/ppermute | solution.py:421
  47.8 11.8 %collective-permute-start.20 = (f32[96,256]{1,0:T(8,128)S(1)}, f32[96,256]{1,0:T(8,128)S(1)}, u32[]{:S(2)}, u32[]{:S(2)}) collective-permute-start(f32[96,256]{1,0:T(8,128)S(1)} %dynamic-slice_add_fusion.9), channel_id=1, source_target_pairs={{0,16},{2,18},{4,20},{6,22},{8,24},{10,26},{12,28},{14,30},{16,0},... | collective-permute-start | bytes 294920 | tf_op jit(solution)/shard_map/ppermute | solution.py:421
  50.5 11.1 %collective-permute-start.12 = (f32[96,256]{1,0:T(8,128)S(1)}, f32[96,256]{1,0:T(8,128)S(1)}, u32[]{:S(2)}, u32[]{:S(2)}) collective-permute-start(f32[96,256]{1,0:T(8,128)S(1)} %dynamic-slice_add_fusion.10), channel_id=1, source_target_pairs={{0,16},{2,18},{4,20},{6,22},{8,24},{10,26},{12,28},{14,30},{16,0},... | collective-permute-start | bytes 294920 | tf_op jit(solution)/shard_map/ppermute | solution.py:421
  52.6 10.6 %collective-permute-start.4 = (f32[96,256]{1,0:T(8,128)S(1)}, f32[96,256]{1,0:T(8,128)S(1)}, u32[]{:S(2)}, u32[]{:S(2)}) collective-permute-start(f32[96,256]{1,0:T(8,128)S(1)} %dynamic-slice_add_fusion.11), channel_id=1, source_target_pairs={{0,16},{2,18},{4,20},{6,22},{8,24},{10,26},{12,28},{14,30},{16,0},... | collective-permute-start | bytes 294920 | tf_op jit(solution)/shard_map/ppermute | solution.py:421
  61.7 5.7 %collective-permute-start.13 = (f32[96,256]{1,0:T(8,128)S(1)}, f32[96,256]{1,0:T(8,128)S(1)}, u32[]{:S(2)}, u32[]{:S(2)}) collective-permute-start(f32[96,256]{1,0:T(8,128)S(1)} %add.204), channel_id=1, source_target_pairs={{0,2},{2,0},{4,6},{6,4},{8,10},{10,8},{12,14},{14,12},{16,18},{18,... | collective-permute-start | bytes 294920 | tf_op jit(solution)/shard_map/ppermute | solution.py:421
  63.2 5.7 %collective-permute-start.5 = (f32[96,256]{1,0:T(8,128)S(1)}, f32[96,256]{1,0:T(8,128)S(1)}, u32[]{:S(2)}, u32[]{:S(2)}) collective-permute-start(f32[96,256]{1,0:T(8,128)S(1)} %add.193), channel_id=1, source_target_pairs={{0,8},{2,10},{4,12},{6,14},{8,0},{10,2},{12,4},{14,6},{16,24},{18,... | collective-permute-start | bytes 294920 | tf_op jit(solution)/shard_map/ppermute | solution.py:421
  64.4 5.7 %collective-permute-start.22 = (f32[192,256]{1,0:T(8,128)S(1)}, f32[192,256]{1,0:T(8,128)S(1)}, u32[]{:S(2)}, u32[]{:S(2)}) collective-permute-start(f32[192,256]{1,0:T(8,128)S(1)} %pad_maximum_fusion.11), channel_id=1, source_target_pairs={{0,2},{2,0},{4,6},{6,4},{8,10},{10,8},{12,14},{14,12},{16,18},{18,... | collective-permute-start | bytes 589832 | tf_op jit(solution)/shard_map/ppermute | solution.py:421
  67.4 7.8 %collective-permute-start.14 = (f32[192,256]{1,0:T(8,128)S(1)}, f32[192,256]{1,0:T(8,128)S(1)}, u32[]{:S(2)}, u32[]{:S(2)}) collective-permute-start(f32[192,256]{1,0:T(8,128)S(1)} %pad_maximum_fusion.10), channel_id=1, source_target_pairs={{0,8},{2,10},{4,12},{6,14},{8,0},{10,2},{12,4},{14,6},{16,24},{18,... | collective-permute-start | bytes 589832 | tf_op jit(solution)/shard_map/ppermute | solution.py:421
  69.0 7.8 %collective-permute-start.6 = (f32[192,256]{1,0:T(8,128)S(1)}, f32[192,256]{1,0:T(8,128)S(1)}, u32[]{:S(2)}, u32[]{:S(2)}) collective-permute-start(f32[192,256]{1,0:T(8,128)S(1)} %pad_maximum_fusion.9), channel_id=1, source_target_pairs={{0,4},{2,6},{4,0},{6,2},{8,12},{10,14},{12,8},{14,10},{16,20},{18,... | collective-permute-start | bytes 589832 | tf_op jit(solution)/shard_map/ppermute | solution.py:421
  70.2 10.8 %collective-permute-start.23 = (f32[384,256]{1,0:T(8,128)S(1)}, f32[384,256]{1,0:T(8,128)S(1)}, u32[]{:S(2)}, u32[]{:S(2)}) collective-permute-start(f32[384,256]{1,0:T(8,128)S(1)} %pad_maximum_fusion.5), channel_id=1, source_target_pairs={{0,8},{2,10},{4,12},{6,14},{8,0},{10,2},{12,4},{14,6},{16,24},{18,... | collective-permute-start | bytes 1179656 | tf_op jit(solution)/shard_map/ppermute | solution.py:421
  75.3 7.8 %collective-permute-start.15 = (f32[384,256]{1,0:T(8,128)S(1)}, f32[384,256]{1,0:T(8,128)S(1)}, u32[]{:S(2)}, u32[]{:S(2)}) collective-permute-start(f32[384,256]{1,0:T(8,128)S(1)} %pad_maximum_fusion.4), channel_id=1, source_target_pairs={{0,4},{2,6},{4,0},{6,2},{8,12},{10,14},{12,8},{14,10},{16,20},{18,... | collective-permute-start | bytes 1179656 | tf_op jit(solution)/shard_map/ppermute | solution.py:421
  76.9 7.8 %collective-permute-start.7 = (f32[384,256]{1,0:T(8,128)S(1)}, f32[384,256]{1,0:T(8,128)S(1)}, u32[]{:S(2)}, u32[]{:S(2)}) collective-permute-start(f32[384,256]{1,0:T(8,128)S(1)} %pad_maximum_fusion.3), channel_id=1, source_target_pairs={{0,2},{2,0},{4,6},{6,4},{8,10},{10,8},{12,14},{14,12},{16,18},{18,... | collective-permute-start | bytes 1179656 | tf_op jit(solution)/shard_map/ppermute | solution.py:421
  176.4 7.5 %collective-permute-start.47 = (f32[64,256]{1,0:T(8,128)S(1)}, f32[64,256]{1,0:T(8,128)S(1)}, u32[]{:S(2)}, u32[]{:S(2)}) collective-permute-start(f32[64,256]{1,0:T(8,128)S(1)} %add.242), channel_id=1, source_target_pairs={{0,16},{2,18},{4,20},{6,22},{8,24},{10,26},{12,28},{14,30},{16,0},... | collective-permute-start | bytes 196616 | tf_op jit(solution)/shard_map/ppermute | solution.py:421
  177.4 7.3 %collective-permute-start.40 = (f32[64,256]{1,0:T(8,128)S(1)}, f32[64,256]{1,0:T(8,128)S(1)}, u32[]{:S(2)}, u32[]{:S(2)}) collective-permute-start(f32[64,256]{1,0:T(8,128)S(1)} %add.233), channel_id=1, source_target_pairs={{0,16},{2,18},{4,20},{6,22},{8,24},{10,26},{12,28},{14,30},{16,0},... | collective-permute-start | bytes 196616 | tf_op jit(solution)/shard_map/ppermute | solution.py:421
  179.5 6.5 %collective-permute-start.33 = (f32[64,256]{1,0:T(8,128)S(1)}, f32[64,256]{1,0:T(8,128)S(1)}, u32[]{:S(2)}, u32[]{:S(2)}) collective-permute-start(f32[64,256]{1,0:T(8,128)S(1)} %add.224), channel_id=1, source_target_pairs={{0,16},{2,18},{4,20},{6,22},{8,24},{10,26},{12,28},{14,30},{16,0},... | collective-permute-start | bytes 196616 | tf_op jit(solution)/shard_map/ppermute | solution.py:421
  (33 other events, 126.2 us)

commit v7 on v6

--- a/solution.py
+++ b/solution.py
@@ -38,17 +38,27 @@
     lane = lax.broadcasted_iota(jnp.int32, (8, 128), 1)
     sub = lax.broadcasted_iota(jnp.int32, (8, 128), 0)
     rows = list(groups)
+
+    def column(w, at):
+        return jnp.broadcast_to(w[:, at:at + 1], (8, 128))
+
+    def row(w, at):
+        return jnp.broadcast_to(w[at:at + 1, :], (8, 128))
+
+    def entries(w, base):
+        cols = [column(w, base + j) for j in range(8)]
+        return {(i, j): row(cols[j], i) for j in range(8) for i in range(j, 8)}
+
+    later = entries(rows[0], 0)
     for k in range(count):
         base = 8 * k
         strip = rows[k]
         inside = (lane >= base) & (lane < base + 8)
         eye = jnp.where(lane == base + sub, 1.0, 0.0).astype(F32)
         mixed = jnp.where(inside, eye, strip)
-        cols = [jnp.broadcast_to(strip[:, base + j:base + j + 1], (8, 128)) for j in range(8)]
-        entry = {}
-        for j in range(8):
-            for i in range(j, 8):
-                entry[i, j] = jnp.broadcast_to(cols[j][i:i + 1, :], (8, 128))
+        entry = later
+        if k + 1 < count:
+            later = entries(rows[k + 1], base + 8)
         scale = []
         low = {}
         for j in range(8):
@@ -59,10 +69,25 @@
             for c in range(j + 1, 8):
                 for i in range(c, 8):
                     entry[i, c] = entry[i, c] - low[i, j] * low[c, j]
+        lefts = {}
+        for g in range(k + 1, count):
+            left = []
+            for j in range(8):
+                c = column(rows[g], base + j)
+                for i in range(j):
+                    c = c - left[i] * low[j, i]
+                left.append(c * scale[j])
+            lefts[g] = left
+            if g == k + 1:
+                for j in range(8):
+                    spread = [row(left[j], i) for i in range(8)]
+                    for c in range(8):
+                        for i in range(c, 8):
+                            later[i, c] = later[i, c] - spread[i] * spread[c]
         upper, both = [], []
         for j in range(8):
-            u = jnp.broadcast_to(strip[j:j + 1, :], (8, 128))
-            v = jnp.broadcast_to(mixed[j:j + 1, :], (8, 128))
+            u = row(strip, j)
+            v = row(mixed, j)
             for i in range(j):
                 u = u - low[j, i] * upper[i]
                 v = v - low[j, i] * both[i]
@@ -79,16 +104,9 @@
             jnp.where(lane <= base + sub, out_m, 0.0),
         )
         for g in range(k + 1, count):
-            w = rows[g]
-            new = jnp.where(inside, 0.0, w)
-            left = []
+            new = jnp.where(inside, 0.0, rows[g])
             for j in range(8):
-                c = jnp.broadcast_to(w[:, base + j:base + j + 1], (8, 128))
-                for i in range(j):
-                    c = c - left[i] * low[j, i]
-                c = c * scale[j]
-                left.append(c)
-                new = new - c * both[j]
+                new = new - lefts[g][j] * both[j]
             rows[g] = new
 
 
@@ -165,29 +183,68 @@
         at += 2 * h
 
 
-def cross_kernel(parts, scale, core_ref, e_ref, x_ref, *refs):
-    sends, keeps, acc = refs[:parts], refs[parts:2 * parts], refs[-1]
+def cross_kernel(parts, tile, core_ref, e_in, x_in, *refs):
+    sends, keeps = refs[:parts], refs[parts:2 * parts]
+    e_ref, x_ref, even, odd, acc, in_sems, out_sems = refs[2 * parts:]
     k = e_ref.shape[1]
     p = x_ref.shape[1] // 2
-    step = pl.program_id(0)
-
-    @pl.when(step == 0)
-    def _():
-        acc[...] = jnp.zeros_like(acc)
-
-    et = e_ref[...].T
-    at = 0
-    for c in range(2):
-        acc[at:at + k] += dot(et, x_ref[:, c * p:(c + 1) * p])
-        at += k
-    for j in range(k // p):
-        m = (j + 1) * p
-        acc[at:at + m] += dot(et[:m], e_ref[:, j * p:(j + 1) * p])
-        at += m
-
-    @pl.when(step == pl.num_programs(0) - 1)
-    def _():
-        deal(core_ref, acc, scale, sends, keeps)
+    tiles = e_ref.shape[0] // tile
+    ahead = min(3, tiles)
+    inputs = [(e_in, e_ref), (x_in, x_ref)]
+    h = sends[0].shape[0]
+    outputs = []
+    for n in range(parts):
+        away, stay = (2 * n + 1 - core_ref[0]) * h, (2 * n + core_ref[0]) * h
+        outputs.append([
+            (acc.at[pl.ds(pl.multiple_of(away, 8), h)], sends[n]),
+            (acc.at[pl.ds(pl.multiple_of(stay, 8), h)], keeps[n]),
+        ])
+    jobs = [(k, x_ref, c) for c in range(2)] + [((j + 1) * p, e_ref, j) for j in range(k // p)]
+
+    def turn(i, target):
+        target[...] = e_ref[tile_rows(i, tile), :].T
+
+    def products(i, left):
+        rows = tile_rows(i, tile)
+        at = 0
+        for m, right, c in jobs:
+            acc[at:at + m] += dot(left[:m], right[rows, c * p:(c + 1) * p])
+            at += m
+
+    def arrive(i):
+        finish(at_tile(inputs, i, tile), in_sems.at[i])
+
+        @pl.when(i + ahead < tiles)
+        def _():
+            begin(at_tile(inputs, i + ahead, tile), in_sems.at[i + ahead])
+
+    for i in range(ahead):
+        begin(at_tile(inputs, i, tile), in_sems.at[i])
+    acc[...] = jnp.zeros_like(acc)
+    arrive(0)
+    turn(0, even)
+
+    def step(t, carry):
+        i = 2 * t
+        arrive(i + 1)
+
+        @pl.when(i + 2 < tiles)
+        def _():
+            arrive(i + 2)
+
+        products(i, even)
+        turn(i + 1, odd)
+        products(i + 1, odd)
+        turn(jnp.minimum(i + 2, tiles - 1), even)
+        return carry
+
+    lax.fori_loop(0, tiles // 2, step, 0)
+    if tiles % 2:
+        products(tiles - 1, even)
+    for n in range(parts):
+        begin(outputs[n], out_sems.at[n])
+    for n in range(parts):
+        finish(outputs[n], out_sems.at[n])
 
 
 def first_kernel(parts, tile, scale, core_ref, *refs):
@@ -213,7 +270,7 @@
     for j in range(k // p):
         cols = slice(j * p, (j + 1) * p)
         for i in range(j + 1):
-            block = total[at:at + p]
+            block = total[at:at + p] * scale
             at += p
             if i == j:
                 a = lax.broadcasted_iota(jnp.int32, (p, p), 0)
@@ -227,7 +284,7 @@
                 offh[cols, rows] = high.T
                 offl[cols, rows] = low.T
     for c in range(2):
-        coef = total[c * k:(c + 1) * k]
+        coef = total[c * k:(c + 1) * k] * scale
         b = coef.astype(BF16)
         b_ref[:, c * p:(c + 1) * p] = b
         after = (coef - wide(b)) - dot(offh[...], b) - dot(offl[...], b)
@@ -468,17 +525,10 @@
     rows = (2 * blocks + blocks * (blocks + 1) // 2) * p
     unit = 2 * devices * 8
     parts = 3 if rows % (3 * unit) == 0 else 1
-    tile = 1024 if n % 1024 == 0 else n
 
     def smem():
         return pl.BlockSpec(memory_space=pltpu.SMEM)
 
-    def whole(*shape):
-        return pl.BlockSpec(shape, lambda i: (0,) * len(shape))
-
-    def tiled(cols):
-        return pl.BlockSpec((tile, cols), lambda i: (i, 0))
-
     def shape(*dims, dtype=F32):
         return jax.ShapeDtypeStruct(dims, dtype)
 
@@ -496,10 +546,9 @@
 
     earlier, snapshots, later = fixed(earlier), fixed(snapshots), fixed(later)
 
-    def call(kernel, name, room, ins, outs, scratch, flops, size, *args, grid=None):
+    def call(kernel, name, room, ins, outs, scratch, flops, size, *args):
         return pl.pallas_call(
             kernel,
-            grid=(n // tile,) if grid is None else grid,
             in_specs=[s for s in ins],
             out_specs=[s for s, _ in outs],
             out_shape=[s for _, s in outs],
@@ -519,23 +568,22 @@
         return pltpu.VMEM(dims, dtype)
 
     half = rows // parts // 2
-    halves = [(whole(half, p), near(half, p))] * (2 * parts)
     got = call(
-        lambda *r: cross_kernel(parts, scale, *r), "cross", 32,
-        [smem(), tiled(k), tiled(2 * p)],
-        halves,
-        [pltpu.VMEM((rows, p), F32)],
+        lambda *r: cross_kernel(parts, short, *r), "cross", 32,
+        [smem(), apart, apart],
+        [(apart, near(half, p))] * (2 * parts),
+        [
+            held(n, k, dtype=BF16),
+            held(n, 2 * p, dtype=BF16),
+            held(k, short, dtype=BF16),
+            held(k, short, dtype=BF16),
+            held(rows, p),
+            dma((tiles, 2)), dma((parts, 2)),
+        ],
         2 * n * rows * p, 2 * n * (k + 2 * p),
         core, earlier, snapshots,
     )
     own, other = summed(got[:parts], got[parts:], 1)
-
-    short = 512 if n % 512 == 0 else n
-    tiles = n // short
-    dma = pltpu.SemaphoreType.DMA
-
-    def held(*dims, dtype=F32):
-        return pltpu.VMEM(dims, dtype)
 
     u, w, z, h, t, send, keep = call(
         lambda *r: first_kernel(parts, short, scale, *r), "first", 50,
@@ -565,7 +613,7 @@
             dma((2 * parts,)), dma((tiles, 2)), dma((tiles, 2)), dma((2,)),
         ],
         2 * n * p * (3 * k + 4 * p) + 12 * k * k * p, n * (2 * k + 12 * p),
-        core, *own, *other, earlier, snapshots, grid=(),
+        core, *own, *other, earlier, snapshots,
     )
     own, other = summed_at_once(send, keep)
 
@@ -599,7 +647,7 @@
             dma((2,)), dma((2,)), dma((tiles, 4)), dma((tiles, 2)),
         ],
         2 * n * p * (k + 15 * p), n * (2 * k + 18 * p),
-        core, own, other, fixed(z), fixed(h), t, earlier, fixed(u), fixed(w), later, grid=(),
+        core, own, other, fixed(z), fixed(h), t, earlier, fixed(u), fixed(w), later,
     )
     q_one, w2, r_one, expected = got[:4]
     own, other = summed(got[4:7], got[7:], 2)
@@ -625,7 +673,7 @@
             dma((6,)), dma((tiles, 2)), dma((tiles, 1)),
         ],
         2 * n * p * 4 * p, n * 10 * p,
-        core, *own, *other, expected, r_one, fixed(q_one), fixed(w2), grid=(),
+        core, *own, *other, expected, r_one, fixed(q_one), fixed(w2),
     ))
 
 

time: 213 us -> 215 us (level)
  no operation moved by 1% of the time
where the time goes in v7:
time: 215 us; the launch traced here: 214 us
  Pallas kernels  74.2 us (35%)
  waiting for transfers between devices  62.7 us (29%)
  starting transfers between devices  41.7 us (19%)
  blocking collectives  27.4 us (13%)
  other arithmetic  5.07 us (2%)
    pallas_call x4, Pallas kernels, call(): pl.pallas_call(kernel, in_specs=[s for s in ins], out_specs=[s for s, _ i...  74.2 us
    ppermute x53, waiting for transfers between devices, exchange(): return lax.ppermute(x, axis, [(i, i ^ 1 << bit) for i in range(size)])  62.7 us
    ppermute x53, starting transfers between devices, exchange(): return lax.ppermute(x, axis, [(i, i ^ 1 << bit) for i in range(size)])  41.7 us
    all_to_all x1, blocking collectives, summed_at_once(): got = lax.all_to_all(x, 'rows', 0, 0, tiled=True)  14.7 us
    all_to_all x1, blocking collectives, summed_at_once(): x = lax.all_to_all(same, 'rows', 0, 0, tiled=True)  12.8 us
  transfers between devices with their start and end apart: 53, of which 40 were waited for; matrix products, arithmetic and copies ran while one was open for 3% of the time, Pallas kernels for 0%

profile of v7, /device:TPU:0, one launch (start us, length us, event | category | flops | bytes accessed | tf_op | source)
XLA Modules:
  0.0 214.5 jit_solution(14708738397298148594)
XLA Ops:
  0.6 14.3 %cross.1 = (f32[768,256]{1,0:T(8,128)S(1)}, f32[768,256]{1,0:T(8,128)}, f32[768,256]{1,0:T(8,128)}, f32[768,256]{1,0:T(8,128)S(1)}, f32[768,256]{1,0:T(8,128)S(1)}, /*index=5*/f32[768,256]{1,0:T(8,128)S(1)}) custom-call(s32[1]{0:T(128)} %bitcast.r_0_, bf16[4096,1024]{1,0:T(8,128)(2,1)} %r_6_.1, bf16[4096,512]{1,0:T(8,128)(2,1)} %r_8_.1), custom_call_target="tpu_custom_call" | custom-call | flops 9663676416 | bytes 12582912 | tf_op jit(solution)/shard_map/cross/pallas_call | solution.py:550
  16.0 1.7 collective-permute-done.16
  20.6 2.9 %collective-permute-start.17 = (f32[384,256]{1,0:T(8,128)}, f32[384,256]{1,0:T(8,128)S(1)}, u32[]{:S(2)}, u32[]{:S(2)}) collective-permute-start(f32[384,256]{1,0:T(8,128)} %constant_dynamic-slice_fusion.8), channel_id=1, source_target_pairs={{0,8},{2,10},{4,12},{6,14},{8,0},{10,2},{12,4},{14,6},{16,24},{18,... | collective-permute-start | bytes 1179656 | tf_op jit(solution)/shard_map/ppermute | solution.py:478
  29.3 3.9 %collective-permute-done.17 = f32[384,256]{1,0:T(8,128)S(1)} collective-permute-done((f32[384,256]{1,0:T(8,128)}, f32[384,256]{1,0:T(8,128)S(1)}, u32[]{:S(2)}, u32[]{:S(2)}) %collective-permute-start.17) | collective-permute-done | bytes 393248 | tf_op jit(solution)/shard_map/ppermute | solution.py:478
  33.3 1.7 collective-permute-start.18
  36.7 3.1 %collective-permute-done.1 = f32[384,256]{1,0:T(8,128)S(1)} collective-permute-done((f32[384,256]{1,0:T(8,128)S(1)}, f32[384,256]{1,0:T(8,128)S(1)}, u32[]{:S(2)}, u32[]{:S(2)}) %collective-permute-start.1) | collective-permute-done | bytes 393248 | tf_op jit(solution)/shard_map/ppermute | solution.py:478
  40.5 2.1 collective-permute-done.18
  44.8 1.9 collective-permute-done.2
  47.8 2.7 %collective-permute-start.20 = (f32[96,256]{1,0:T(8,128)S(1)}, f32[96,256]{1,0:T(8,128)S(1)}, u32[]{:S(2)}, u32[]{:S(2)}) collective-permute-start(f32[96,256]{1,0:T(8,128)S(1)} %dynamic-slice_add_fusion.9), channel_id=1, source_target_pairs={{0,16},{2,18},{4,20},{6,22},{8,24},{10,26},{12,28},{14,30},{16,0},... | collective-permute-start | bytes 294920 | tf_op jit(solution)/shard_map/ppermute | solution.py:478
  52.5 2.7 %collective-permute-start.4 = (f32[96,256]{1,0:T(8,128)S(1)}, f32[96,256]{1,0:T(8,128)S(1)}, u32[]{:S(2)}, u32[]{:S(2)}) collective-permute-start(f32[96,256]{1,0:T(8,128)S(1)} %dynamic-slice_add_fusion.11), channel_id=1, source_target_pairs={{0,16},{2,18},{4,20},{6,22},{8,24},{10,26},{12,28},{14,30},{16,0},... | collective-permute-start | bytes 294920 | tf_op jit(solution)/shard_map/ppermute | solution.py:478
  55.1 4.4 %collective-permute-done.20 = f32[96,256]{1,0:T(8,128)S(1)} collective-permute-done((f32[96,256]{1,0:T(8,128)S(1)}, f32[96,256]{1,0:T(8,128)S(1)}, u32[]{:S(2)}, u32[]{:S(2)}) %collective-permute-start.20) | collective-permute-done | bytes 98336 | tf_op jit(solution)/shard_map/ppermute | solution.py:478
  59.8 1.7 collective-permute-done.12
  71.1 4.0 %collective-permute-done.14 = f32[192,256]{1,0:T(8,128)S(1)} collective-permute-done((f32[192,256]{1,0:T(8,128)S(1)}, f32[192,256]{1,0:T(8,128)S(1)}, u32[]{:S(2)}, u32[]{:S(2)}) %collective-permute-start.14) | collective-permute-done | bytes 196640 | tf_op jit(solution)/shard_map/ppermute | solution.py:478
  77.8 3.0 %collective-permute-done.23 = f32[384,256]{1,0:T(8,128)S(1)} collective-permute-done((f32[384,256]{1,0:T(8,128)S(1)}, f32[384,256]{1,0:T(8,128)S(1)}, u32[]{:S(2)}, u32[]{:S(2)}) %collective-permute-start.23) | collective-permute-done | bytes 393248 | tf_op jit(solution)/shard_map/ppermute | solution.py:478
  81.1 2.0 collective-permute-done.15
  87.1 18.1 %first.1 = (f32[4096,256]{1,0:T(8,128)}, bf16[4096,512]{1,0:T(8,128)(2,1)}, f32[1024,256]{1,0:T(8,128)}, f32[1024,256]{1,0:T(8,128)}, f32[256,256]{1,0:T(8,128)S...) custom-call(s32[1]{0:T(128)} %bitcast.r_0_, f32[768,256]{1,0:T(8,128)S(1)} %pad_maximum_fusion.r_1_, ...), custom_call_target="tpu_custom_call" | custom-call | flops 11811160064 | bytes 20971520 | tf_op jit(solution)/shard_map/first/pallas_call | solution.py:550
  106.8 14.7 %all_to_all.17 = f32[16,16,256]{2,1,0:T(8,128)S(1)} all-to-all(f32[16,16,256]{2,1,0:T(8,128)S(1)} %bitcast.5), channel_id=1, replica_groups=mesh['rows'=16,'grp'=2] {'rows'}, dimensions={0} | all-to-all | bytes 524288 | tf_op jit(solution)/shard_map/all_to_all | solution.py:511
  121.5 12.8 %all_to_all.18 = f32[16,16,256]{2,1,0:T(8,128)S(1)} all-to-all(f32[16,16,256]{2,1,0:T(8,128)S(1)} %broadcast_in_dim.2), channel_id=1, replica_groups=mesh['rows'=16,'grp'=2] {'rows'}, dimensions={0} | all-to-all | bytes 524288 | tf_op jit(solution)/shard_map/all_to_all | solution.py:514
  135.8 25.7 %second.1 = (bf16[4096,256]{1,0:T(8,128)(2,1)}, bf16[4096,512]{1,0:T(8,128)(2,1)}, f32[256,256]{1,0:T(8,128)S(1)}, f32[256,256]{1,0:T(8,128)S(1)}, f32[256,256]{...) custom-call(s32[1]{0:T(128)} %bitcast.r_0_, ...), custom_call_target="tpu_custom_call" | custom-call | flops 10200547328 | bytes 27262976 | tf_op jit(solution)/shard_map/second/pallas_call | solution.py:550
  165.9 2.9 %collective-permute-done.44 = f32[128,256]{1,0:T(8,128)S(1)} collective-permute-done((f32[128,256]{1,0:T(8,128)S(1)}, f32[128,256]{1,0:T(8,128)S(1)}, u32[]{:S(2)}, u32[]{:S(2)}) %collective-permute-start.44) | collective-permute-done | bytes 131104 | tf_op jit(solution)/shard_map/ppermute | solution.py:478
  178.5 2.1 collective-permute-start.40
  181.6 3.4 %collective-permute-done.47 = f32[64,256]{1,0:T(8,128)S(1)} collective-permute-done((f32[64,256]{1,0:T(8,128)S(1)}, f32[64,256]{1,0:T(8,128)S(1)}, u32[]{:S(2)}, u32[]{:S(2)}) %collective-permute-start.47) | collective-permute-done | bytes 65568 | tf_op jit(solution)/shard_map/ppermute | solution.py:478
  192.6 1.8 collective-permute-done.49
  198.2 16.1 %last.1 = (bf16[4096,512]{1,0:T(8,128)(2,1)}, f32[2,256,256]{2,1,0:T(8,128)}, f32[512,512]{1,0:T(8,128)}) custom-call(s32[1]{0:T(128)} %bitcast.r_0_, f32[256,256]{1,0:T(8,128)S(1)} %pad_maximum_fusion.6.r_1_, f32[256,256]{1,0:T(8,128)S(1)} %pad_maximum_fusion.7.r_2_, f32[256,256]{1,0:T(8,128)S(1)} %pad_maximum_fusion.8.r_3_, ...), custom_call_target="tpu_custom_call" | custom-call | flops 2147483648 | bytes 10485760 | tf_op jit(solution)/shard_map/last/pallas_call | solution.py:550
  (174 shorter events, 63.4 us)
Async XLA Ops:
  15.5 8.1 %collective-permute-start.8 = (f32[768,256]{1,0:T(8,128)}, f32[768,256]{1,0:T(8,128)}, u32[]{:S(2)}, u32[]{:S(2)}) collective-permute-start(f32[768,256]{1,0:T(8,128)} %get-tuple-element.29), channel_id=1, source_target_pairs={{0,1},{1,0},{2,3},{3,2},{4,5},{5,4},{6,7},{7,6},{8,9},{9,8},{10,11... | collective-permute-start | bytes 2359304 | tf_op jit(solution)/shard_map/ppermute | solution.py:478
  15.5 10.9 %collective-permute-start = (f32[768,256]{1,0:T(8,128)S(1)}, f32[768,256]{1,0:T(8,128)}, u32[]{:S(2)}, u32[]{:S(2)}) collective-permute-start(f32[768,256]{1,0:T(8,128)S(1)} %get-tuple-element.27), channel_id=1, source_target_pairs={{0,1},{1,0},{2,3},{3,2},{4,5},{5,4},{6,7},{7,6},{8,9},{9,8},{10,11... | collective-permute-start | bytes 2359304 | tf_op jit(solution)/shard_map/ppermute | solution.py:478
  20.6 12.6 %collective-permute-start.17 = (f32[384,256]{1,0:T(8,128)}, f32[384,256]{1,0:T(8,128)S(1)}, u32[]{:S(2)}, u32[]{:S(2)}) collective-permute-start(f32[384,256]{1,0:T(8,128)} %constant_dynamic-slice_fusion.8), channel_id=1, source_target_pairs={{0,8},{2,10},{4,12},{6,14},{8,0},{10,2},{12,4},{14,6},{16,24},{18,... | collective-permute-start | bytes 1179656 | tf_op jit(solution)/shard_map/ppermute | solution.py:478
  24.8 10.9 %collective-permute-start.9 = (f32[384,256]{1,0:T(8,128)S(1)}, f32[384,256]{1,0:T(8,128)S(1)}, u32[]{:S(2)}, u32[]{:S(2)}) collective-permute-start(f32[384,256]{1,0:T(8,128)S(1)} %constant_dynamic-slice_fusion.11), channel_id=1, source_target_pairs={{0,4},{2,6},{4,0},{6,2},{8,12},{10,14},{12,8},{14,10},{16,20},{18,... | collective-permute-start | bytes 1179656 | tf_op jit(solution)/shard_map/ppermute | solution.py:478
  27.7 12.1 %collective-permute-start.1 = (f32[384,256]{1,0:T(8,128)S(1)}, f32[384,256]{1,0:T(8,128)S(1)}, u32[]{:S(2)}, u32[]{:S(2)}) collective-permute-start(f32[384,256]{1,0:T(8,128)S(1)} %constant_dynamic-slice_fusion.14), channel_id=1, source_target_pairs={{0,2},{2,0},{4,6},{6,4},{8,10},{10,8},{12,14},{14,12},{16,18},{18,... | collective-permute-start | bytes 1179656 | tf_op jit(solution)/shard_map/ppermute | solution.py:478
  33.3 9.3 %collective-permute-start.18 = (f32[192,256]{1,0:T(8,128)S(1)}, f32[192,256]{1,0:T(8,128)S(1)}, u32[]{:S(2)}, u32[]{:S(2)}) collective-permute-start(f32[192,256]{1,0:T(8,128)S(1)} %constant_dynamic-slice_fusion.7), channel_id=1, source_target_pairs={{0,2},{2,0},{4,6},{6,4},{8,10},{10,8},{12,14},{14,12},{16,18},{18,... | collective-permute-start | bytes 589832 | tf_op jit(solution)/shard_map/ppermute | solution.py:478
  35.9 7.3 %collective-permute-start.10 = (f32[192,256]{1,0:T(8,128)S(1)}, f32[192,256]{1,0:T(8,128)S(1)}, u32[]{:S(2)}, u32[]{:S(2)}) collective-permute-start(f32[192,256]{1,0:T(8,128)S(1)} %constant_dynamic-slice_fusion.10), channel_id=1, source_target_pairs={{0,8},{2,10},{4,12},{6,14},{8,0},{10,2},{12,4},{14,6},{16,24},{18,... | collective-permute-start | bytes 589832 | tf_op jit(solution)/shard_map/ppermute | solution.py:478
  39.9 6.8 %collective-permute-start.2 = (f32[192,256]{1,0:T(8,128)S(1)}, f32[192,256]{1,0:T(8,128)S(1)}, u32[]{:S(2)}, u32[]{:S(2)}) collective-permute-start(f32[192,256]{1,0:T(8,128)S(1)} %constant_dynamic-slice_fusion.13), channel_id=1, source_target_pairs={{0,4},{2,6},{4,0},{6,2},{8,12},{10,14},{12,8},{14,10},{16,20},{18,... | collective-permute-start | bytes 589832 | tf_op jit(solution)/shard_map/ppermute | solution.py:478
  43.3 7.2 %collective-permute-start.11 = (f32[96,256]{1,0:T(8,128)S(1)}, f32[96,256]{1,0:T(8,128)S(1)}, u32[]{:S(2)}, u32[]{:S(2)}) collective-permute-start(f32[96,256]{1,0:T(8,128)S(1)} %constant_dynamic-slice_fusion.9), channel_id=1, source_target_pairs={{0,2},{2,0},{4,6},{6,4},{8,10},{10,8},{12,14},{14,12},{16,18},{18,... | collective-permute-start | bytes 294920 | tf_op jit(solution)/shard_map/ppermute | solution.py:478
  46.7 5.7 %collective-permute-start.3 = (f32[96,256]{1,0:T(8,128)S(1)}, f32[96,256]{1,0:T(8,128)S(1)}, u32[]{:S(2)}, u32[]{:S(2)}) collective-permute-start(f32[96,256]{1,0:T(8,128)S(1)} %constant_dynamic-slice_fusion.12), channel_id=1, source_target_pairs={{0,8},{2,10},{4,12},{6,14},{8,0},{10,2},{12,4},{14,6},{16,24},{18,... | collective-permute-start | bytes 294920 | tf_op jit(solution)/shard_map/ppermute | solution.py:478
  47.8 11.8 %collective-permute-start.20 = (f32[96,256]{1,0:T(8,128)S(1)}, f32[96,256]{1,0:T(8,128)S(1)}, u32[]{:S(2)}, u32[]{:S(2)}) collective-permute-start(f32[96,256]{1,0:T(8,128)S(1)} %dynamic-slice_add_fusion.9), channel_id=1, source_target_pairs={{0,16},{2,18},{4,20},{6,22},{8,24},{10,26},{12,28},{14,30},{16,0},... | collective-permute-start | bytes 294920 | tf_op jit(solution)/shard_map/ppermute | solution.py:478
  50.4 11.1 %collective-permute-start.12 = (f32[96,256]{1,0:T(8,128)S(1)}, f32[96,256]{1,0:T(8,128)S(1)}, u32[]{:S(2)}, u32[]{:S(2)}) collective-permute-start(f32[96,256]{1,0:T(8,128)S(1)} %dynamic-slice_add_fusion.10), channel_id=1, source_target_pairs={{0,16},{2,18},{4,20},{6,22},{8,24},{10,26},{12,28},{14,30},{16,0},... | collective-permute-start | bytes 294920 | tf_op jit(solution)/shard_map/ppermute | solution.py:478
  52.5 10.6 %collective-permute-start.4 = (f32[96,256]{1,0:T(8,128)S(1)}, f32[96,256]{1,0:T(8,128)S(1)}, u32[]{:S(2)}, u32[]{:S(2)}) collective-permute-start(f32[96,256]{1,0:T(8,128)S(1)} %dynamic-slice_add_fusion.11), channel_id=1, source_target_pairs={{0,16},{2,18},{4,20},{6,22},{8,24},{10,26},{12,28},{14,30},{16,0},... | collective-permute-start | bytes 294920 | tf_op jit(solution)/shard_map/ppermute | solution.py:478
  61.6 5.7 %collective-permute-start.13 = (f32[96,256]{1,0:T(8,128)S(1)}, f32[96,256]{1,0:T(8,128)S(1)}, u32[]{:S(2)}, u32[]{:S(2)}) collective-permute-start(f32[96,256]{1,0:T(8,128)S(1)} %add.204), channel_id=1, source_target_pairs={{0,2},{2,0},{4,6},{6,4},{8,10},{10,8},{12,14},{14,12},{16,18},{18,... | collective-permute-start | bytes 294920 | tf_op jit(solution)/shard_map/ppermute | solution.py:478
  63.1 5.7 %collective-permute-start.5 = (f32[96,256]{1,0:T(8,128)S(1)}, f32[96,256]{1,0:T(8,128)S(1)}, u32[]{:S(2)}, u32[]{:S(2)}) collective-permute-start(f32[96,256]{1,0:T(8,128)S(1)} %add.193), channel_id=1, source_target_pairs={{0,8},{2,10},{4,12},{6,14},{8,0},{10,2},{12,4},{14,6},{16,24},{18,... | collective-permute-start | bytes 294920 | tf_op jit(solution)/shard_map/ppermute | solution.py:478
  64.3 5.7 %collective-permute-start.22 = (f32[192,256]{1,0:T(8,128)S(1)}, f32[192,256]{1,0:T(8,128)S(1)}, u32[]{:S(2)}, u32[]{:S(2)}) collective-permute-start(f32[192,256]{1,0:T(8,128)S(1)} %pad_maximum_fusion.11), channel_id=1, source_target_pairs={{0,2},{2,0},{4,6},{6,4},{8,10},{10,8},{12,14},{14,12},{16,18},{18,... | collective-permute-start | bytes 589832 | tf_op jit(solution)/shard_map/ppermute | solution.py:478
  67.3 7.8 %collective-permute-start.14 = (f32[192,256]{1,0:T(8,128)S(1)}, f32[192,256]{1,0:T(8,128)S(1)}, u32[]{:S(2)}, u32[]{:S(2)}) collective-permute-start(f32[192,256]{1,0:T(8,128)S(1)} %pad_maximum_fusion.10), channel_id=1, source_target_pairs={{0,8},{2,10},{4,12},{6,14},{8,0},{10,2},{12,4},{14,6},{16,24},{18,... | collective-permute-start | bytes 589832 | tf_op jit(solution)/shard_map/ppermute | solution.py:478
  68.9 7.8 %collective-permute-start.6 = (f32[192,256]{1,0:T(8,128)S(1)}, f32[192,256]{1,0:T(8,128)S(1)}, u32[]{:S(2)}, u32[]{:S(2)}) collective-permute-start(f32[192,256]{1,0:T(8,128)S(1)} %pad_maximum_fusion.9), channel_id=1, source_target_pairs={{0,4},{2,6},{4,0},{6,2},{8,12},{10,14},{12,8},{14,10},{16,20},{18,... | collective-permute-start | bytes 589832 | tf_op jit(solution)/shard_map/ppermute | solution.py:478
  70.1 10.7 %collective-permute-start.23 = (f32[384,256]{1,0:T(8,128)S(1)}, f32[384,256]{1,0:T(8,128)S(1)}, u32[]{:S(2)}, u32[]{:S(2)}) collective-permute-start(f32[384,256]{1,0:T(8,128)S(1)} %pad_maximum_fusion.5), channel_id=1, source_target_pairs={{0,8},{2,10},{4,12},{6,14},{8,0},{10,2},{12,4},{14,6},{16,24},{18,... | collective-permute-start | bytes 1179656 | tf_op jit(solution)/shard_map/ppermute | solution.py:478
  75.2 7.8 %collective-permute-start.15 = (f32[384,256]{1,0:T(8,128)S(1)}, f32[384,256]{1,0:T(8,128)S(1)}, u32[]{:S(2)}, u32[]{:S(2)}) collective-permute-start(f32[384,256]{1,0:T(8,128)S(1)} %pad_maximum_fusion.4), channel_id=1, source_target_pairs={{0,4},{2,6},{4,0},{6,2},{8,12},{10,14},{12,8},{14,10},{16,20},{18,... | collective-permute-start | bytes 1179656 | tf_op jit(solution)/shard_map/ppermute | solution.py:478
  76.8 7.8 %collective-permute-start.7 = (f32[384,256]{1,0:T(8,128)S(1)}, f32[384,256]{1,0:T(8,128)S(1)}, u32[]{:S(2)}, u32[]{:S(2)}) collective-permute-start(f32[384,256]{1,0:T(8,128)S(1)} %pad_maximum_fusion.3), channel_id=1, source_target_pairs={{0,2},{2,0},{4,6},{6,4},{8,10},{10,8},{12,14},{14,12},{16,18},{18,... | collective-permute-start | bytes 1179656 | tf_op jit(solution)/shard_map/ppermute | solution.py:478
  177.5 7.5 %collective-permute-start.47 = (f32[64,256]{1,0:T(8,128)S(1)}, f32[64,256]{1,0:T(8,128)S(1)}, u32[]{:S(2)}, u32[]{:S(2)}) collective-permute-start(f32[64,256]{1,0:T(8,128)S(1)} %add.242), channel_id=1, source_target_pairs={{0,16},{2,18},{4,20},{6,22},{8,24},{10,26},{12,28},{14,30},{16,0},... | collective-permute-start | bytes 196616 | tf_op jit(solution)/shard_map/ppermute | solution.py:478
  178.5 7.2 %collective-permute-start.40 = (f32[64,256]{1,0:T(8,128)S(1)}, f32[64,256]{1,0:T(8,128)S(1)}, u32[]{:S(2)}, u32[]{:S(2)}) collective-permute-start(f32[64,256]{1,0:T(8,128)S(1)} %add.233), channel_id=1, source_target_pairs={{0,16},{2,18},{4,20},{6,22},{8,24},{10,26},{12,28},{14,30},{16,0},... | collective-permute-start | bytes 196616 | tf_op jit(solution)/shard_map/ppermute | solution.py:478
  180.6 6.5 %collective-permute-start.33 = (f32[64,256]{1,0:T(8,128)S(1)}, f32[64,256]{1,0:T(8,128)S(1)}, u32[]{:S(2)}, u32[]{:S(2)}) collective-permute-start(f32[64,256]{1,0:T(8,128)S(1)} %add.224), channel_id=1, source_target_pairs={{0,16},{2,18},{4,20},{6,22},{8,24},{10,26},{12,28},{14,30},{16,0},... | collective-permute-start | bytes 196616 | tf_op jit(solution)/shard_map/ppermute | solution.py:478
  (33 other events, 126.3 us)

commit v8 on v6

--- a/solution.py
+++ b/solution.py
@@ -38,8 +38,13 @@
     lane = lax.broadcasted_iota(jnp.int32, (8, 128), 1)
     sub = lax.broadcasted_iota(jnp.int32, (8, 128), 0)
     rows = list(groups)
+    wide_strip = 4
+    ups, boths = [], []
     for k in range(count):
         base = 8 * k
+        first = k - k % wide_strip
+        end = min(first + wide_strip, count)
+        block = (lane >= 8 * first) & (lane < 8 * end)
         strip = rows[k]
         inside = (lane >= base) & (lane < base + 8)
         eye = jnp.where(lane == base + sub, 1.0, 0.0).astype(F32)
@@ -73,12 +78,11 @@
         for j in range(1, 8):
             out_r = jnp.where(sub == j, upper[j], out_r)
             out_m = jnp.where(sub == j, both[j], out_m)
-        emit(
-            k,
-            jnp.where(lane >= base + sub, out_r, 0.0),
-            jnp.where(lane <= base + sub, out_m, 0.0),
-        )
-        for g in range(k + 1, count):
+        up = jnp.where(lane >= base + sub, out_r, 0.0)
+        emit(k, up, jnp.where(lane <= base + sub, out_m, 0.0))
+        ups.append(up)
+        boths.append(jnp.where(block & (lane > base + sub), 0.0, out_m))
+        for g in range(k + 1, end):
             w = rows[g]
             new = jnp.where(inside, 0.0, w)
             left = []
@@ -90,6 +94,11 @@
                 left.append(c)
                 new = new - c * both[j]
             rows[g] = new
+        if k + 1 == end and end < count:
+            take = full(jnp.concatenate(ups, axis=0).T, jnp.concatenate(boths, axis=0))
+            for g in range(end, count):
+                rows[g] = jnp.where(block, 0.0, rows[g]) - take[8 * g:8 * g + 8]
+            ups, boths = [], []
 
 
 def factor(r_ref, m_ref):
@@ -426,16 +435,19 @@
     turn, last = bits[:-1], bits[-1:]
     orders = [turn[n % len(turn):] + turn[:n % len(turn)] + last for n in range(len(sends))]
     me = lax.axis_index("rows")
-    parts = [keep + exchange(send, "grp", 0) for send, keep in zip(sends, keeps)]
+    terms = [[keep, exchange(send, "grp", 0)] for send, keep in zip(sends, keeps)]
     halving = len(bits) - tail
     for step in range(halving):
         for n, order in enumerate(orders):
-            x, bit = parts[n], order[step]
-            half = x.shape[0] // 2
+            bit = order[step]
+            half = terms[n][0].shape[0] // 2
             mine = (me >> bit) & 1
-            send = lax.dynamic_slice_in_dim(x, (1 - mine) * half, half, 0)
-            keep = lax.dynamic_slice_in_dim(x, mine * half, half, 0)
-            parts[n] = keep + exchange(send, "rows", bit)
+            send, keep = (
+                sum(lax.dynamic_slice_in_dim(x, at * half, half, 0) for x in terms[n])
+                for at in (1 - mine, mine)
+            )
+            terms[n] = [keep, exchange(send, "rows", bit)]
+    parts = [a + b for a, b in terms]
     for step in range(halving, len(bits)):
         for n, order in enumerate(orders):
             parts[n] = parts[n] + exchange(parts[n], "rows", order[step])

time: 213 us -> 214 us (level)
  other arithmetic: 5.07 us -> 7.49 us
    add x21, other arithmetic: 4.15 us -> 6.57 us  [the longest x15 6.48 us: summed(): sum((lax.dynamic_slice_in_dim(x, at * half, half, 0) for x in terms[n]))]
  transfers between devices with their start and end apart: 53 -> 53, of which waited for: 40 -> 39; matrix products, arithmetic and copies ran while one was open for 3% -> 3% of each run, Pallas kernels for 0% -> 0%
where the time goes in v8:
time: 214 us; the launch traced here: 213 us
  Pallas kernels  73.2 us (34%)
  waiting for transfers between devices  61.4 us (29%)
  starting transfers between devices  42.3 us (20%)
  blocking collectives  27.6 us (13%)
  other arithmetic  7.49 us (4%)
    pallas_call x4, Pallas kernels, call(): pl.pallas_call(kernel, grid=(n // tile,) if grid is None else grid, in_sp...  73.2 us
    ppermute x53, waiting for transfers between devices, exchange(): return lax.ppermute(x, axis, [(i, i ^ 1 << bit) for i in range(size)])  61.4 us
    ppermute x53, starting transfers between devices, exchange(): return lax.ppermute(x, axis, [(i, i ^ 1 << bit) for i in range(size)])  42.3 us
    all_to_all x1, blocking collectives, summed_at_once(): got = lax.all_to_all(x, 'rows', 0, 0, tiled=True)  14.9 us
    all_to_all x1, blocking collectives, summed_at_once(): x = lax.all_to_all(same, 'rows', 0, 0, tiled=True)  12.8 us
    add x15, other arithmetic, summed(): sum((lax.dynamic_slice_in_dim(x, at * half, half, 0) for x in terms[n]))  6.48 us
  transfers between devices with their start and end apart: 53, of which 39 were waited for; matrix products, arithmetic and copies ran while one was open for 3% of the time, Pallas kernels for 0%

profile of v8, /device:TPU:0, one launch (start us, length us, event | category | flops | bytes accessed | tf_op | source)
XLA Modules:
  0.0 213.3 jit_solution(3398181786340774097)
XLA Ops:
  0.6 14.5 %cross.1 = (f32[768,256]{1,0:T(8,128)S(1)}, f32[768,256]{1,0:T(8,128)}, f32[768,256]{1,0:T(8,128)}, f32[768,256]{1,0:T(8,128)S(1)}, f32[768,256]{1,0:T(8,128)S(1)}, /*index=5*/f32[768,256]{1,0:T(8,128)S(1)}) custom-call(s32[1]{0:T(128)} %bitcast.r_0_, bf16[4096,1024]{1,0:T(8,128)(2,1)} %r_6_.1, bf16[4096,512]{1,0:T(8,128)(2,1)} %r_8_.1), custom_call_target="tpu_custom_call" | custom-call | flops 9663676416 | bytes 12582912 | tf_op jit(solution)/shard_map/cross/pallas_call | solution.py:512
  16.1 1.7 collective-permute-done.16
  17.8 2.0 dynamic-slice_add_fusion.1
  19.8 2.9 %collective-permute-start.17 = (f32[384,256]{1,0:T(8,128)}, f32[384,256]{1,0:T(8,128)}, u32[]{:S(2)}, u32[]{:S(2)}) collective-permute-start(f32[384,256]{1,0:T(8,128)} %get-tuple-element.50), channel_id=1, source_target_pairs={{0,8},{2,10},{4,12},{6,14},{8,0},{10,2},{12,4},{14,6},{16,24},{18,... | collective-permute-start | bytes 1179656 | tf_op jit(solution)/shard_map/ppermute | solution.py:430
  22.7 2.0 dynamic-slice_add_fusion.3
  29.0 3.5 %collective-permute-done.17 = f32[384,256]{1,0:T(8,128)} collective-permute-done((f32[384,256]{1,0:T(8,128)}, f32[384,256]{1,0:T(8,128)}, u32[]{:S(2)}, u32[]{:S(2)}) %collective-permute-start.17) | collective-permute-done | bytes 393248 | tf_op jit(solution)/shard_map/ppermute | solution.py:430
  36.9 2.6 %collective-permute-done.1 = f32[384,256]{1,0:T(8,128)S(1)} collective-permute-done((f32[384,256]{1,0:T(8,128)S(1)}, f32[384,256]{1,0:T(8,128)S(1)}, u32[]{:S(2)}, u32[]{:S(2)}) %collective-permute-start.1) | collective-permute-done | bytes 393248 | tf_op jit(solution)/shard_map/ppermute | solution.py:430
  40.1 2.2 %collective-permute-done.18 = f32[192,256]{1,0:T(8,128)S(1)} collective-permute-done((f32[192,256]{1,0:T(8,128)S(1)}, f32[192,256]{1,0:T(8,128)S(1)}, u32[]{:S(2)}, u32[]{:S(2)}) %collective-permute-start.18) | collective-permute-done | bytes 196640 | tf_op jit(solution)/shard_map/ppermute | solution.py:430
  44.5 1.9 collective-permute-done.2
  47.4 2.7 %collective-permute-start.20 = (f32[96,256]{1,0:T(8,128)S(1)}, f32[96,256]{1,0:T(8,128)S(1)}, u32[]{:S(2)}, u32[]{:S(2)}) collective-permute-start(f32[96,256]{1,0:T(8,128)S(1)} %add_add_fusion), channel_id=1, source_target_pairs={{0,16},{2,18},{4,20},{6,22},{8,24},{10,26},{12,28},{14,30},{16,0},... | collective-permute-start | bytes 294920 | tf_op jit(solution)/shard_map/ppermute | solution.py:430
  52.1 2.6 %collective-permute-start.4 = (f32[96,256]{1,0:T(8,128)S(1)}, f32[96,256]{1,0:T(8,128)S(1)}, u32[]{:S(2)}, u32[]{:S(2)}) collective-permute-start(f32[96,256]{1,0:T(8,128)S(1)} %add_add_fusion.2), channel_id=1, source_target_pairs={{0,16},{2,18},{4,20},{6,22},{8,24},{10,26},{12,28},{14,30},{16,0},... | collective-permute-start | bytes 294920 | tf_op jit(solution)/shard_map/ppermute | solution.py:430
  54.8 4.5 %collective-permute-done.20 = f32[96,256]{1,0:T(8,128)S(1)} collective-permute-done((f32[96,256]{1,0:T(8,128)S(1)}, f32[96,256]{1,0:T(8,128)S(1)}, u32[]{:S(2)}, u32[]{:S(2)}) %collective-permute-start.20) | collective-permute-done | bytes 98336 | tf_op jit(solution)/shard_map/ppermute | solution.py:430
  70.8 4.0 %collective-permute-done.14 = f32[192,256]{1,0:T(8,128)S(1)} collective-permute-done((f32[192,256]{1,0:T(8,128)S(1)}, f32[192,256]{1,0:T(8,128)S(1)}, u32[]{:S(2)}, u32[]{:S(2)}) %collective-permute-start.14) | collective-permute-done | bytes 196640 | tf_op jit(solution)/shard_map/ppermute | solution.py:430
  77.4 3.1 %collective-permute-done.23 = f32[384,256]{1,0:T(8,128)S(1)} collective-permute-done((f32[384,256]{1,0:T(8,128)S(1)}, f32[384,256]{1,0:T(8,128)S(1)}, u32[]{:S(2)}, u32[]{:S(2)}) %collective-permute-start.23) | collective-permute-done | bytes 393248 | tf_op jit(solution)/shard_map/ppermute | solution.py:430
  80.7 2.0 collective-permute-done.15
  86.7 18.1 %first.1 = (f32[4096,256]{1,0:T(8,128)}, bf16[4096,512]{1,0:T(8,128)(2,1)}, f32[1024,256]{1,0:T(8,128)}, f32[1024,256]{1,0:T(8,128)}, f32[256,256]{1,0:T(8,128)S...) custom-call(s32[1]{0:T(128)} %bitcast.r_0_, f32[768,256]{1,0:T(8,128)S(1)} %pad_maximum_fusion.r_1_, ...), custom_call_target="tpu_custom_call" | custom-call | flops 11811160064 | bytes 20971520 | tf_op jit(solution)/shard_map/first/pallas_call | solution.py:512
  106.4 14.9 %all_to_all.17 = f32[16,16,256]{2,1,0:T(8,128)S(1)} all-to-all(f32[16,16,256]{2,1,0:T(8,128)S(1)} %bitcast.5), channel_id=1, replica_groups=mesh['rows'=16,'grp'=2] {'rows'}, dimensions={0} | all-to-all | bytes 524288 | tf_op jit(solution)/shard_map/all_to_all | solution.py:466
  121.3 12.8 %all_to_all.18 = f32[16,16,256]{2,1,0:T(8,128)S(1)} all-to-all(f32[16,16,256]{2,1,0:T(8,128)S(1)} %broadcast_in_dim.2), channel_id=1, replica_groups=mesh['rows'=16,'grp'=2] {'rows'}, dimensions={0} | all-to-all | bytes 524288 | tf_op jit(solution)/shard_map/all_to_all | solution.py:469
  135.6 24.9 %second.1 = (bf16[4096,256]{1,0:T(8,128)(2,1)}, bf16[4096,512]{1,0:T(8,128)(2,1)}, f32[256,256]{1,0:T(8,128)S(1)}, f32[256,256]{1,0:T(8,128)S(1)}, f32[256,256]{...) custom-call(s32[1]{0:T(128)} %bitcast.r_0_, ...), custom_call_target="tpu_custom_call" | custom-call | flops 10200547328 | bytes 27262976 | tf_op jit(solution)/shard_map/second/pallas_call | solution.py:512
  164.9 2.9 %collective-permute-done.44 = f32[128,256]{1,0:T(8,128)S(1)} collective-permute-done((f32[128,256]{1,0:T(8,128)S(1)}, f32[128,256]{1,0:T(8,128)S(1)}, u32[]{:S(2)}, u32[]{:S(2)}) %collective-permute-start.44) | collective-permute-done | bytes 131104 | tf_op jit(solution)/shard_map/ppermute | solution.py:430
  177.5 2.1 collective-permute-start.40
  180.6 3.5 %collective-permute-done.47 = f32[64,256]{1,0:T(8,128)S(1)} collective-permute-done((f32[64,256]{1,0:T(8,128)S(1)}, f32[64,256]{1,0:T(8,128)S(1)}, u32[]{:S(2)}, u32[]{:S(2)}) %collective-permute-start.47) | collective-permute-done | bytes 65568 | tf_op jit(solution)/shard_map/ppermute | solution.py:430
  191.7 1.8 collective-permute-done.49
  197.3 15.8 %last.1 = (bf16[4096,512]{1,0:T(8,128)(2,1)}, f32[2,256,256]{2,1,0:T(8,128)}, f32[512,512]{1,0:T(8,128)}) custom-call(s32[1]{0:T(128)} %bitcast.r_0_, f32[256,256]{1,0:T(8,128)S(1)} %pad_maximum_fusion.6.r_1_, f32[256,256]{1,0:T(8,128)S(1)} %pad_maximum_fusion.7.r_2_, f32[256,256]{1,0:T(8,128)S(1)} %pad_maximum_fusion.8.r_3_, ...), custom_call_target="tpu_custom_call" | custom-call | flops 2147483648 | bytes 10485760 | tf_op jit(solution)/shard_map/last/pallas_call | solution.py:512
  (155 shorter events, 63.1 us)
Async XLA Ops:
  15.5 7.2 %collective-permute-start.8 = (f32[768,256]{1,0:T(8,128)}, f32[768,256]{1,0:T(8,128)}, u32[]{:S(2)}, u32[]{:S(2)}) collective-permute-start(f32[768,256]{1,0:T(8,128)} %get-tuple-element.29), channel_id=1, source_target_pairs={{0,1},{1,0},{2,3},{3,2},{4,5},{5,4},{6,7},{7,6},{8,9},{9,8},{10,11... | collective-permute-start | bytes 2359304 | tf_op jit(solution)/shard_map/ppermute | solution.py:430
  15.6 10.6 %collective-permute-start = (f32[768,256]{1,0:T(8,128)S(1)}, f32[768,256]{1,0:T(8,128)}, u32[]{:S(2)}, u32[]{:S(2)}) collective-permute-start(f32[768,256]{1,0:T(8,128)S(1)} %get-tuple-element.27), channel_id=1, source_target_pairs={{0,1},{1,0},{2,3},{3,2},{4,5},{5,4},{6,7},{7,6},{8,9},{9,8},{10,11... | collective-permute-start | bytes 2359304 | tf_op jit(solution)/shard_map/ppermute | solution.py:430
  19.8 12.7 %collective-permute-start.17 = (f32[384,256]{1,0:T(8,128)}, f32[384,256]{1,0:T(8,128)}, u32[]{:S(2)}, u32[]{:S(2)}) collective-permute-start(f32[384,256]{1,0:T(8,128)} %get-tuple-element.50), channel_id=1, source_target_pairs={{0,8},{2,10},{4,12},{6,14},{8,0},{10,2},{12,4},{14,6},{16,24},{18,... | collective-permute-start | bytes 1179656 | tf_op jit(solution)/shard_map/ppermute | solution.py:430
  24.7 11.1 %collective-permute-start.9 = (f32[384,256]{1,0:T(8,128)}, f32[384,256]{1,0:T(8,128)S(1)}, u32[]{:S(2)}, u32[]{:S(2)}) collective-permute-start(f32[384,256]{1,0:T(8,128)} %get-tuple-element.52), channel_id=1, source_target_pairs={{0,4},{2,6},{4,0},{6,2},{8,12},{10,14},{12,8},{14,10},{16,20},{18,... | collective-permute-start | bytes 1179656 | tf_op jit(solution)/shard_map/ppermute | solution.py:430
  27.4 12.1 %collective-permute-start.1 = (f32[384,256]{1,0:T(8,128)S(1)}, f32[384,256]{1,0:T(8,128)S(1)}, u32[]{:S(2)}, u32[]{:S(2)}) collective-permute-start(f32[384,256]{1,0:T(8,128)S(1)} %get-tuple-element.54), channel_id=1, source_target_pairs={{0,2},{2,0},{4,6},{6,4},{8,10},{10,8},{12,14},{14,12},{16,18},{18,... | collective-permute-start | bytes 1179656 | tf_op jit(solution)/shard_map/ppermute | solution.py:430
  33.5 8.8 %collective-permute-start.18 = (f32[192,256]{1,0:T(8,128)S(1)}, f32[192,256]{1,0:T(8,128)S(1)}, u32[]{:S(2)}, u32[]{:S(2)}) collective-permute-start(f32[192,256]{1,0:T(8,128)S(1)} %get-tuple-element.58), channel_id=1, source_target_pairs={{0,2},{2,0},{4,6},{6,4},{8,10},{10,8},{12,14},{14,12},{16,18},{18,... | collective-permute-start | bytes 589832 | tf_op jit(solution)/shard_map/ppermute | solution.py:430
  35.8 7.1 %collective-permute-start.10 = (f32[192,256]{1,0:T(8,128)S(1)}, f32[192,256]{1,0:T(8,128)S(1)}, u32[]{:S(2)}, u32[]{:S(2)}) collective-permute-start(f32[192,256]{1,0:T(8,128)S(1)} %get-tuple-element.62), channel_id=1, source_target_pairs={{0,8},{2,10},{4,12},{6,14},{8,0},{10,2},{12,4},{14,6},{16,24},{18,... | collective-permute-start | bytes 589832 | tf_op jit(solution)/shard_map/ppermute | solution.py:430
  39.6 6.8 %collective-permute-start.2 = (f32[192,256]{1,0:T(8,128)S(1)}, f32[192,256]{1,0:T(8,128)S(1)}, u32[]{:S(2)}, u32[]{:S(2)}) collective-permute-start(f32[192,256]{1,0:T(8,128)S(1)} %get-tuple-element.66), channel_id=1, source_target_pairs={{0,4},{2,6},{4,0},{6,2},{8,12},{10,14},{12,8},{14,10},{16,20},{18,... | collective-permute-start | bytes 589832 | tf_op jit(solution)/shard_map/ppermute | solution.py:430
  42.9 7.2 %collective-permute-start.11 = (f32[96,256]{1,0:T(8,128)S(1)}, f32[96,256]{1,0:T(8,128)S(1)}, u32[]{:S(2)}, u32[]{:S(2)}) collective-permute-start(f32[96,256]{1,0:T(8,128)S(1)} %dynamic-slice_add_fusion.19), channel_id=1, source_target_pairs={{0,2},{2,0},{4,6},{6,4},{8,10},{10,8},{12,14},{14,12},{16,18},{18,... | collective-permute-start | bytes 294920 | tf_op jit(solution)/shard_map/ppermute | solution.py:430
  46.4 5.7 %collective-permute-start.3 = (f32[96,256]{1,0:T(8,128)S(1)}, f32[96,256]{1,0:T(8,128)S(1)}, u32[]{:S(2)}, u32[]{:S(2)}) collective-permute-start(f32[96,256]{1,0:T(8,128)S(1)} %dynamic-slice_add_fusion.20), channel_id=1, source_target_pairs={{0,8},{2,10},{4,12},{6,14},{8,0},{10,2},{12,4},{14,6},{16,24},{18,... | collective-permute-start | bytes 294920 | tf_op jit(solution)/shard_map/ppermute | solution.py:430
  47.4 11.9 %collective-permute-start.20 = (f32[96,256]{1,0:T(8,128)S(1)}, f32[96,256]{1,0:T(8,128)S(1)}, u32[]{:S(2)}, u32[]{:S(2)}) collective-permute-start(f32[96,256]{1,0:T(8,128)S(1)} %add_add_fusion), channel_id=1, source_target_pairs={{0,16},{2,18},{4,20},{6,22},{8,24},{10,26},{12,28},{14,30},{16,0},... | collective-permute-start | bytes 294920 | tf_op jit(solution)/shard_map/ppermute | solution.py:430
  50.1 11.1 %collective-permute-start.12 = (f32[96,256]{1,0:T(8,128)S(1)}, f32[96,256]{1,0:T(8,128)S(1)}, u32[]{:S(2)}, u32[]{:S(2)}) collective-permute-start(f32[96,256]{1,0:T(8,128)S(1)} %add_add_fusion.1), channel_id=1, source_target_pairs={{0,16},{2,18},{4,20},{6,22},{8,24},{10,26},{12,28},{14,30},{16,0},... | collective-permute-start | bytes 294920 | tf_op jit(solution)/shard_map/ppermute | solution.py:430
  52.1 10.7 %collective-permute-start.4 = (f32[96,256]{1,0:T(8,128)S(1)}, f32[96,256]{1,0:T(8,128)S(1)}, u32[]{:S(2)}, u32[]{:S(2)}) collective-permute-start(f32[96,256]{1,0:T(8,128)S(1)} %add_add_fusion.2), channel_id=1, source_target_pairs={{0,16},{2,18},{4,20},{6,22},{8,24},{10,26},{12,28},{14,30},{16,0},... | collective-permute-start | bytes 294920 | tf_op jit(solution)/shard_map/ppermute | solution.py:430
  61.2 5.7 %collective-permute-start.13 = (f32[96,256]{1,0:T(8,128)S(1)}, f32[96,256]{1,0:T(8,128)S(1)}, u32[]{:S(2)}, u32[]{:S(2)}) collective-permute-start(f32[96,256]{1,0:T(8,128)S(1)} %add.285), channel_id=1, source_target_pairs={{0,2},{2,0},{4,6},{6,4},{8,10},{10,8},{12,14},{14,12},{16,18},{18,... | collective-permute-start | bytes 294920 | tf_op jit(solution)/shard_map/ppermute | solution.py:430
  62.8 5.6 %collective-permute-start.5 = (f32[96,256]{1,0:T(8,128)S(1)}, f32[96,256]{1,0:T(8,128)S(1)}, u32[]{:S(2)}, u32[]{:S(2)}) collective-permute-start(f32[96,256]{1,0:T(8,128)S(1)} %add.271), channel_id=1, source_target_pairs={{0,8},{2,10},{4,12},{6,14},{8,0},{10,2},{12,4},{14,6},{16,24},{18,... | collective-permute-start | bytes 294920 | tf_op jit(solution)/shard_map/ppermute | solution.py:430
  64.1 5.7 %collective-permute-start.22 = (f32[192,256]{1,0:T(8,128)S(1)}, f32[192,256]{1,0:T(8,128)S(1)}, u32[]{:S(2)}, u32[]{:S(2)}) collective-permute-start(f32[192,256]{1,0:T(8,128)S(1)} %pad_maximum_fusion.11), channel_id=1, source_target_pairs={{0,2},{2,0},{4,6},{6,4},{8,10},{10,8},{12,14},{14,12},{16,18},{18,... | collective-permute-start | bytes 589832 | tf_op jit(solution)/shard_map/ppermute | solution.py:430
  67.0 7.8 %collective-permute-start.14 = (f32[192,256]{1,0:T(8,128)S(1)}, f32[192,256]{1,0:T(8,128)S(1)}, u32[]{:S(2)}, u32[]{:S(2)}) collective-permute-start(f32[192,256]{1,0:T(8,128)S(1)} %pad_maximum_fusion.10), channel_id=1, source_target_pairs={{0,8},{2,10},{4,12},{6,14},{8,0},{10,2},{12,4},{14,6},{16,24},{18,... | collective-permute-start | bytes 589832 | tf_op jit(solution)/shard_map/ppermute | solution.py:430
  68.5 7.8 %collective-permute-start.6 = (f32[192,256]{1,0:T(8,128)S(1)}, f32[192,256]{1,0:T(8,128)S(1)}, u32[]{:S(2)}, u32[]{:S(2)}) collective-permute-start(f32[192,256]{1,0:T(8,128)S(1)} %pad_maximum_fusion.9), channel_id=1, source_target_pairs={{0,4},{2,6},{4,0},{6,2},{8,12},{10,14},{12,8},{14,10},{16,20},{18,... | collective-permute-start | bytes 589832 | tf_op jit(solution)/shard_map/ppermute | solution.py:430
  69.9 10.6 %collective-permute-start.23 = (f32[384,256]{1,0:T(8,128)S(1)}, f32[384,256]{1,0:T(8,128)S(1)}, u32[]{:S(2)}, u32[]{:S(2)}) collective-permute-start(f32[384,256]{1,0:T(8,128)S(1)} %pad_maximum_fusion.5), channel_id=1, source_target_pairs={{0,8},{2,10},{4,12},{6,14},{8,0},{10,2},{12,4},{14,6},{16,24},{18,... | collective-permute-start | bytes 1179656 | tf_op jit(solution)/shard_map/ppermute | solution.py:430
  74.9 7.8 %collective-permute-start.15 = (f32[384,256]{1,0:T(8,128)S(1)}, f32[384,256]{1,0:T(8,128)S(1)}, u32[]{:S(2)}, u32[]{:S(2)}) collective-permute-start(f32[384,256]{1,0:T(8,128)S(1)} %pad_maximum_fusion.4), channel_id=1, source_target_pairs={{0,4},{2,6},{4,0},{6,2},{8,12},{10,14},{12,8},{14,10},{16,20},{18,... | collective-permute-start | bytes 1179656 | tf_op jit(solution)/shard_map/ppermute | solution.py:430
  76.4 7.8 %collective-permute-start.7 = (f32[384,256]{1,0:T(8,128)S(1)}, f32[384,256]{1,0:T(8,128)S(1)}, u32[]{:S(2)}, u32[]{:S(2)}) collective-permute-start(f32[384,256]{1,0:T(8,128)S(1)} %pad_maximum_fusion.3), channel_id=1, source_target_pairs={{0,2},{2,0},{4,6},{6,4},{8,10},{10,8},{12,14},{14,12},{16,18},{18,... | collective-permute-start | bytes 1179656 | tf_op jit(solution)/shard_map/ppermute | solution.py:430
  176.5 7.6 %collective-permute-start.47 = (f32[64,256]{1,0:T(8,128)S(1)}, f32[64,256]{1,0:T(8,128)S(1)}, u32[]{:S(2)}, u32[]{:S(2)}) collective-permute-start(f32[64,256]{1,0:T(8,128)S(1)} %add.332), channel_id=1, source_target_pairs={{0,16},{2,18},{4,20},{6,22},{8,24},{10,26},{12,28},{14,30},{16,0},... | collective-permute-start | bytes 196616 | tf_op jit(solution)/shard_map/ppermute | solution.py:430
  177.5 7.6 %collective-permute-start.40 = (f32[64,256]{1,0:T(8,128)S(1)}, f32[64,256]{1,0:T(8,128)S(1)}, u32[]{:S(2)}, u32[]{:S(2)}) collective-permute-start(f32[64,256]{1,0:T(8,128)S(1)} %add.321), channel_id=1, source_target_pairs={{0,16},{2,18},{4,20},{6,22},{8,24},{10,26},{12,28},{14,30},{16,0},... | collective-permute-start | bytes 196616 | tf_op jit(solution)/shard_map/ppermute | solution.py:430
  179.6 6.6 %collective-permute-start.33 = (f32[64,256]{1,0:T(8,128)S(1)}, f32[64,256]{1,0:T(8,128)S(1)}, u32[]{:S(2)}, u32[]{:S(2)}) collective-permute-start(f32[64,256]{1,0:T(8,128)S(1)} %add.310), channel_id=1, source_target_pairs={{0,16},{2,18},{4,20},{6,22},{8,24},{10,26},{12,28},{14,30},{16,0},... | collective-permute-start | bytes 196616 | tf_op jit(solution)/shard_map/ppermute | solution.py:430
  (31 other events, 112.6 us)

commit v9 on v8

--- a/solution.py
+++ b/solution.py
@@ -38,7 +38,7 @@
     lane = lax.broadcasted_iota(jnp.int32, (8, 128), 1)
     sub = lax.broadcasted_iota(jnp.int32, (8, 128), 0)
     rows = list(groups)
-    wide_strip = 4
+    wide_strip = 8
     ups, boths = [], []
     for k in range(count):
         base = 8 * k
@@ -247,8 +247,9 @@
             h_ref[...] = against
         else:
             z_ref[...] = after
-            high, low = split(against.T)
-            t_ref[...] = dot(high, b) + dot(low, b)
+            high, low = split(against)
+            bt = b.T
+            t_ref[...] = (dot(bt, high) + dot(bt, low)).T
     begin(small, small_sems)
 
     for i in range(tiles):
@@ -323,14 +324,15 @@
     finish(small, small_sems)
     inv_s = split(inv)
     against = split(h_ref[...])
-    at = split(h_ref[...].T)
     turned = split(dot(high, d_b) + dot(low, d_b))
     upper = (z_ref[...] - thrice(against, turned)).astype(BF16)
     ub[...] = upper
     lower = (d - wide(d_b)) - thrice(inv_s, split(t_ref[...]))
     lower_b = lower.astype(BF16)
     lb[...] = lower_b
-    x_ref[...] = (lower - wide(lower_b)) - thrice(inv_s, split(dot(at[0], upper) + dot(at[1], upper)))
+    upt = upper.T
+    both = (dot(upt, against[0]) + dot(upt, against[1])).T
+    x_ref[...] = (lower - wide(lower_b)) - thrice(inv_s, split(both))
 
     for i in range(tiles):
         finish(at_tile(inputs, i, tile), in_sems.at[i])

time: 214 us -> 213 us (level)
  no operation moved by 1% of the time
where the time goes in v9:
time: 213 us
  Pallas kernels  72.7 us (34%)
  waiting for transfers between devices  61.4 us (29%)
  starting transfers between devices  42.3 us (20%)
  blocking collectives  27.6 us (13%)
  other arithmetic  7.49 us (4%)
    pallas_call x4, Pallas kernels, call(): pl.pallas_call(kernel, grid=(n // tile,) if grid is None else grid, in_sp...  72.7 us
    ppermute x53, waiting for transfers between devices, exchange(): return lax.ppermute(x, axis, [(i, i ^ 1 << bit) for i in range(size)])  61.4 us
    ppermute x53, starting transfers between devices, exchange(): return lax.ppermute(x, axis, [(i, i ^ 1 << bit) for i in range(size)])  42.3 us
    all_to_all x1, blocking collectives, summed_at_once(): got = lax.all_to_all(x, 'rows', 0, 0, tiled=True)  14.9 us
    all_to_all x1, blocking collectives, summed_at_once(): x = lax.all_to_all(same, 'rows', 0, 0, tiled=True)  12.8 us
    add x15, other arithmetic, summed(): sum((lax.dynamic_slice_in_dim(x, at * half, half, 0) for x in terms[n]))  6.48 us
  transfers between devices with their start and end apart: 53, of which 39 were waited for; matrix products, arithmetic and copies ran while one was open for 3% of the time, Pallas kernels for 0%

profile of v9, /device:TPU:0, one launch (start us, length us, event | category | flops | bytes accessed | tf_op | source)
XLA Modules:
  0.0 212.7 jit_solution(12731353910298617780)
XLA Ops:
  0.6 14.5 %cross.1 = (f32[768,256]{1,0:T(8,128)S(1)}, f32[768,256]{1,0:T(8,128)}, f32[768,256]{1,0:T(8,128)}, f32[768,256]{1,0:T(8,128)S(1)}, f32[768,256]{1,0:T(8,128)S(1)}, /*index=5*/f32[768,256]{1,0:T(8,128)S(1)}) custom-call(s32[1]{0:T(128)} %bitcast.r_0_, bf16[4096,1024]{1,0:T(8,128)(2,1)} %r_6_.1, bf16[4096,512]{1,0:T(8,128)(2,1)} %r_8_.1), custom_call_target="tpu_custom_call" | custom-call | flops 9663676416 | bytes 12582912 | tf_op jit(solution)/shard_map/cross/pallas_call | solution.py:514
  16.1 1.7 collective-permute-done.16
  17.8 2.0 dynamic-slice_add_fusion.1
  19.8 2.9 %collective-permute-start.17 = (f32[384,256]{1,0:T(8,128)}, f32[384,256]{1,0:T(8,128)}, u32[]{:S(2)}, u32[]{:S(2)}) collective-permute-start(f32[384,256]{1,0:T(8,128)} %get-tuple-element.50), channel_id=1, source_target_pairs={{0,8},{2,10},{4,12},{6,14},{8,0},{10,2},{12,4},{14,6},{16,24},{18,... | collective-permute-start | bytes 1179656 | tf_op jit(solution)/shard_map/ppermute | solution.py:432
  22.7 2.0 dynamic-slice_add_fusion.3
  29.0 3.5 %collective-permute-done.17 = f32[384,256]{1,0:T(8,128)} collective-permute-done((f32[384,256]{1,0:T(8,128)}, f32[384,256]{1,0:T(8,128)}, u32[]{:S(2)}, u32[]{:S(2)}) %collective-permute-start.17) | collective-permute-done | bytes 393248 | tf_op jit(solution)/shard_map/ppermute | solution.py:432
  36.9 2.6 %collective-permute-done.1 = f32[384,256]{1,0:T(8,128)S(1)} collective-permute-done((f32[384,256]{1,0:T(8,128)S(1)}, f32[384,256]{1,0:T(8,128)S(1)}, u32[]{:S(2)}, u32[]{:S(2)}) %collective-permute-start.1) | collective-permute-done | bytes 393248 | tf_op jit(solution)/shard_map/ppermute | solution.py:432
  40.1 2.2 %collective-permute-done.18 = f32[192,256]{1,0:T(8,128)S(1)} collective-permute-done((f32[192,256]{1,0:T(8,128)S(1)}, f32[192,256]{1,0:T(8,128)S(1)}, u32[]{:S(2)}, u32[]{:S(2)}) %collective-permute-start.18) | collective-permute-done | bytes 196640 | tf_op jit(solution)/shard_map/ppermute | solution.py:432
  44.5 1.9 collective-permute-done.2
  47.4 2.7 %collective-permute-start.20 = (f32[96,256]{1,0:T(8,128)S(1)}, f32[96,256]{1,0:T(8,128)S(1)}, u32[]{:S(2)}, u32[]{:S(2)}) collective-permute-start(f32[96,256]{1,0:T(8,128)S(1)} %add_add_fusion), channel_id=1, source_target_pairs={{0,16},{2,18},{4,20},{6,22},{8,24},{10,26},{12,28},{14,30},{16,0},... | collective-permute-start | bytes 294920 | tf_op jit(solution)/shard_map/ppermute | solution.py:432
  52.1 2.6 %collective-permute-start.4 = (f32[96,256]{1,0:T(8,128)S(1)}, f32[96,256]{1,0:T(8,128)S(1)}, u32[]{:S(2)}, u32[]{:S(2)}) collective-permute-start(f32[96,256]{1,0:T(8,128)S(1)} %add_add_fusion.2), channel_id=1, source_target_pairs={{0,16},{2,18},{4,20},{6,22},{8,24},{10,26},{12,28},{14,30},{16,0},... | collective-permute-start | bytes 294920 | tf_op jit(solution)/shard_map/ppermute | solution.py:432
  54.8 4.5 %collective-permute-done.20 = f32[96,256]{1,0:T(8,128)S(1)} collective-permute-done((f32[96,256]{1,0:T(8,128)S(1)}, f32[96,256]{1,0:T(8,128)S(1)}, u32[]{:S(2)}, u32[]{:S(2)}) %collective-permute-start.20) | collective-permute-done | bytes 98336 | tf_op jit(solution)/shard_map/ppermute | solution.py:432
  70.8 4.0 %collective-permute-done.14 = f32[192,256]{1,0:T(8,128)S(1)} collective-permute-done((f32[192,256]{1,0:T(8,128)S(1)}, f32[192,256]{1,0:T(8,128)S(1)}, u32[]{:S(2)}, u32[]{:S(2)}) %collective-permute-start.14) | collective-permute-done | bytes 196640 | tf_op jit(solution)/shard_map/ppermute | solution.py:432
  77.4 3.1 %collective-permute-done.23 = f32[384,256]{1,0:T(8,128)S(1)} collective-permute-done((f32[384,256]{1,0:T(8,128)S(1)}, f32[384,256]{1,0:T(8,128)S(1)}, u32[]{:S(2)}, u32[]{:S(2)}) %collective-permute-start.23) | collective-permute-done | bytes 393248 | tf_op jit(solution)/shard_map/ppermute | solution.py:432
  80.7 2.0 collective-permute-done.15
  86.7 18.1 %first.1 = (f32[4096,256]{1,0:T(8,128)}, bf16[4096,512]{1,0:T(8,128)(2,1)}, f32[1024,256]{1,0:T(8,128)}, f32[1024,256]{1,0:T(8,128)}, f32[256,256]{1,0:T(8,128)S...) custom-call(s32[1]{0:T(128)} %bitcast.r_0_, f32[768,256]{1,0:T(8,128)S(1)} %pad_maximum_fusion.r_1_, ...), custom_call_target="tpu_custom_call" | custom-call | flops 11811160064 | bytes 20971520 | tf_op jit(solution)/shard_map/first/pallas_call | solution.py:514
  106.4 14.9 %all_to_all.17 = f32[16,16,256]{2,1,0:T(8,128)S(1)} all-to-all(f32[16,16,256]{2,1,0:T(8,128)S(1)} %bitcast.5), channel_id=1, replica_groups=mesh['rows'=16,'grp'=2] {'rows'}, dimensions={0} | all-to-all | bytes 524288 | tf_op jit(solution)/shard_map/all_to_all | solution.py:468
  121.3 12.8 %all_to_all.18 = f32[16,16,256]{2,1,0:T(8,128)S(1)} all-to-all(f32[16,16,256]{2,1,0:T(8,128)S(1)} %broadcast_in_dim.2), channel_id=1, replica_groups=mesh['rows'=16,'grp'=2] {'rows'}, dimensions={0} | all-to-all | bytes 524288 | tf_op jit(solution)/shard_map/all_to_all | solution.py:471
  135.6 24.7 %second.1 = (bf16[4096,256]{1,0:T(8,128)(2,1)}, bf16[4096,512]{1,0:T(8,128)(2,1)}, f32[256,256]{1,0:T(8,128)S(1)}, f32[256,256]{1,0:T(8,128)S(1)}, f32[256,256]{...) custom-call(s32[1]{0:T(128)} %bitcast.r_0_, ...), custom_call_target="tpu_custom_call" | custom-call | flops 10200547328 | bytes 27262976 | tf_op jit(solution)/shard_map/second/pallas_call | solution.py:514
  164.6 2.9 %collective-permute-done.44 = f32[128,256]{1,0:T(8,128)S(1)} collective-permute-done((f32[128,256]{1,0:T(8,128)S(1)}, f32[128,256]{1,0:T(8,128)S(1)}, u32[]{:S(2)}, u32[]{:S(2)}) %collective-permute-start.44) | collective-permute-done | bytes 131104 | tf_op jit(solution)/shard_map/ppermute | solution.py:432
  177.3 2.1 collective-permute-start.40
  180.4 3.5 %collective-permute-done.47 = f32[64,256]{1,0:T(8,128)S(1)} collective-permute-done((f32[64,256]{1,0:T(8,128)S(1)}, f32[64,256]{1,0:T(8,128)S(1)}, u32[]{:S(2)}, u32[]{:S(2)}) %collective-permute-start.47) | collective-permute-done | bytes 65568 | tf_op jit(solution)/shard_map/ppermute | solution.py:432
  191.5 1.8 collective-permute-done.49
  197.1 15.5 %last.1 = (bf16[4096,512]{1,0:T(8,128)(2,1)}, f32[2,256,256]{2,1,0:T(8,128)}, f32[512,512]{1,0:T(8,128)}) custom-call(s32[1]{0:T(128)} %bitcast.r_0_, f32[256,256]{1,0:T(8,128)S(1)} %pad_maximum_fusion.6.r_1_, f32[256,256]{1,0:T(8,128)S(1)} %pad_maximum_fusion.7.r_2_, f32[256,256]{1,0:T(8,128)S(1)} %pad_maximum_fusion.8.r_3_, ...), custom_call_target="tpu_custom_call" | custom-call | flops 2147483648 | bytes 10485760 | tf_op jit(solution)/shard_map/last/pallas_call | solution.py:514
  (155 shorter events, 63.0 us)
Async XLA Ops:
  15.5 7.2 %collective-permute-start.8 = (f32[768,256]{1,0:T(8,128)}, f32[768,256]{1,0:T(8,128)}, u32[]{:S(2)}, u32[]{:S(2)}) collective-permute-start(f32[768,256]{1,0:T(8,128)} %get-tuple-element.29), channel_id=1, source_target_pairs={{0,1},{1,0},{2,3},{3,2},{4,5},{5,4},{6,7},{7,6},{8,9},{9,8},{10,11... | collective-permute-start | bytes 2359304 | tf_op jit(solution)/shard_map/ppermute | solution.py:432
  15.6 10.6 %collective-permute-start = (f32[768,256]{1,0:T(8,128)S(1)}, f32[768,256]{1,0:T(8,128)}, u32[]{:S(2)}, u32[]{:S(2)}) collective-permute-start(f32[768,256]{1,0:T(8,128)S(1)} %get-tuple-element.27), channel_id=1, source_target_pairs={{0,1},{1,0},{2,3},{3,2},{4,5},{5,4},{6,7},{7,6},{8,9},{9,8},{10,11... | collective-permute-start | bytes 2359304 | tf_op jit(solution)/shard_map/ppermute | solution.py:432
  19.8 12.7 %collective-permute-start.17 = (f32[384,256]{1,0:T(8,128)}, f32[384,256]{1,0:T(8,128)}, u32[]{:S(2)}, u32[]{:S(2)}) collective-permute-start(f32[384,256]{1,0:T(8,128)} %get-tuple-element.50), channel_id=1, source_target_pairs={{0,8},{2,10},{4,12},{6,14},{8,0},{10,2},{12,4},{14,6},{16,24},{18,... | collective-permute-start | bytes 1179656 | tf_op jit(solution)/shard_map/ppermute | solution.py:432
  24.7 11.1 %collective-permute-start.9 = (f32[384,256]{1,0:T(8,128)}, f32[384,256]{1,0:T(8,128)S(1)}, u32[]{:S(2)}, u32[]{:S(2)}) collective-permute-start(f32[384,256]{1,0:T(8,128)} %get-tuple-element.52), channel_id=1, source_target_pairs={{0,4},{2,6},{4,0},{6,2},{8,12},{10,14},{12,8},{14,10},{16,20},{18,... | collective-permute-start | bytes 1179656 | tf_op jit(solution)/shard_map/ppermute | solution.py:432
  27.4 12.1 %collective-permute-start.1 = (f32[384,256]{1,0:T(8,128)S(1)}, f32[384,256]{1,0:T(8,128)S(1)}, u32[]{:S(2)}, u32[]{:S(2)}) collective-permute-start(f32[384,256]{1,0:T(8,128)S(1)} %get-tuple-element.54), channel_id=1, source_target_pairs={{0,2},{2,0},{4,6},{6,4},{8,10},{10,8},{12,14},{14,12},{16,18},{18,... | collective-permute-start | bytes 1179656 | tf_op jit(solution)/shard_map/ppermute | solution.py:432
  33.5 8.8 %collective-permute-start.18 = (f32[192,256]{1,0:T(8,128)S(1)}, f32[192,256]{1,0:T(8,128)S(1)}, u32[]{:S(2)}, u32[]{:S(2)}) collective-permute-start(f32[192,256]{1,0:T(8,128)S(1)} %get-tuple-element.58), channel_id=1, source_target_pairs={{0,2},{2,0},{4,6},{6,4},{8,10},{10,8},{12,14},{14,12},{16,18},{18,... | collective-permute-start | bytes 589832 | tf_op jit(solution)/shard_map/ppermute | solution.py:432
  35.8 7.1 %collective-permute-start.10 = (f32[192,256]{1,0:T(8,128)S(1)}, f32[192,256]{1,0:T(8,128)S(1)}, u32[]{:S(2)}, u32[]{:S(2)}) collective-permute-start(f32[192,256]{1,0:T(8,128)S(1)} %get-tuple-element.62), channel_id=1, source_target_pairs={{0,8},{2,10},{4,12},{6,14},{8,0},{10,2},{12,4},{14,6},{16,24},{18,... | collective-permute-start | bytes 589832 | tf_op jit(solution)/shard_map/ppermute | solution.py:432
  39.6 6.8 %collective-permute-start.2 = (f32[192,256]{1,0:T(8,128)S(1)}, f32[192,256]{1,0:T(8,128)S(1)}, u32[]{:S(2)}, u32[]{:S(2)}) collective-permute-start(f32[192,256]{1,0:T(8,128)S(1)} %get-tuple-element.66), channel_id=1, source_target_pairs={{0,4},{2,6},{4,0},{6,2},{8,12},{10,14},{12,8},{14,10},{16,20},{18,... | collective-permute-start | bytes 589832 | tf_op jit(solution)/shard_map/ppermute | solution.py:432
  42.9 7.2 %collective-permute-start.11 = (f32[96,256]{1,0:T(8,128)S(1)}, f32[96,256]{1,0:T(8,128)S(1)}, u32[]{:S(2)}, u32[]{:S(2)}) collective-permute-start(f32[96,256]{1,0:T(8,128)S(1)} %dynamic-slice_add_fusion.19), channel_id=1, source_target_pairs={{0,2},{2,0},{4,6},{6,4},{8,10},{10,8},{12,14},{14,12},{16,18},{18,... | collective-permute-start | bytes 294920 | tf_op jit(solution)/shard_map/ppermute | solution.py:432
  46.4 5.7 %collective-permute-start.3 = (f32[96,256]{1,0:T(8,128)S(1)}, f32[96,256]{1,0:T(8,128)S(1)}, u32[]{:S(2)}, u32[]{:S(2)}) collective-permute-start(f32[96,256]{1,0:T(8,128)S(1)} %dynamic-slice_add_fusion.20), channel_id=1, source_target_pairs={{0,8},{2,10},{4,12},{6,14},{8,0},{10,2},{12,4},{14,6},{16,24},{18,... | collective-permute-start | bytes 294920 | tf_op jit(solution)/shard_map/ppermute | solution.py:432
  47.4 11.9 %collective-permute-start.20 = (f32[96,256]{1,0:T(8,128)S(1)}, f32[96,256]{1,0:T(8,128)S(1)}, u32[]{:S(2)}, u32[]{:S(2)}) collective-permute-start(f32[96,256]{1,0:T(8,128)S(1)} %add_add_fusion), channel_id=1, source_target_pairs={{0,16},{2,18},{4,20},{6,22},{8,24},{10,26},{12,28},{14,30},{16,0},... | collective-permute-start | bytes 294920 | tf_op jit(solution)/shard_map/ppermute | solution.py:432
  50.1 11.1 %collective-permute-start.12 = (f32[96,256]{1,0:T(8,128)S(1)}, f32[96,256]{1,0:T(8,128)S(1)}, u32[]{:S(2)}, u32[]{:S(2)}) collective-permute-start(f32[96,256]{1,0:T(8,128)S(1)} %add_add_fusion.1), channel_id=1, source_target_pairs={{0,16},{2,18},{4,20},{6,22},{8,24},{10,26},{12,28},{14,30},{16,0},... | collective-permute-start | bytes 294920 | tf_op jit(solution)/shard_map/ppermute | solution.py:432
  52.1 10.7 %collective-permute-start.4 = (f32[96,256]{1,0:T(8,128)S(1)}, f32[96,256]{1,0:T(8,128)S(1)}, u32[]{:S(2)}, u32[]{:S(2)}) collective-permute-start(f32[96,256]{1,0:T(8,128)S(1)} %add_add_fusion.2), channel_id=1, source_target_pairs={{0,16},{2,18},{4,20},{6,22},{8,24},{10,26},{12,28},{14,30},{16,0},... | collective-permute-start | bytes 294920 | tf_op jit(solution)/shard_map/ppermute | solution.py:432
  61.2 5.7 %collective-permute-start.13 = (f32[96,256]{1,0:T(8,128)S(1)}, f32[96,256]{1,0:T(8,128)S(1)}, u32[]{:S(2)}, u32[]{:S(2)}) collective-permute-start(f32[96,256]{1,0:T(8,128)S(1)} %add.285), channel_id=1, source_target_pairs={{0,2},{2,0},{4,6},{6,4},{8,10},{10,8},{12,14},{14,12},{16,18},{18,... | collective-permute-start | bytes 294920 | tf_op jit(solution)/shard_map/ppermute | solution.py:432
  62.8 5.6 %collective-permute-start.5 = (f32[96,256]{1,0:T(8,128)S(1)}, f32[96,256]{1,0:T(8,128)S(1)}, u32[]{:S(2)}, u32[]{:S(2)}) collective-permute-start(f32[96,256]{1,0:T(8,128)S(1)} %add.271), channel_id=1, source_target_pairs={{0,8},{2,10},{4,12},{6,14},{8,0},{10,2},{12,4},{14,6},{16,24},{18,... | collective-permute-start | bytes 294920 | tf_op jit(solution)/shard_map/ppermute | solution.py:432
  64.1 5.7 %collective-permute-start.22 = (f32[192,256]{1,0:T(8,128)S(1)}, f32[192,256]{1,0:T(8,128)S(1)}, u32[]{:S(2)}, u32[]{:S(2)}) collective-permute-start(f32[192,256]{1,0:T(8,128)S(1)} %pad_maximum_fusion.11), channel_id=1, source_target_pairs={{0,2},{2,0},{4,6},{6,4},{8,10},{10,8},{12,14},{14,12},{16,18},{18,... | collective-permute-start | bytes 589832 | tf_op jit(solution)/shard_map/ppermute | solution.py:432
  67.0 7.8 %collective-permute-start.14 = (f32[192,256]{1,0:T(8,128)S(1)}, f32[192,256]{1,0:T(8,128)S(1)}, u32[]{:S(2)}, u32[]{:S(2)}) collective-permute-start(f32[192,256]{1,0:T(8,128)S(1)} %pad_maximum_fusion.10), channel_id=1, source_target_pairs={{0,8},{2,10},{4,12},{6,14},{8,0},{10,2},{12,4},{14,6},{16,24},{18,... | collective-permute-start | bytes 589832 | tf_op jit(solution)/shard_map/ppermute | solution.py:432
  68.5 7.8 %collective-permute-start.6 = (f32[192,256]{1,0:T(8,128)S(1)}, f32[192,256]{1,0:T(8,128)S(1)}, u32[]{:S(2)}, u32[]{:S(2)}) collective-permute-start(f32[192,256]{1,0:T(8,128)S(1)} %pad_maximum_fusion.9), channel_id=1, source_target_pairs={{0,4},{2,6},{4,0},{6,2},{8,12},{10,14},{12,8},{14,10},{16,20},{18,... | collective-permute-start | bytes 589832 | tf_op jit(solution)/shard_map/ppermute | solution.py:432
  69.9 10.6 %collective-permute-start.23 = (f32[384,256]{1,0:T(8,128)S(1)}, f32[384,256]{1,0:T(8,128)S(1)}, u32[]{:S(2)}, u32[]{:S(2)}) collective-permute-start(f32[384,256]{1,0:T(8,128)S(1)} %pad_maximum_fusion.5), channel_id=1, source_target_pairs={{0,8},{2,10},{4,12},{6,14},{8,0},{10,2},{12,4},{14,6},{16,24},{18,... | collective-permute-start | bytes 1179656 | tf_op jit(solution)/shard_map/ppermute | solution.py:432
  74.9 7.8 %collective-permute-start.15 = (f32[384,256]{1,0:T(8,128)S(1)}, f32[384,256]{1,0:T(8,128)S(1)}, u32[]{:S(2)}, u32[]{:S(2)}) collective-permute-start(f32[384,256]{1,0:T(8,128)S(1)} %pad_maximum_fusion.4), channel_id=1, source_target_pairs={{0,4},{2,6},{4,0},{6,2},{8,12},{10,14},{12,8},{14,10},{16,20},{18,... | collective-permute-start | bytes 1179656 | tf_op jit(solution)/shard_map/ppermute | solution.py:432
  76.4 7.8 %collective-permute-start.7 = (f32[384,256]{1,0:T(8,128)S(1)}, f32[384,256]{1,0:T(8,128)S(1)}, u32[]{:S(2)}, u32[]{:S(2)}) collective-permute-start(f32[384,256]{1,0:T(8,128)S(1)} %pad_maximum_fusion.3), channel_id=1, source_target_pairs={{0,2},{2,0},{4,6},{6,4},{8,10},{10,8},{12,14},{14,12},{16,18},{18,... | collective-permute-start | bytes 1179656 | tf_op jit(solution)/shard_map/ppermute | solution.py:432
  176.3 7.6 %collective-permute-start.47 = (f32[64,256]{1,0:T(8,128)S(1)}, f32[64,256]{1,0:T(8,128)S(1)}, u32[]{:S(2)}, u32[]{:S(2)}) collective-permute-start(f32[64,256]{1,0:T(8,128)S(1)} %add.332), channel_id=1, source_target_pairs={{0,16},{2,18},{4,20},{6,22},{8,24},{10,26},{12,28},{14,30},{16,0},... | collective-permute-start | bytes 196616 | tf_op jit(solution)/shard_map/ppermute | solution.py:432
  177.3 7.6 %collective-permute-start.40 = (f32[64,256]{1,0:T(8,128)S(1)}, f32[64,256]{1,0:T(8,128)S(1)}, u32[]{:S(2)}, u32[]{:S(2)}) collective-permute-start(f32[64,256]{1,0:T(8,128)S(1)} %add.321), channel_id=1, source_target_pairs={{0,16},{2,18},{4,20},{6,22},{8,24},{10,26},{12,28},{14,30},{16,0},... | collective-permute-start | bytes 196616 | tf_op jit(solution)/shard_map/ppermute | solution.py:432
  179.4 6.6 %collective-permute-start.33 = (f32[64,256]{1,0:T(8,128)S(1)}, f32[64,256]{1,0:T(8,128)S(1)}, u32[]{:S(2)}, u32[]{:S(2)}) collective-permute-start(f32[64,256]{1,0:T(8,128)S(1)} %add.310), channel_id=1, source_target_pairs={{0,16},{2,18},{4,20},{6,22},{8,24},{10,26},{12,28},{14,30},{16,0},... | collective-permute-start | bytes 196616 | tf_op jit(solution)/shard_map/ppermute | solution.py:432
  (31 other events, 112.5 us)

commit v10 on v6

--- a/solution.py
+++ b/solution.py
@@ -176,10 +176,10 @@
         acc[...] = jnp.zeros_like(acc)
 
     et = e_ref[...].T
-    at = 0
+    got = dot(et, x_ref[...])
     for c in range(2):
-        acc[at:at + k] += dot(et, x_ref[:, c * p:(c + 1) * p])
-        at += k
+        acc[c * k:(c + 1) * k] += got[:, c * p:(c + 1) * p]
+    at = 2 * k
     for j in range(k // p):
         m = (j + 1) * p
         acc[at:at + m] += dot(et[:m], e_ref[:, j * p:(j + 1) * p])
@@ -258,11 +258,10 @@
         rows = tile_rows(i, tile)
         high = w_ref[rows, :p]
         both = jnp.concatenate([high.T, w_ref[rows, p:].T], axis=0)
-        square = dot(both, high)
-        acc[:p] += square[:p]
-        hl[...] += square[p:]
-        other_two = dot(both, x_ref[rows, p:])
-        acc[p:] += other_two[:p] + other_two[p:]
+        got = dot(both, jnp.concatenate([high, x_ref[rows, p:]], axis=1))
+        acc[:p] += got[:p, :p]
+        hl[...] += got[p:, :p]
+        acc[p:] += got[:p, p:] + got[p:, p:]
 
     def step(i, carry):
         gather(i)
@@ -340,14 +339,14 @@
         high, low = w2_ref[rows, :p], w2_ref[rows, p:]
         qt = q_ref[rows, :].T
         left = jnp.concatenate([high.T, low.T, qt], axis=0)
-        square = dot(left, high)
-        acc[:p] += square[:p]
-        hl[...] += square[p:2 * p]
-        acc[p:2 * p] += square[2 * p:] + dot(qt, low)
+        got = dot(left, jnp.concatenate([high, l_ref[rows, :]], axis=1))
+        acc[:p] += got[:p, :p]
+        hl[...] += got[p:2 * p, :p]
+        acc[p:2 * p] += got[2 * p:, :p] + dot(qt, low)
         for c in range(2):
-            mixed = dot(left, l_ref[rows, c * p:(c + 1) * p])
-            acc[(2 + c) * p:(3 + c) * p] += mixed[:p] + mixed[p:2 * p]
-            acc[(4 + c) * p:(5 + c) * p] += mixed[2 * p:]
+            cols = slice((1 + c) * p, (2 + c) * p)
+            acc[(2 + c) * p:(3 + c) * p] += got[:p, cols] + got[p:2 * p, cols]
+            acc[(4 + c) * p:(5 + c) * p] += got[2 * p:, cols]
 
     def step(i, carry):
         gather(i)

time: 213 us -> 213 us (level)
  transfers between devices with their start and end apart: 53 -> 53, of which waited for: 40 -> 39; matrix products, arithmetic and copies ran while one was open for 3% -> 3% of each run, Pallas kernels for 0% -> 0%
where the time goes in v10:
time: 213 us
  Pallas kernels  72.2 us (34%)
  waiting for transfers between devices  62.8 us (29%)
  starting transfers between devices  41.8 us (20%)
  blocking collectives  27.5 us (13%)
  other arithmetic  5.07 us (2%)
    pallas_call x4, Pallas kernels, call(): pl.pallas_call(kernel, grid=(n // tile,) if grid is None else grid, in_sp...  72.2 us
    ppermute x53, waiting for transfers between devices, exchange(): return lax.ppermute(x, axis, [(i, i ^ 1 << bit) for i in range(size)])  62.8 us
    ppermute x53, starting transfers between devices, exchange(): return lax.ppermute(x, axis, [(i, i ^ 1 << bit) for i in range(size)])  41.8 us
    all_to_all x1, blocking collectives, summed_at_once(): got = lax.all_to_all(x, 'rows', 0, 0, tiled=True)  14.7 us
    all_to_all x1, blocking collectives, summed_at_once(): x = lax.all_to_all(same, 'rows', 0, 0, tiled=True)  12.8 us
  transfers between devices with their start and end apart: 53, of which 39 were waited for; matrix products, arithmetic and copies ran while one was open for 3% of the time, Pallas kernels for 0%

profile of v10, /device:TPU:0, one launch (start us, length us, event | category | flops | bytes accessed | tf_op | source)
XLA Modules:
  0.0 212.7 jit_solution(15867579673077326155)
XLA Ops:
  0.6 14.5 %cross.1 = (f32[768,256]{1,0:T(8,128)S(1)}, f32[768,256]{1,0:T(8,128)}, f32[768,256]{1,0:T(8,128)}, f32[768,256]{1,0:T(8,128)S(1)}, f32[768,256]{1,0:T(8,128)S(1)}, /*index=5*/f32[768,256]{1,0:T(8,128)S(1)}) custom-call(s32[1]{0:T(128)} %bitcast.r_0_, bf16[4096,1024]{1,0:T(8,128)(2,1)} %r_6_.1, bf16[4096,512]{1,0:T(8,128)(2,1)} %r_8_.1), custom_call_target="tpu_custom_call" | custom-call | flops 9663676416 | bytes 12582912 | tf_op jit(solution)/shard_map/cross/pallas_call | solution.py:499
  16.1 1.7 collective-permute-done.16
  20.7 2.9 %collective-permute-start.17 = (f32[384,256]{1,0:T(8,128)}, f32[384,256]{1,0:T(8,128)S(1)}, u32[]{:S(2)}, u32[]{:S(2)}) collective-permute-start(f32[384,256]{1,0:T(8,128)} %constant_dynamic-slice_fusion.8), channel_id=1, source_target_pairs={{0,8},{2,10},{4,12},{6,14},{8,0},{10,2},{12,4},{14,6},{16,24},{18,... | collective-permute-start | bytes 1179656 | tf_op jit(solution)/shard_map/ppermute | solution.py:420
  29.3 3.9 %collective-permute-done.17 = f32[384,256]{1,0:T(8,128)S(1)} collective-permute-done((f32[384,256]{1,0:T(8,128)}, f32[384,256]{1,0:T(8,128)S(1)}, u32[]{:S(2)}, u32[]{:S(2)}) %collective-permute-start.17) | collective-permute-done | bytes 393248 | tf_op jit(solution)/shard_map/ppermute | solution.py:420
  33.4 1.7 collective-permute-start.18
  36.8 3.1 %collective-permute-done.1 = f32[384,256]{1,0:T(8,128)S(1)} collective-permute-done((f32[384,256]{1,0:T(8,128)S(1)}, f32[384,256]{1,0:T(8,128)S(1)}, u32[]{:S(2)}, u32[]{:S(2)}) %collective-permute-start.1) | collective-permute-done | bytes 393248 | tf_op jit(solution)/shard_map/ppermute | solution.py:420
  40.6 2.1 collective-permute-done.18
  44.9 1.9 collective-permute-done.2
  47.8 2.7 %collective-permute-start.20 = (f32[96,256]{1,0:T(8,128)S(1)}, f32[96,256]{1,0:T(8,128)S(1)}, u32[]{:S(2)}, u32[]{:S(2)}) collective-permute-start(f32[96,256]{1,0:T(8,128)S(1)} %dynamic-slice_add_fusion.9), channel_id=1, source_target_pairs={{0,16},{2,18},{4,20},{6,22},{8,24},{10,26},{12,28},{14,30},{16,0},... | collective-permute-start | bytes 294920 | tf_op jit(solution)/shard_map/ppermute | solution.py:420
  52.6 2.7 %collective-permute-start.4 = (f32[96,256]{1,0:T(8,128)S(1)}, f32[96,256]{1,0:T(8,128)S(1)}, u32[]{:S(2)}, u32[]{:S(2)}) collective-permute-start(f32[96,256]{1,0:T(8,128)S(1)} %dynamic-slice_add_fusion.11), channel_id=1, source_target_pairs={{0,16},{2,18},{4,20},{6,22},{8,24},{10,26},{12,28},{14,30},{16,0},... | collective-permute-start | bytes 294920 | tf_op jit(solution)/shard_map/ppermute | solution.py:420
  55.2 4.4 %collective-permute-done.20 = f32[96,256]{1,0:T(8,128)S(1)} collective-permute-done((f32[96,256]{1,0:T(8,128)S(1)}, f32[96,256]{1,0:T(8,128)S(1)}, u32[]{:S(2)}, u32[]{:S(2)}) %collective-permute-start.20) | collective-permute-done | bytes 98336 | tf_op jit(solution)/shard_map/ppermute | solution.py:420
  59.9 1.7 collective-permute-done.12
  71.2 4.0 %collective-permute-done.14 = f32[192,256]{1,0:T(8,128)S(1)} collective-permute-done((f32[192,256]{1,0:T(8,128)S(1)}, f32[192,256]{1,0:T(8,128)S(1)}, u32[]{:S(2)}, u32[]{:S(2)}) %collective-permute-start.14) | collective-permute-done | bytes 196640 | tf_op jit(solution)/shard_map/ppermute | solution.py:420
  77.9 3.0 %collective-permute-done.23 = f32[384,256]{1,0:T(8,128)S(1)} collective-permute-done((f32[384,256]{1,0:T(8,128)S(1)}, f32[384,256]{1,0:T(8,128)S(1)}, u32[]{:S(2)}, u32[]{:S(2)}) %collective-permute-start.23) | collective-permute-done | bytes 393248 | tf_op jit(solution)/shard_map/ppermute | solution.py:420
  81.2 2.0 collective-permute-done.15
  87.2 18.1 %first.1 = (f32[4096,256]{1,0:T(8,128)}, bf16[4096,512]{1,0:T(8,128)(2,1)}, f32[1024,256]{1,0:T(8,128)}, f32[1024,256]{1,0:T(8,128)}, f32[256,256]{1,0:T(8,128)S...) custom-call(s32[1]{0:T(128)} %bitcast.r_0_, f32[768,256]{1,0:T(8,128)S(1)} %pad_maximum_fusion.r_1_, ...), custom_call_target="tpu_custom_call" | custom-call | flops 11811160064 | bytes 20971520 | tf_op jit(solution)/shard_map/first/pallas_call | solution.py:499
  106.9 14.7 %all_to_all.17 = f32[16,16,256]{2,1,0:T(8,128)S(1)} all-to-all(f32[16,16,256]{2,1,0:T(8,128)S(1)} %bitcast.5), channel_id=1, replica_groups=mesh['rows'=16,'grp'=2] {'rows'}, dimensions={0} | all-to-all | bytes 524288 | tf_op jit(solution)/shard_map/all_to_all | solution.py:453
  121.6 12.8 %all_to_all.18 = f32[16,16,256]{2,1,0:T(8,128)S(1)} all-to-all(f32[16,16,256]{2,1,0:T(8,128)S(1)} %broadcast_in_dim.2), channel_id=1, replica_groups=mesh['rows'=16,'grp'=2] {'rows'}, dimensions={0} | all-to-all | bytes 524288 | tf_op jit(solution)/shard_map/all_to_all | solution.py:456
  135.9 24.4 %second.1 = (bf16[4096,256]{1,0:T(8,128)(2,1)}, bf16[4096,512]{1,0:T(8,128)(2,1)}, f32[256,256]{1,0:T(8,128)S(1)}, f32[256,256]{1,0:T(8,128)S(1)}, f32[256,256]{...) custom-call(s32[1]{0:T(128)} %bitcast.r_0_, ...), custom_call_target="tpu_custom_call" | custom-call | flops 10200547328 | bytes 27262976 | tf_op jit(solution)/shard_map/second/pallas_call | solution.py:499
  164.7 2.9 %collective-permute-done.44 = f32[128,256]{1,0:T(8,128)S(1)} collective-permute-done((f32[128,256]{1,0:T(8,128)S(1)}, f32[128,256]{1,0:T(8,128)S(1)}, u32[]{:S(2)}, u32[]{:S(2)}) %collective-permute-start.44) | collective-permute-done | bytes 131104 | tf_op jit(solution)/shard_map/ppermute | solution.py:420
  177.4 2.1 collective-permute-start.40
  180.4 3.5 %collective-permute-done.47 = f32[64,256]{1,0:T(8,128)S(1)} collective-permute-done((f32[64,256]{1,0:T(8,128)S(1)}, f32[64,256]{1,0:T(8,128)S(1)}, u32[]{:S(2)}, u32[]{:S(2)}) %collective-permute-start.47) | collective-permute-done | bytes 65568 | tf_op jit(solution)/shard_map/ppermute | solution.py:420
  191.4 1.9 collective-permute-done.49
  197.3 15.3 %last.1 = (bf16[4096,512]{1,0:T(8,128)(2,1)}, f32[2,256,256]{2,1,0:T(8,128)}, f32[512,512]{1,0:T(8,128)}) custom-call(s32[1]{0:T(128)} %bitcast.r_0_, f32[256,256]{1,0:T(8,128)S(1)} %pad_maximum_fusion.6.r_1_, f32[256,256]{1,0:T(8,128)S(1)} %pad_maximum_fusion.7.r_2_, f32[256,256]{1,0:T(8,128)S(1)} %pad_maximum_fusion.8.r_3_, ...), custom_call_target="tpu_custom_call" | custom-call | flops 2147483648 | bytes 10485760 | tf_op jit(solution)/shard_map/last/pallas_call | solution.py:499
  (174 shorter events, 63.5 us)
Async XLA Ops:
  15.5 8.1 %collective-permute-start.8 = (f32[768,256]{1,0:T(8,128)}, f32[768,256]{1,0:T(8,128)}, u32[]{:S(2)}, u32[]{:S(2)}) collective-permute-start(f32[768,256]{1,0:T(8,128)} %get-tuple-element.29), channel_id=1, source_target_pairs={{0,1},{1,0},{2,3},{3,2},{4,5},{5,4},{6,7},{7,6},{8,9},{9,8},{10,11... | collective-permute-start | bytes 2359304 | tf_op jit(solution)/shard_map/ppermute | solution.py:420
  15.6 10.9 %collective-permute-start = (f32[768,256]{1,0:T(8,128)S(1)}, f32[768,256]{1,0:T(8,128)}, u32[]{:S(2)}, u32[]{:S(2)}) collective-permute-start(f32[768,256]{1,0:T(8,128)S(1)} %get-tuple-element.27), channel_id=1, source_target_pairs={{0,1},{1,0},{2,3},{3,2},{4,5},{5,4},{6,7},{7,6},{8,9},{9,8},{10,11... | collective-permute-start | bytes 2359304 | tf_op jit(solution)/shard_map/ppermute | solution.py:420
  20.7 12.6 %collective-permute-start.17 = (f32[384,256]{1,0:T(8,128)}, f32[384,256]{1,0:T(8,128)S(1)}, u32[]{:S(2)}, u32[]{:S(2)}) collective-permute-start(f32[384,256]{1,0:T(8,128)} %constant_dynamic-slice_fusion.8), channel_id=1, source_target_pairs={{0,8},{2,10},{4,12},{6,14},{8,0},{10,2},{12,4},{14,6},{16,24},{18,... | collective-permute-start | bytes 1179656 | tf_op jit(solution)/shard_map/ppermute | solution.py:420
  24.9 10.9 %collective-permute-start.9 = (f32[384,256]{1,0:T(8,128)S(1)}, f32[384,256]{1,0:T(8,128)S(1)}, u32[]{:S(2)}, u32[]{:S(2)}) collective-permute-start(f32[384,256]{1,0:T(8,128)S(1)} %constant_dynamic-slice_fusion.11), channel_id=1, source_target_pairs={{0,4},{2,6},{4,0},{6,2},{8,12},{10,14},{12,8},{14,10},{16,20},{18,... | collective-permute-start | bytes 1179656 | tf_op jit(solution)/shard_map/ppermute | solution.py:420
  27.8 12.1 %collective-permute-start.1 = (f32[384,256]{1,0:T(8,128)S(1)}, f32[384,256]{1,0:T(8,128)S(1)}, u32[]{:S(2)}, u32[]{:S(2)}) collective-permute-start(f32[384,256]{1,0:T(8,128)S(1)} %constant_dynamic-slice_fusion.14), channel_id=1, source_target_pairs={{0,2},{2,0},{4,6},{6,4},{8,10},{10,8},{12,14},{14,12},{16,18},{18,... | collective-permute-start | bytes 1179656 | tf_op jit(solution)/shard_map/ppermute | solution.py:420
  33.4 9.3 %collective-permute-start.18 = (f32[192,256]{1,0:T(8,128)S(1)}, f32[192,256]{1,0:T(8,128)S(1)}, u32[]{:S(2)}, u32[]{:S(2)}) collective-permute-start(f32[192,256]{1,0:T(8,128)S(1)} %constant_dynamic-slice_fusion.7), channel_id=1, source_target_pairs={{0,2},{2,0},{4,6},{6,4},{8,10},{10,8},{12,14},{14,12},{16,18},{18,... | collective-permute-start | bytes 589832 | tf_op jit(solution)/shard_map/ppermute | solution.py:420
  36.0 7.3 %collective-permute-start.10 = (f32[192,256]{1,0:T(8,128)S(1)}, f32[192,256]{1,0:T(8,128)S(1)}, u32[]{:S(2)}, u32[]{:S(2)}) collective-permute-start(f32[192,256]{1,0:T(8,128)S(1)} %constant_dynamic-slice_fusion.10), channel_id=1, source_target_pairs={{0,8},{2,10},{4,12},{6,14},{8,0},{10,2},{12,4},{14,6},{16,24},{18,... | collective-permute-start | bytes 589832 | tf_op jit(solution)/shard_map/ppermute | solution.py:420
  40.0 6.8 %collective-permute-start.2 = (f32[192,256]{1,0:T(8,128)S(1)}, f32[192,256]{1,0:T(8,128)S(1)}, u32[]{:S(2)}, u32[]{:S(2)}) collective-permute-start(f32[192,256]{1,0:T(8,128)S(1)} %constant_dynamic-slice_fusion.13), channel_id=1, source_target_pairs={{0,4},{2,6},{4,0},{6,2},{8,12},{10,14},{12,8},{14,10},{16,20},{18,... | collective-permute-start | bytes 589832 | tf_op jit(solution)/shard_map/ppermute | solution.py:420
  43.4 7.1 %collective-permute-start.11 = (f32[96,256]{1,0:T(8,128)S(1)}, f32[96,256]{1,0:T(8,128)S(1)}, u32[]{:S(2)}, u32[]{:S(2)}) collective-permute-start(f32[96,256]{1,0:T(8,128)S(1)} %constant_dynamic-slice_fusion.9), channel_id=1, source_target_pairs={{0,2},{2,0},{4,6},{6,4},{8,10},{10,8},{12,14},{14,12},{16,18},{18,... | collective-permute-start | bytes 294920 | tf_op jit(solution)/shard_map/ppermute | solution.py:420
  46.8 5.7 %collective-permute-start.3 = (f32[96,256]{1,0:T(8,128)S(1)}, f32[96,256]{1,0:T(8,128)S(1)}, u32[]{:S(2)}, u32[]{:S(2)}) collective-permute-start(f32[96,256]{1,0:T(8,128)S(1)} %constant_dynamic-slice_fusion.12), channel_id=1, source_target_pairs={{0,8},{2,10},{4,12},{6,14},{8,0},{10,2},{12,4},{14,6},{16,24},{18,... | collective-permute-start | bytes 294920 | tf_op jit(solution)/shard_map/ppermute | solution.py:420
  47.8 11.8 %collective-permute-start.20 = (f32[96,256]{1,0:T(8,128)S(1)}, f32[96,256]{1,0:T(8,128)S(1)}, u32[]{:S(2)}, u32[]{:S(2)}) collective-permute-start(f32[96,256]{1,0:T(8,128)S(1)} %dynamic-slice_add_fusion.9), channel_id=1, source_target_pairs={{0,16},{2,18},{4,20},{6,22},{8,24},{10,26},{12,28},{14,30},{16,0},... | collective-permute-start | bytes 294920 | tf_op jit(solution)/shard_map/ppermute | solution.py:420
  50.5 11.1 %collective-permute-start.12 = (f32[96,256]{1,0:T(8,128)S(1)}, f32[96,256]{1,0:T(8,128)S(1)}, u32[]{:S(2)}, u32[]{:S(2)}) collective-permute-start(f32[96,256]{1,0:T(8,128)S(1)} %dynamic-slice_add_fusion.10), channel_id=1, source_target_pairs={{0,16},{2,18},{4,20},{6,22},{8,24},{10,26},{12,28},{14,30},{16,0},... | collective-permute-start | bytes 294920 | tf_op jit(solution)/shard_map/ppermute | solution.py:420
  52.6 10.6 %collective-permute-start.4 = (f32[96,256]{1,0:T(8,128)S(1)}, f32[96,256]{1,0:T(8,128)S(1)}, u32[]{:S(2)}, u32[]{:S(2)}) collective-permute-start(f32[96,256]{1,0:T(8,128)S(1)} %dynamic-slice_add_fusion.11), channel_id=1, source_target_pairs={{0,16},{2,18},{4,20},{6,22},{8,24},{10,26},{12,28},{14,30},{16,0},... | collective-permute-start | bytes 294920 | tf_op jit(solution)/shard_map/ppermute | solution.py:420
  61.7 5.7 %collective-permute-start.13 = (f32[96,256]{1,0:T(8,128)S(1)}, f32[96,256]{1,0:T(8,128)S(1)}, u32[]{:S(2)}, u32[]{:S(2)}) collective-permute-start(f32[96,256]{1,0:T(8,128)S(1)} %add.204), channel_id=1, source_target_pairs={{0,2},{2,0},{4,6},{6,4},{8,10},{10,8},{12,14},{14,12},{16,18},{18,... | collective-permute-start | bytes 294920 | tf_op jit(solution)/shard_map/ppermute | solution.py:420
  63.2 5.7 %collective-permute-start.5 = (f32[96,256]{1,0:T(8,128)S(1)}, f32[96,256]{1,0:T(8,128)S(1)}, u32[]{:S(2)}, u32[]{:S(2)}) collective-permute-start(f32[96,256]{1,0:T(8,128)S(1)} %add.193), channel_id=1, source_target_pairs={{0,8},{2,10},{4,12},{6,14},{8,0},{10,2},{12,4},{14,6},{16,24},{18,... | collective-permute-start | bytes 294920 | tf_op jit(solution)/shard_map/ppermute | solution.py:420
  64.4 5.7 %collective-permute-start.22 = (f32[192,256]{1,0:T(8,128)S(1)}, f32[192,256]{1,0:T(8,128)S(1)}, u32[]{:S(2)}, u32[]{:S(2)}) collective-permute-start(f32[192,256]{1,0:T(8,128)S(1)} %pad_maximum_fusion.11), channel_id=1, source_target_pairs={{0,2},{2,0},{4,6},{6,4},{8,10},{10,8},{12,14},{14,12},{16,18},{18,... | collective-permute-start | bytes 589832 | tf_op jit(solution)/shard_map/ppermute | solution.py:420
  67.4 7.8 %collective-permute-start.14 = (f32[192,256]{1,0:T(8,128)S(1)}, f32[192,256]{1,0:T(8,128)S(1)}, u32[]{:S(2)}, u32[]{:S(2)}) collective-permute-start(f32[192,256]{1,0:T(8,128)S(1)} %pad_maximum_fusion.10), channel_id=1, source_target_pairs={{0,8},{2,10},{4,12},{6,14},{8,0},{10,2},{12,4},{14,6},{16,24},{18,... | collective-permute-start | bytes 589832 | tf_op jit(solution)/shard_map/ppermute | solution.py:420
  69.0 7.8 %collective-permute-start.6 = (f32[192,256]{1,0:T(8,128)S(1)}, f32[192,256]{1,0:T(8,128)S(1)}, u32[]{:S(2)}, u32[]{:S(2)}) collective-permute-start(f32[192,256]{1,0:T(8,128)S(1)} %pad_maximum_fusion.9), channel_id=1, source_target_pairs={{0,4},{2,6},{4,0},{6,2},{8,12},{10,14},{12,8},{14,10},{16,20},{18,... | collective-permute-start | bytes 589832 | tf_op jit(solution)/shard_map/ppermute | solution.py:420
  70.2 10.8 %collective-permute-start.23 = (f32[384,256]{1,0:T(8,128)S(1)}, f32[384,256]{1,0:T(8,128)S(1)}, u32[]{:S(2)}, u32[]{:S(2)}) collective-permute-start(f32[384,256]{1,0:T(8,128)S(1)} %pad_maximum_fusion.5), channel_id=1, source_target_pairs={{0,8},{2,10},{4,12},{6,14},{8,0},{10,2},{12,4},{14,6},{16,24},{18,... | collective-permute-start | bytes 1179656 | tf_op jit(solution)/shard_map/ppermute | solution.py:420
  75.3 7.8 %collective-permute-start.15 = (f32[384,256]{1,0:T(8,128)S(1)}, f32[384,256]{1,0:T(8,128)S(1)}, u32[]{:S(2)}, u32[]{:S(2)}) collective-permute-start(f32[384,256]{1,0:T(8,128)S(1)} %pad_maximum_fusion.4), channel_id=1, source_target_pairs={{0,4},{2,6},{4,0},{6,2},{8,12},{10,14},{12,8},{14,10},{16,20},{18,... | collective-permute-start | bytes 1179656 | tf_op jit(solution)/shard_map/ppermute | solution.py:420
  76.9 7.8 %collective-permute-start.7 = (f32[384,256]{1,0:T(8,128)S(1)}, f32[384,256]{1,0:T(8,128)S(1)}, u32[]{:S(2)}, u32[]{:S(2)}) collective-permute-start(f32[384,256]{1,0:T(8,128)S(1)} %pad_maximum_fusion.3), channel_id=1, source_target_pairs={{0,2},{2,0},{4,6},{6,4},{8,10},{10,8},{12,14},{14,12},{16,18},{18,... | collective-permute-start | bytes 1179656 | tf_op jit(solution)/shard_map/ppermute | solution.py:420
  176.4 7.6 %collective-permute-start.47 = (f32[64,256]{1,0:T(8,128)S(1)}, f32[64,256]{1,0:T(8,128)S(1)}, u32[]{:S(2)}, u32[]{:S(2)}) collective-permute-start(f32[64,256]{1,0:T(8,128)S(1)} %add.242), channel_id=1, source_target_pairs={{0,16},{2,18},{4,20},{6,22},{8,24},{10,26},{12,28},{14,30},{16,0},... | collective-permute-start | bytes 196616 | tf_op jit(solution)/shard_map/ppermute | solution.py:420
  177.4 7.4 %collective-permute-start.40 = (f32[64,256]{1,0:T(8,128)S(1)}, f32[64,256]{1,0:T(8,128)S(1)}, u32[]{:S(2)}, u32[]{:S(2)}) collective-permute-start(f32[64,256]{1,0:T(8,128)S(1)} %add.233), channel_id=1, source_target_pairs={{0,16},{2,18},{4,20},{6,22},{8,24},{10,26},{12,28},{14,30},{16,0},... | collective-permute-start | bytes 196616 | tf_op jit(solution)/shard_map/ppermute | solution.py:420
  179.4 6.6 %collective-permute-start.33 = (f32[64,256]{1,0:T(8,128)S(1)}, f32[64,256]{1,0:T(8,128)S(1)}, u32[]{:S(2)}, u32[]{:S(2)}) collective-permute-start(f32[64,256]{1,0:T(8,128)S(1)} %add.224), channel_id=1, source_target_pairs={{0,16},{2,18},{4,20},{6,22},{8,24},{10,26},{12,28},{14,30},{16,0},... | collective-permute-start | bytes 196616 | tf_op jit(solution)/shard_map/ppermute | solution.py:420
  (33 other events, 126.5 us)
